TPU v7x, 32 devices: a whole 2x2x4 slice. The times are simulated.
32 devices in a mesh: wide: 16 (over z, y, core), narrow: 2 (over x).
Axes of the slice: x: 2, y: 2, z: 4, core: 2. Of those that a mesh axis runs over, the one named last changes fastest.
Arguments:
- inputs: bfloat16 [32, 1024, 1024], P(('wide', 'narrow')), may hold values from -6 to 6
- norm_first: bfloat16 [1024], P(('wide', 'narrow')), may hold values from 0.5 to 1.5
- w_query: bfloat16 [1024, 1024], P(('wide', 'narrow')), may hold values from -0.046875 to 0.046875
- w_key: bfloat16 [1024, 1024], P(('wide', 'narrow')), may hold values from -0.1875 to 0.1875
- w_value: bfloat16 [1024, 1024], P(('wide', 'narrow')), may hold values from -0.1875 to 0.1875
- w_out: bfloat16 [1024, 1024], P(('wide', 'narrow')), may hold values from -1 to 1
- rel_table: bfloat16 [512], P(('wide', 'narrow')), may hold values from -4 to 4
- x_table: bfloat16 [512], P(('wide', 'narrow')), may hold values from -4 to 4
- y_table: bfloat16 [512], P(('wide', 'narrow')), may hold values from -4 to 4
- norm_second: bfloat16 [1024], P(('wide', 'narrow')), may hold values from 0.5 to 1.5
- w_gate: bfloat16 [1024, 2816], P(('wide', 'narrow')), may hold values from -0.1875 to 0.1875
- w_up: bfloat16 [1024, 2816], P(('wide', 'narrow')), may hold values from -0.1875 to 0.1875
- w_down: bfloat16 [2816, 1024], P(('wide', 'narrow')), may hold values from -0.109375 to 0.109375
- lengths: int32 [32], P(('wide', 'narrow')), may hold values from 320 to 1024, as said below
- boxes: int32 [32, 2, 1024], P(('wide', 'narrow')), may hold values from 0 to 1000
- cotangent: bfloat16 [32, 1024, 1024], P(('wide', 'narrow')), may hold values from -6 to 6
Outputs:
- output: bfloat16 [32, 1024, 1024], P(('wide', 'narrow'))
- grad_inputs: float32 [32, 1024, 1024], P(('wide', 'narrow'))
- grad_norm_first: float32 [1024], P(('wide', 'narrow'))
- grad_w_query: float32 [1024, 1024], P(('wide', 'narrow'))
- grad_w_key: float32 [1024, 1024], P(('wide', 'narrow'))
- grad_w_value: float32 [1024, 1024], P(('wide', 'narrow'))
- grad_w_out: float32 [1024, 1024], P(('wide', 'narrow'))
- grad_rel_table: float32 [512], P(('wide', 'narrow'))
- grad_x_table: float32 [512], P(('wide', 'narrow'))
- grad_y_table: float32 [512], P(('wide', 'narrow'))
- grad_norm_second: float32 [1024], P(('wide', 'narrow'))
- grad_w_gate: float32 [1024, 2816], P(('wide', 'narrow'))
- grad_w_up: float32 [1024, 2816], P(('wide', 'narrow'))
- grad_w_down: float32 [2816, 1024], P(('wide', 'narrow'))
Inputs may be any that keep to these rules, and one draw needn't show every extreme that they name: `lengths`: every sequence has 320 to 704 true tokens, except 32 // 7 sequences placed anywhere, which are full at 1024.
All inputs are finite; a program needn't handle non-finite values.
Results may differ from a plain program's by a relative error of at most 0.014.
The roundings to bfloat16 on the way count: a program that leaves them out, or rounds other values in their place, can miss the bound.
Values may be sent and summed in bfloat16 or wider, within the bound.
No kernel may reach another device: no remote copies, remote signals or barrier semaphores. Data moves between devices by JAX's collectives and lax.ppermute only.
A program may use at most 384 MiB of HBM per device.

v0:
```python
import jax
import jax.numpy as jnp
import numpy as np
from jax import lax
from jax.sharding import PartitionSpec as P

HEADS = 16
HEAD_DIM = 64
BUCKETS = 32


epsilon = 1e-06
coord_top = 1000
token_reach = 128
layout_reach = 256
masked_score = -1e30
gelu_scale = 0.7978845608028654


def bucket_table(span, buckets, reach):
    offsets = np.arange(-span, span + 1)
    half = buckets // 2
    exact = half // 2
    side = np.where(offsets > 0, half, 0)
    distance = np.abs(offsets)
    safe = np.maximum(distance, 1)
    large = exact + (np.log(safe / exact) / np.log(reach / exact) * (half - exact)).astype(np.int64)
    large = np.minimum(large, half - 1)
    return side + np.where(distance < exact, distance, large)


def magnitude_steps(span, reach):
    half = BUCKETS // 2
    exact = half // 2
    offsets = np.arange(span + 1)
    table = bucket_table(span, BUCKETS, reach)[span:]
    magnitude = table - np.where(offsets > 0, half, 0)
    steps = []
    for level in range(exact + 1, half):
        if (magnitude >= level).any():
            steps.append(int(np.argmax(magnitude >= level)))
    return steps


def bucket_index(offset, span, reach):
    half = BUCKETS // 2
    exact = half // 2
    distance = jnp.abs(offset)
    counted = jnp.zeros(offset.shape, jnp.int32)
    for edge in magnitude_steps(span, reach):
        counted = counted + (distance >= edge).astype(jnp.int32)
    magnitude = jnp.where(distance < exact, distance, exact + counted)
    return jnp.where(offset > 0, half, 0).astype(jnp.int32) + magnitude.astype(jnp.int32)


def layout_hot(box, start, count, slots):
    places = jnp.arange(slots, dtype=jnp.int32)
    rel_offset = places[None, :] - (start + jnp.arange(count, dtype=jnp.int32))[:, None]
    x_offset = box[0][None, :] - box[0][start : start + count][:, None]
    y_offset = box[1][None, :] - box[1][start : start + count][:, None]
    rel_bucket = bucket_index(rel_offset, slots - 1, token_reach).reshape(1, -1)
    x_bucket = bucket_index(x_offset, coord_top, layout_reach).reshape(1, -1) + BUCKETS
    y_bucket = bucket_index(y_offset, coord_top, layout_reach).reshape(1, -1) + 2 * BUCKETS
    columns = jnp.arange(3 * BUCKETS, dtype=jnp.int32)[:, None]
    return (rel_bucket == columns) | (x_bucket == columns) | (y_bucket == columns)


def block_bias(tables, box, begin, span, slots):
    step = min(64, span)
    parts = []
    for start in range(begin, begin + span, step):
        marks = layout_hot(box, start, step, slots).astype(jnp.bfloat16)
        parts.append(
            jnp.dot(tables, marks, preferred_element_type=jnp.float32).reshape(
                tables.shape[0], step, slots
            )
        )
    return jnp.concatenate(parts, axis=1)


def table_grads(total, grad_scores, box, begin, span, slots):
    step = min(64, span)
    heads = grad_scores.shape[0]
    for start in range(begin, begin + span, step):
        marks = layout_hot(box, start, step, slots).astype(jnp.float32)
        piece = grad_scores[:, start - begin : start - begin + step].reshape(heads, -1)
        total = total + lax.dot_general(
            piece,
            marks,
            (((1,), (1,)), ((), ())),
            precision=lax.Precision.HIGHEST,
            preferred_element_type=jnp.float32,
        )
    return total


def stack_tables(rel_full, x_full, y_full):
    return jnp.concatenate(
        [
            rel_full.reshape(HEADS, BUCKETS),
            x_full.reshape(HEADS, BUCKETS),
            y_full.reshape(HEADS, BUCKETS),
        ],
        axis=1,
    )


def norm_apply(values, gain):
    return values * lax.rsqrt(jnp.mean(values * values, axis=-1, keepdims=True) + epsilon) * gain


def gate_apply(gate, upper):
    return (
        0.5 * gate * (1.0 + jnp.tanh(gelu_scale * (gate + 0.044715 * gate * gate * gate))) * upper
    )


def plain_product(left, right):
    return jnp.dot(left, right, preferred_element_type=jnp.float32)


def left_transposed(left, right):
    return lax.dot_general(
        left, right, (((0,), (0,)), ((), ())), preferred_element_type=jnp.float32
    )


def right_transposed(left, right):
    return lax.dot_general(
        left, right, (((1,), (1,)), ((), ())), preferred_element_type=jnp.float32
    )


def split_heads(values):
    return values.reshape(values.shape[0], HEADS, HEAD_DIM)


def block_scores(query_block, heads_k, bias_block, keep):
    scores = (
        jnp.einsum("qhd,khd->hqk", query_block, heads_k, preferred_element_type=jnp.float32)
        + bias_block
    )
    return jnp.where(keep[None, None, :], scores, masked_score)


def attend_forward(query, key_rows, value_rows, tables, box, length):
    slots = query.shape[0]
    span = min(512, slots)
    heads_q, heads_k, heads_v = (split_heads(query), split_heads(key_rows), split_heads(value_rows))
    keep = jnp.arange(slots) < length
    outputs = []
    logsums = []
    for begin in range(0, slots, span):
        bias_block = block_bias(tables, box, begin, span, slots)
        scores = block_scores(heads_q[begin : begin + span], heads_k, bias_block, keep)
        top = jnp.max(scores, axis=-1, keepdims=True)
        weights = jnp.exp(scores - top)
        total = jnp.sum(weights, axis=-1, keepdims=True)
        probs_low = (weights / total).astype(jnp.bfloat16)
        mixed_block = jnp.einsum(
            "hqk,khd->qhd", probs_low, heads_v, preferred_element_type=jnp.float32
        )
        outputs.append(mixed_block.reshape(span, -1))
        logsums.append(top + jnp.log(total))
    return (jnp.concatenate(outputs, axis=0).astype(jnp.bfloat16), jnp.concatenate(logsums, axis=1))


def attend_backward(
    query, key_rows, value_rows, tables, box, length, logsum, grad_mixed, table_total
):
    slots = query.shape[0]
    span = min(512, slots)
    heads_q, heads_k, heads_v = (split_heads(query), split_heads(key_rows), split_heads(value_rows))
    heads_grad = split_heads(grad_mixed)
    keep = jnp.arange(slots) < length
    grad_keys = jnp.zeros(heads_k.shape, jnp.float32)
    grad_values = jnp.zeros(heads_v.shape, jnp.float32)
    query_parts = []
    for begin in range(0, slots, span):
        query_block = heads_q[begin : begin + span]
        grad_block = heads_grad[begin : begin + span]
        bias_block = block_bias(tables, box, begin, span, slots)
        scores = block_scores(query_block, heads_k, bias_block, keep)
        probs = jnp.exp(scores - logsum[:, begin : begin + span])
        grad_probs = jnp.einsum(
            "qhd,khd->hqk", grad_block, heads_v, preferred_element_type=jnp.float32
        )
        grad_scores = probs * (grad_probs - jnp.sum(probs * grad_probs, axis=-1, keepdims=True))
        table_total = table_grads(table_total, grad_scores, box, begin, span, slots)
        scores_low = grad_scores.astype(jnp.bfloat16)
        query_part = jnp.einsum(
            "hqk,khd->qhd", scores_low, heads_k, preferred_element_type=jnp.float32
        )
        query_parts.append(query_part.reshape(span, -1))
        grad_keys = grad_keys + jnp.einsum(
            "hqk,qhd->khd", scores_low, query_block, preferred_element_type=jnp.float32
        )
        grad_values = grad_values + jnp.einsum(
            "hqk,qhd->khd",
            probs.astype(jnp.bfloat16),
            grad_block,
            preferred_element_type=jnp.float32,
        )
    grad_query = jnp.concatenate(query_parts, axis=0).astype(jnp.bfloat16)
    return (
        grad_query,
        grad_keys.reshape(slots, -1).astype(jnp.bfloat16),
        grad_values.reshape(slots, -1).astype(jnp.bfloat16),
        table_total,
    )


def local(
    inputs,
    norm_first,
    w_query,
    w_key,
    w_value,
    w_out,
    rel_table,
    x_table,
    y_table,
    norm_second,
    w_gate,
    w_up,
    w_down,
    lengths,
    boxes,
    cotangent,
):
    seq_count, slots, width = inputs.shape
    attn_params = (
        lax.all_gather(norm_first, ("wide", "narrow"), axis=0, tiled=True),
        lax.all_gather(w_query, ("wide", "narrow"), axis=0, tiled=True),
        lax.all_gather(w_key, ("wide", "narrow"), axis=0, tiled=True),
        lax.all_gather(w_value, ("wide", "narrow"), axis=0, tiled=True),
        lax.all_gather(w_out, ("wide", "narrow"), axis=0, tiled=True),
        lax.all_gather(rel_table, ("wide", "narrow"), axis=0, tiled=True),
        lax.all_gather(x_table, ("wide", "narrow"), axis=0, tiled=True),
        lax.all_gather(y_table, ("wide", "narrow"), axis=0, tiled=True),
    )
    gain_one, query_full, key_full, value_full, out_full, rel_full, x_full, y_full = attn_params
    rows = inputs.reshape(seq_count * slots, width).astype(jnp.float32)
    normed_one = norm_apply(rows, gain_one.astype(jnp.float32)).astype(jnp.bfloat16)
    query = plain_product(normed_one, query_full).astype(jnp.bfloat16)
    key_rows = plain_product(normed_one, key_full).astype(jnp.bfloat16)
    value_rows = plain_product(normed_one, value_full).astype(jnp.bfloat16)
    tables = stack_tables(rel_full, x_full, y_full)
    index = 0
    mixed_seq, logsum = attend_forward(
        query, key_rows, value_rows, tables, boxes[index], lengths[index]
    )
    logsum_parts = [logsum]
    hidden = rows + plain_product(mixed_seq, out_full)
    ffn_params = (
        lax.all_gather(norm_second, ("wide", "narrow"), axis=0, tiled=True),
        lax.all_gather(w_gate, ("wide", "narrow"), axis=0, tiled=True),
        lax.all_gather(w_up, ("wide", "narrow"), axis=0, tiled=True),
        lax.all_gather(w_down, ("wide", "narrow"), axis=0, tiled=True),
    )
    gain_two, gate_full, up_full, down_full = ffn_params
    normed_two = norm_apply(hidden, gain_two.astype(jnp.float32)).astype(jnp.bfloat16)
    gate = plain_product(normed_two, gate_full)
    upper = plain_product(normed_two, up_full)
    product, gate_pull = jax.vjp(gate_apply, gate, upper)
    activated = product.astype(jnp.bfloat16)
    output = (
        (hidden + plain_product(activated, down_full)).astype(jnp.bfloat16).reshape(inputs.shape)
    )
    back_ffn = (
        lax.all_gather(norm_second, ("wide", "narrow"), axis=0, tiled=True),
        lax.all_gather(w_gate, ("wide", "narrow"), axis=0, tiled=True),
        lax.all_gather(w_up, ("wide", "narrow"), axis=0, tiled=True),
        lax.all_gather(w_down, ("wide", "narrow"), axis=0, tiled=True),
    )
    gain_two_back, gate_back, up_back, down_back = back_ffn
    seed = cotangent.reshape(seq_count * slots, width)
    grad_w_down = left_transposed(activated, seed)
    grad_activated = right_transposed(seed, down_back)
    grad_gate, grad_upper = gate_pull(grad_activated)
    gate_low = grad_gate.astype(jnp.bfloat16)
    upper_low = grad_upper.astype(jnp.bfloat16)
    grad_w_gate = left_transposed(normed_two, gate_low)
    grad_w_up = left_transposed(normed_two, upper_low)
    grad_normed_two = right_transposed(gate_low, gate_back) + right_transposed(upper_low, up_back)
    unused_two, norm_two_pull = jax.vjp(norm_apply, hidden, gain_two_back.astype(jnp.float32))
    hidden_part, grad_gain_two = norm_two_pull(grad_normed_two)
    grad_hidden = seed.astype(jnp.float32) + hidden_part
    ffn_shares = (
        lax.psum_scatter(grad_gain_two, ("wide", "narrow"), scatter_dimension=0, tiled=True),
        lax.psum_scatter(grad_w_gate, ("wide", "narrow"), scatter_dimension=0, tiled=True),
        lax.psum_scatter(grad_w_up, ("wide", "narrow"), scatter_dimension=0, tiled=True),
        lax.psum_scatter(grad_w_down, ("wide", "narrow"), scatter_dimension=0, tiled=True),
    )
    back_attn = (
        lax.all_gather(norm_first, ("wide", "narrow"), axis=0, tiled=True),
        lax.all_gather(w_query, ("wide", "narrow"), axis=0, tiled=True),
        lax.all_gather(w_key, ("wide", "narrow"), axis=0, tiled=True),
        lax.all_gather(w_value, ("wide", "narrow"), axis=0, tiled=True),
        lax.all_gather(w_out, ("wide", "narrow"), axis=0, tiled=True),
        lax.all_gather(rel_table, ("wide", "narrow"), axis=0, tiled=True),
        lax.all_gather(x_table, ("wide", "narrow"), axis=0, tiled=True),
        lax.all_gather(y_table, ("wide", "narrow"), axis=0, tiled=True),
    )
    gain_one_back, query_back, key_back, value_back, out_back, rel_back, x_back, y_back = back_attn
    branch_low = grad_hidden.astype(jnp.bfloat16)
    grad_w_out = left_transposed(mixed_seq, branch_low)
    grad_mixed = right_transposed(branch_low, out_back).astype(jnp.bfloat16)
    tables_back = stack_tables(rel_back, x_back, y_back)
    table_total = jnp.zeros((tables_back.shape[0], tables_back.shape[1]), jnp.float32)
    index = 0
    grad_q_seq, grad_k_seq, grad_v_seq, table_total = attend_backward(
        query,
        key_rows,
        value_rows,
        tables_back,
        boxes[index],
        lengths[index],
        logsum_parts[index],
        grad_mixed,
        table_total,
    )
    grad_w_query = left_transposed(normed_one, grad_q_seq)
    grad_w_key = left_transposed(normed_one, grad_k_seq)
    grad_w_value = left_transposed(normed_one, grad_v_seq)
    grad_normed_one = (
        right_transposed(grad_q_seq, query_back)
        + right_transposed(grad_k_seq, key_back)
        + right_transposed(grad_v_seq, value_back)
    )
    unused_one, norm_one_pull = jax.vjp(norm_apply, rows, gain_one_back.astype(jnp.float32))
    rows_part, grad_gain_one = norm_one_pull(grad_normed_one)
    grad_inputs = (grad_hidden + rows_part).reshape(inputs.shape)
    grad_rel = table_total[:, :BUCKETS].reshape(-1)
    grad_x = table_total[:, BUCKETS : 2 * BUCKETS].reshape(-1)
    grad_y = table_total[:, 2 * BUCKETS :].reshape(-1)
    attn_shares = (
        lax.psum_scatter(grad_gain_one, ("wide", "narrow"), scatter_dimension=0, tiled=True),
        lax.psum_scatter(grad_w_query, ("wide", "narrow"), scatter_dimension=0, tiled=True),
        lax.psum_scatter(grad_w_key, ("wide", "narrow"), scatter_dimension=0, tiled=True),
        lax.psum_scatter(grad_w_value, ("wide", "narrow"), scatter_dimension=0, tiled=True),
        lax.psum_scatter(grad_w_out, ("wide", "narrow"), scatter_dimension=0, tiled=True),
        lax.psum_scatter(grad_rel, ("wide", "narrow"), scatter_dimension=0, tiled=True),
        lax.psum_scatter(grad_x, ("wide", "narrow"), scatter_dimension=0, tiled=True),
        lax.psum_scatter(grad_y, ("wide", "narrow"), scatter_dimension=0, tiled=True),
    )
    shares = attn_shares + ffn_shares
    return (
        output,
        grad_inputs,
        shares[0],
        shares[1],
        shares[2],
        shares[3],
        shares[4],
        shares[5],
        shares[6],
        shares[7],
        shares[8],
        shares[9],
        shares[10],
        shares[11],
    )


def solution(mesh):
    in_specs = (
        P(("wide", "narrow"), None, None),
        P(("wide", "narrow")),
        P(("wide", "narrow"), None),
        P(("wide", "narrow"), None),
        P(("wide", "narrow"), None),
        P(("wide", "narrow"), None),
        P(("wide", "narrow")),
        P(("wide", "narrow")),
        P(("wide", "narrow")),
        P(("wide", "narrow")),
        P(("wide", "narrow"), None),
        P(("wide", "narrow"), None),
        P(("wide", "narrow"), None),
        P(("wide", "narrow")),
        P(("wide", "narrow"), None, None),
        P(("wide", "narrow"), None, None),
    )
    out_specs = (
        P(("wide", "narrow"), None, None),
        P(("wide", "narrow"), None, None),
        P(("wide", "narrow")),
        P(("wide", "narrow"), None),
        P(("wide", "narrow"), None),
        P(("wide", "narrow"), None),
        P(("wide", "narrow"), None),
        P(("wide", "narrow")),
        P(("wide", "narrow")),
        P(("wide", "narrow")),
        P(("wide", "narrow")),
        P(("wide", "narrow"), None),
        P(("wide", "narrow"), None),
        P(("wide", "narrow"), None),
    )
    return jax.shard_map(local, mesh=mesh, in_specs=in_specs, out_specs=out_specs, check_vma=False)
```

profile of v0, /device:TPU:0, one launch (start us, length us, event | category | flops | bytes accessed | tf_op | source)
XLA Modules:
  0.0 1898.7 jit_solution(10287116350114028516)
XLA Ops:
  20.8 42.1 %all-reduce.11 = (bf16[1024]{0:T(1024)(128)(2,1)S(1)}, bf16[512]{0:T(512)(128)(2,1)S(1)}, bf16[512]{0:T(512)(128)(2,1)S(1)}, bf16[512]{0:T(512)(128)(2,1)S(1)}, bf16[1024]{0:T(1024)(128)(2,1)S(1)}) all-reduce(bf16[1024]{0:T(1024)(128)(2,1)S(1)} %dynamic-update-slice, ...), channel_id=1, replica_groups=mesh['wide'=16,'narrow'=2] {'wide','narrow'}, use_global_device_ids=true, to_apply=%add | all-reduce | flops 3584 | bytes 14336
  378.8 22.5 %fusion.354 = (f32[16,512]{1,0:T(8,128)S(1)}, f32[16,512,1024]{2,1,0:T(8,128)}) fusion(f32[16,512,1024]{2,1,0:T(8,128)} %copy-done, bf16[512,16,64]{0,2,1:T(8,128)(2,1)S(1)} %bitcast.614, bf16[1024,16,64]{0,2,1:T(8,128)(2,1)S(1)} %bitcast.572, pred[1024]{0:T(1024)(128)(4,1)S(1)} %copy-done.190), kind=kOutput, calls=%fused_computation.625 | convolution fusion | flops 1098899456 | bytes 70288384 | tf_op jit(solution)/shard_map/qhd,khd->hqk/dot_general | solution.py:140
  401.3 14.3 fusion.1
  420.5 15.3 fusion.154
  435.9 21.7 %fusion.355 = (f32[16,512]{1,0:T(8,128)S(1)}, f32[16,512,1024]{2,1,0:T(8,128)}) fusion(f32[16,512,1024]{2,1,0:T(8,128)} %constant_dynamic-update-slice_fusion, bf16[512,16,64]{0,2,1:T(8,128)(2,1)S(1)} %bitcast.612, bf16[1024,16,64]{0,2,1:T(8,128)(2,1)S(1)} %bitcast.573, pred[1024]{0:T(1024)(128)(4,1)S(1)} %copy-done.190), kind=kOutput, calls=%fused_computation.626 | convolution fusion | flops 1098899456 | bytes 70288384 | tf_op jit(solution)/shard_map/qhd,khd->hqk/dot_general | solution.py:140
  457.6 14.3 fusion
  471.9 14.5 fusion.155
  494.8 11.8 fusion.357
  506.6 12.0 fusion.356
  518.6 24.5 %multiply_convert_fusion = (bf16[1024,2816]{1,0:T(8,128)(2,1)}, bf16[1024,2816]{1,0:T(8,128)(2,1)}, bf16[1024,2816]{1,0:T(8,128)(2,1)}) fusion(f32[1024,2816]{1,0:T(8,128)} %fusion.356, f32[1024,2816]{1,0:T(8,128)} %fusion.357, bf16[2816,1024]{1,0:T(8,128)(2,1)} %all-gather.20.cloned.1.call-done, bf16[1,1024,1024]{2,1,0:T(8,128)(2,1)} %param.31), kind=kOutput, calls=%fused_computation.144 | convolution fusion | flops 5992087552 | bytes 48234496 | tf_op jit(solution)/shard_map/dot_general | solution.py:129
  543.1 10.0 fusion.358
  553.2 9.6 multiply_reduce_fusion.2
  576.7 15.4 fusion.36
  592.1 16.7 add_convert_fusion
  614.8 23.6 %multiply_reduce_fusion.1 = (f32[16,512]{1,0:T(8,128)S(1)}, f32[16,512,1024]{2,1,0:T(8,128)}) fusion(f32[16,512,1024]{2,1,0:T(8,128)} %get-tuple-element.273, f32[16,512]{1,0:T(8,128)S(1)} %log_add_fusion.1, bf16[512,16,64]{0,2,1:T(8,128)(2,1)} %bitcast.619, bf16[1024,16,64]{0,2,1:T(8,128)(2,1)} %bitcast.578), kind=kOutput, calls=%fused_computation.4 | convolution fusion | flops 1098899456 | bytes 70320128 | tf_op jit(solution)/shard_map/qhd,khd->hqk/dot_general | solution.py:185
  638.4 33.7 %subtract_multiply_fusion.1 = f32[16,512,1024]{2,1,0:T(8,128)} fusion(f32[16,512,1024]{2,1,0:T(8,128)} %get-tuple-element.280, f32[16,512,1024]{2,1,0:T(8,128)} %get-tuple-element.273, f32[16,512]{1,0:T(8,128)S(1)} %get-tuple-element.279, f32[16,512]{1,0:T(8,128)S(1)} %log_add_fusion.1), kind=kLoop, calls=%fused_computation.3 | loop fusion | flops 25165824 | bytes 100728832 | tf_op jit(solution)/shard_map/mul | solution.py:188
  672.1 14.4 fusion.148
  686.6 23.3 %multiply_reduce_fusion = (f32[16,512]{1,0:T(8,128)S(1)}, f32[16,512,1024]{2,1,0:T(8,128)}) fusion(f32[16,512,1024]{2,1,0:T(8,128)} %get-tuple-element.271, f32[16,512]{1,0:T(8,128)S(1)} %log_add_fusion, bf16[512,16,64]{0,2,1:T(8,128)(2,1)S(1)} %bitcast.617, bf16[1024,16,64]{0,2,1:T(8,128)(2,1)} %bitcast.579), kind=kOutput, calls=%fused_computation.1 | convolution fusion | flops 1098899456 | bytes 70320128 | tf_op jit(solution)/shard_map/qhd,khd->hqk/dot_general | solution.py:185
  709.9 33.5 %subtract_multiply_fusion = f32[16,512,1024]{2,1,0:T(8,128)} fusion(f32[16,512,1024]{2,1,0:T(8,128)} %get-tuple-element.278, f32[16,512,1024]{2,1,0:T(8,128)} %get-tuple-element.271, f32[16,512]{1,0:T(8,128)S(1)} %get-tuple-element.277, f32[16,512]{1,0:T(8,128)S(1)} %log_add_fusion), kind=kLoop, calls=%fused_computation | loop fusion | flops 25165824 | bytes 100728832 | tf_op jit(solution)/shard_map/mul | solution.py:188
  743.4 14.5 fusion.151
  764.8 15.6 fusion.114
  780.4 16.3 add_convert_fusion.1
  802.8 11.9 fusion.360
  814.7 11.8 fusion.359
  826.8 12.0 fusion.140
  838.7 11.5 fusion.138
  854.2 20.6 %fusion.348 = (f32[16,64,1024]{2,1,0:T(8,128)S(1)}, f32[16,64,1024]{2,1,0:T(8,128)S(1)}, f32[16,64,1024]{2,1,0:T(8,128)}, f32[16,64,1024]{2,1,0:T(8,128)}, f32[1...) fusion(f32[16,512,1024]{2,1,0:T(8,128)} %subtract_multiply_fusion.1), kind=kLoop, calls=%fused_computation.619 | loop fusion | bytes 67108864 | tf_op jit(solution)/shard_map/slice | solution.py:86
  883.6 21.0 %fusion.349 = (f32[16,64,1024]{2,1,0:T(8,128)S(1)}, f32[16,64,1024]{2,1,0:T(8,128)S(1)}, f32[16,64,1024]{2,1,0:T(8,128)}, f32[16,64,1024]{2,1,0:T(8,128)}, f32[1...) fusion(f32[16,512,1024]{2,1,0:T(8,128)} %subtract_multiply_fusion), kind=kLoop, calls=%fused_computation.620 | loop fusion | bytes 67108864 | tf_op jit(solution)/shard_map/slice | solution.py:86
  974.6 17.0 fusion.76
  991.6 17.1 fusion.72
  1008.6 17.4 fusion.44
  1026.1 15.7 fusion.48
  1041.8 15.7 fusion.52
  1057.6 15.3 fusion.56
  1073.0 15.1 fusion.60
  1088.1 15.1 fusion.64
  1103.3 15.3 fusion.68
  1118.7 15.1 fusion.80
  1133.9 15.1 fusion.84
  1149.1 15.3 fusion.88
  1164.5 15.1 fusion.92
  1179.6 15.1 fusion.96
  1194.9 15.4 fusion.100
  1210.4 15.4 fusion.201
  1226.1 42.3 %all-reduce.10 = (f32[1024]{0:T(1024)S(1)}, f32[512]{0:T(512)S(1)}, f32[512]{0:T(512)S(1)}, f32[512]{0:T(512)S(1)}, f32[1024]{0:T(1024)S(1)}) all-reduce(f32[1024]{0:T(1024)S(1)} %copy-done.189, f32[512]{0:T(512)S(1)} %reshape.2940, f32[512]{0:T(512)S(1)} %reshape.2941, ...), channel_id=2, replica_groups=mesh['wide'=16,'narrow'=2] {'wide','narrow'}, use_global_device_ids=true, to_apply=%region_11.12.clone | all-reduce | flops 3584 | bytes 28672
  1271.3 114.9 %reduce-scatter.18.cloned.1.call-done = f32[32,2816]{1,0:T(8,128)} async-done(((f32[1024,2816]{1,0:T(8,128)}), f32[32,2816]{1,0:T(8,128)}) %reduce-scatter.18.cloned.1.call-update) | async-done | bytes 360464 | tf_op jit(solution)/shard_map/reduce_scatter | solution.py:292
  1386.2 253.0 %reduce-scatter.16.cloned.1.call-done = f32[32,2816]{1,0:T(8,128)} async-done(((f32[1024,2816]{1,0:T(8,128)}), f32[32,2816]{1,0:T(8,128)}) %reduce-scatter.16.cloned.1.call-update) | async-done | bytes 360464 | tf_op jit(solution)/shard_map/reduce_scatter | solution.py:291
  1639.1 252.8 %reduce-scatter.20.cloned.1.call-done = f32[88,1024]{1,0:T(8,128)} async-done(((f32[2816,1024]{1,0:T(8,128)}), f32[88,1024]{1,0:T(8,128)}) %reduce-scatter.20.cloned.1.call-update) | async-done | bytes 360464 | tf_op jit(solution)/shard_map/reduce_scatter | solution.py:293
  (728 shorter events, 458.8 us)
Async XLA Ops:
  7.2 360.7 %all-gather.10.cloned.1.call-start = ((), (), s32[]{:S(2)}) async-start(), calls=%async_computation.8 | async-start | bytes 2162688 | tf_op jit(solution)/shard_map/all_gather | solution.py:234
  7.9 365.3 %all-gather.12.cloned.1.call-start = ((), (), s32[]{:S(2)}) async-start(), calls=%async_computation.9 | async-start | bytes 2162688 | tf_op jit(solution)/shard_map/all_gather | solution.py:235
  8.7 407.0 %all-gather.8.cloned.1.call-start = ((), (), s32[]{:S(2)}) async-start(), calls=%async_computation.7 | async-start | bytes 2162688 | tf_op jit(solution)/shard_map/all_gather | solution.py:236
  9.4 477.1 %all-gather.14.cloned.1.call-start = ((), (), s32[]{:S(2)}) async-start(), calls=%async_computation.10 | async-start | bytes 2162688 | tf_op jit(solution)/shard_map/all_gather | solution.py:237
  10.0 484.8 %all-gather.18.cloned.1.call-start = ((), (), s32[]{:S(2)}) async-start(), calls=%async_computation.12 | async-start | bytes 5947392 | tf_op jit(solution)/shard_map/all_gather | solution.py:258
  10.6 496.0 %all-gather.16.cloned.1.call-start = ((), (), s32[]{:S(2)}) async-start(), calls=%async_computation.11 | async-start | bytes 5947392 | tf_op jit(solution)/shard_map/all_gather | solution.py:257
  11.1 507.5 %all-gather.20.cloned.1.call-start = ((), (), s32[]{:S(2)}) async-start(), calls=%async_computation.13 | async-start | bytes 5947392 | tf_op jit(solution)/shard_map/all_gather | solution.py:259
  11.9 1259.4 %reduce-scatter.14.cloned.1.call-start = ((), (), s32[]{:S(2)}) async-start(), calls=%async_computation.17 | async-start | bytes 4325376 | tf_op jit(solution)/shard_map/reduce_scatter | solution.py:342
  334.6 25.3 %copy-start = (f32[16,512,1024]{2,1,0:T(8,128)}, f32[16,512,1024]{2,1,0:T(8,128)S(1)}, u32[]{:S(2)}) copy-start(f32[16,512,1024]{2,1,0:T(8,128)S(1)} %constant_dynamic-update-slice_fusion.8) | copy-start | bytes 100663296
  373.2 62.6 %copy-start.31 = (bf16[512,1024]{0,1:T(8,128)(2,1)}, bf16[512,1024]{0,1:T(8,128)(2,1)S(1)}, u32[]{:S(2)}) copy-start(bf16[512,1024]{0,1:T(8,128)(2,1)S(1)} %get-tuple-element.77) | copy-start | bytes 3145732
  378.8 57.1 %copy-start.1 = (bf16[1024,1024]{0,1:T(8,128)(2,1)}, bf16[1024,1024]{0,1:T(8,128)(2,1)S(1)}, u32[]{:S(2)}) copy-start(bf16[1024,1024]{0,1:T(8,128)(2,1)S(1)} %convolution_convert_fusion.1) | copy-start | bytes 6291460
  401.3 19.2 %copy-start.91 = (f32[16,512]{1,0:T(8,128)}, f32[16,512]{1,0:T(8,128)S(1)}, u32[]{:S(2)}) copy-start(f32[16,512]{1,0:T(8,128)S(1)} %get-tuple-element.270) | copy-start | bytes 98308
  420.5 51.4 %copy-start.7 = (bf16[1024,1024]{0,1:T(8,128)(2,1)}, bf16[1024,1024]{0,1:T(8,128)(2,1)S(1)}, u32[]{:S(2)}) copy-start(bf16[1024,1024]{0,1:T(8,128)(2,1)S(1)} %convolution_convert_fusion.3) | copy-start | bytes 6291460
  570.3 700.9 %reduce-scatter.12.cloned.1.call-start = ((), (), s32[]{:S(2)}) async-start(), calls=%async_computation.16 | async-start | bytes 4325376 | tf_op jit(solution)/shard_map/reduce_scatter | solution.py:341
  592.1 16.7 copy-start.181
  592.1 16.7 copy-start.185
  638.4 632.9 %reduce-scatter.8.cloned.1.call-start = ((), (), s32[]{:S(2)}) async-start(), calls=%async_computation.14 | async-start | bytes 4325376 | tf_op jit(solution)/shard_map/reduce_scatter | solution.py:339
  638.4 33.7 %copy-start.2 = (bf16[1024,1024]{0,1:T(8,128)(2,1)S(1)}, bf16[1024,1024]{0,1:T(8,128)(2,1)}, u32[]{:S(2)}) copy-start(bf16[1024,1024]{0,1:T(8,128)(2,1)} %copy-done.1) | copy-start | bytes 6291460
  764.3 16.1 copy-start.32
  764.3 507.0 %reduce-scatter.10.cloned.1.call-start = ((), (), s32[]{:S(2)}) async-start(), calls=%async_computation.15 | async-start | bytes 4325376 | tf_op jit(solution)/shard_map/reduce_scatter | solution.py:340
  780.4 16.3 copy-start.6
  802.7 583.5 %reduce-scatter.18.cloned.1.call-start = ((), (), s32[]{:S(2)}) async-start(), calls=%async_computation.19 | async-start | bytes 11894784 | tf_op jit(solution)/shard_map/reduce_scatter | solution.py:292
  814.7 824.5 %reduce-scatter.16.cloned.1.call-start = ((), (), s32[]{:S(2)}) async-start(), calls=%async_computation.18 | async-start | bytes 11894784 | tf_op jit(solution)/shard_map/reduce_scatter | solution.py:291
  826.5 1065.4 %reduce-scatter.20.cloned.1.call-start = ((), (), s32[]{:S(2)}) async-start(), calls=%async_computation.20 | async-start | bytes 11894784 | tf_op jit(solution)/shard_map/reduce_scatter | solution.py:293
  974.6 17.0 copy-start.45
  991.6 17.1 copy-start.43
  1008.6 17.4 copy-start.119
  1008.6 17.4 copy-start.173
  1008.6 17.4 copy-start.175
  1026.1 15.7 copy-start.117
  1026.1 15.7 copy-start.169
  1026.1 15.7 copy-start.171
  1041.8 15.8 copy-start.115
  1041.8 15.8 copy-start.165
  1041.8 15.7 copy-start.167
  1103.3 15.4 copy-start.106
  1103.3 15.4 copy-start.147
  1194.8 15.5 copy-start.38
  1194.8 15.5 copy-start.94
  1194.8 15.5 copy-start.123
  1194.8 15.5 copy-start.125
  1194.8 15.5 copy-start.198
  1194.8 15.5 copy-start.199
  1194.9 15.5 copy-start.200
  1194.9 15.5 copy-start.201
  1194.9 15.5 copy-start.202
  1210.4 15.7 copy-start.189
  1210.4 15.7 copy-start.191
  (169 other events, 1162.7 us)
Sparse Core Ops, SparseCore 0:
  11.0 59.5 all-gather.9
  73.5 55.5 all-gather.11
  132.2 55.3 all-gather.7
  190.4 55.3 all-gather.13
  248.6 66.0 all-gather.17
  317.5 66.2 all-gather.15
  386.6 66.2 all-gather.19
  570.5 141.3 reduce-scatter.13
  714.7 139.0 reduce-scatter.11
  856.5 138.1 reduce-scatter.7
  997.6 139.3 reduce-scatter.9
  1139.7 246.3 reduce-scatter.17
  1389.1 250.0 reduce-scatter.15
  1641.9 250.0 reduce-scatter.19
where the time goes:
time: 1910 us; the launch traced here: 1900 us
  matrix products  748 us (39%)
  waiting for transfers between devices  625 us (33%)
  local copies, waits for them, and re-layouts  302 us (16%)
  other arithmetic  119 us (6%)
  blocking collectives  84.4 us (4%)
    reduce_scatter x1, waiting for transfers between devices, local(): lax.psum_scatter(grad_w_gate, ('wide', 'narrow'), scatter_dimension=0, ti...  253 us
    reduce_scatter x1, waiting for transfers between devices, local(): lax.psum_scatter(grad_w_down, ('wide', 'narrow'), scatter_dimension=0, ti...  253 us
    dot_general x16, matrix products, table_grads(): lax.dot_general(piece, marks, (((1,), (1,)), ((), ())), precision=lax.Pre...  250 us
    unnamed x567, local copies, waits for them, and re-layouts  250 us
    reduce_scatter x1, waiting for transfers between devices, local(): lax.psum_scatter(grad_w_up, ('wide', 'narrow'), scatter_dimension=0, tile...  115 us
    dot_general x16, matrix products, block_bias(): jnp.dot(tables, marks, preferred_element_type=jnp.float32)  114 us
    unnamed x2, blocking collectives  84.4 us
    mul x2, other arithmetic, attend_backward(): probs * (grad_probs - jnp.sum(probs * grad_probs, axis=-1, keepdims=True))  67.2 us
  transfers between devices with their start and end apart: 14, of which 3 were waited for; matrix products, arithmetic and copies ran while one was open for 58% of the time, Pallas kernels for 0%

commit v1 on v0

v1 whole, which is shorter than its diff:
```python
import functools

import jax
import jax.numpy as jnp
import numpy as np
from jax import lax
from jax.experimental import pallas as pl
from jax.experimental.pallas import tpu as pltpu
from jax.sharding import PartitionSpec as P

HEADS = 16
HEAD_DIM = 64
BUCKETS = 32
AXES = ("wide", "narrow")

epsilon = 1e-06
coord_top = 1000
token_reach = 128
layout_reach = 256
masked_score = -1e30
gelu_scale = 0.7978845608028654

VMEM_LIMIT = 60 * 2**20
ROW_TILE = 256
STRIP = 16
BIAS_TILE = 128
DEAD_BUCKET = 16
CORE_BIT = 1


def params_for(flops, moved):
    return dict(
        compiler_params=pltpu.CompilerParams(vmem_limit_bytes=VMEM_LIMIT),
        cost_estimate=pl.CostEstimate(
            flops=int(flops), bytes_accessed=int(moved), transcendentals=0
        ),
    )


def bucket_table(span, buckets, reach):
    offsets = np.arange(-span, span + 1)
    half = buckets // 2
    exact = half // 2
    side = np.where(offsets > 0, half, 0)
    distance = np.abs(offsets)
    safe = np.maximum(distance, 1)
    large = exact + (np.log(safe / exact) / np.log(reach / exact) * (half - exact)).astype(np.int64)
    large = np.minimum(large, half - 1)
    return side + np.where(distance < exact, distance, large)


def magnitude_steps(span, reach):
    half = BUCKETS // 2
    exact = half // 2
    offsets = np.arange(span + 1)
    table = bucket_table(span, BUCKETS, reach)[span:]
    magnitude = table - np.where(offsets > 0, half, 0)
    steps = []
    for level in range(exact + 1, half):
        if (magnitude >= level).any():
            steps.append(int(np.argmax(magnitude >= level)))
    return steps


def bucket_index(offset, span, reach):
    half = BUCKETS // 2
    exact = half // 2
    distance = jnp.abs(offset)
    magnitude = jnp.minimum(distance, exact)
    for edge in magnitude_steps(span, reach):
        magnitude = magnitude + (distance >= edge).astype(jnp.int32)
    return magnitude + jnp.where(offset > 0, half, 0)


def rel_marks(slots, zero):
    places = np.arange(slots)
    offset = np.where(places < 768, places - zero, -300)
    table = bucket_table(slots - 1, BUCKETS, token_reach)
    return table[offset + slots - 1][None, :] == np.arange(BUCKETS)[:, None]


def write_marks(marks_ref, x_tile, y_tile):
    one = jnp.ones(x_tile.shape, jnp.bfloat16)
    zero = jnp.zeros(x_tile.shape, jnp.bfloat16)
    for b in range(BUCKETS):
        marks_ref[b * 16 : b * 16 + 16, :] = jnp.where(x_tile == b, one, zero)
        marks_ref[512 + b * 16 : 512 + b * 16 + 16, :] = jnp.where(y_tile == b, one, zero)


def index_kernel(len_ref, box_ref, turned_ref, ix_ref, iy_ref):
    place = lax.broadcasted_iota(jnp.int32, ix_ref.shape, 1)
    x_bucket = bucket_index(box_ref[0:1, :] - turned_ref[:, 0:1], coord_top, layout_reach)
    y_bucket = bucket_index(box_ref[1:2, :] - turned_ref[:, 1:2], coord_top, layout_reach)
    x_bucket = jnp.where(place < len_ref[0], x_bucket, DEAD_BUCKET)
    ix_ref[...] = x_bucket.astype(jnp.float32).astype(jnp.bfloat16)
    iy_ref[...] = y_bucket.astype(jnp.float32).astype(jnp.bfloat16)


def index_call(length, box):
    slots = box.shape[1]
    tile = pl.BlockSpec((BIAS_TILE, slots), lambda i: (i, 0))
    return pl.pallas_call(
        index_kernel,
        grid=(slots // BIAS_TILE,),
        in_specs=[
            pl.BlockSpec(memory_space=pltpu.SMEM),
            pl.BlockSpec((2, slots), lambda i: (0, 0)),
            pl.BlockSpec((BIAS_TILE, 2), lambda i: (i, 0)),
        ],
        out_specs=[tile, tile],
        out_shape=[jax.ShapeDtypeStruct((slots, slots), jnp.bfloat16)] * 2,
        name="index",
        **params_for(1e9, 4e6),
    )(length, box, box.T)


def prepare_kernel(tables_ref, marks_ref, lhs_ref, skew_ref):
    slots = marks_ref.shape[1]
    tables = tables_ref[...]
    rel_row = jnp.dot(
        tables[:, :BUCKETS], marks_ref[...], preferred_element_type=jnp.float32
    )
    for h in range(HEADS):
        wide = jnp.broadcast_to(rel_row[h : h + 1, :], (BIAS_TILE, slots))
        skew_ref[h] = pltpu.roll(wide, 0, 1, stride=1, stride_axis=0)[:, :640]
    tall, long = HEADS * 16, 2 * BUCKETS * 16
    layout = tables[:, BUCKETS:]
    dead = lax.broadcasted_iota(jnp.int32, layout.shape, 1) == DEAD_BUCKET
    layout = jnp.where(dead, jnp.asarray(masked_score, jnp.bfloat16), layout)
    head_of = lax.broadcasted_iota(jnp.int32, (tall, HEADS), 0) // 16
    pick_head = head_of == lax.broadcasted_iota(jnp.int32, (tall, HEADS), 1)
    bucket_of = lax.broadcasted_iota(jnp.int32, (2 * BUCKETS, long), 1) // 16
    pick_bucket = bucket_of == lax.broadcasted_iota(jnp.int32, (2 * BUCKETS, long), 0)
    by_head = jnp.dot(
        pick_head.astype(jnp.bfloat16), layout, preferred_element_type=jnp.float32
    ).astype(jnp.bfloat16)
    full = jnp.dot(
        by_head, pick_bucket.astype(jnp.bfloat16), preferred_element_type=jnp.float32
    )
    same = (
        lax.broadcasted_iota(jnp.int32, (tall, long), 0) % 16
        == lax.broadcasted_iota(jnp.int32, (tall, long), 1) % 16
    )
    lhs_ref[...] = jnp.where(same, full, 0.0).astype(jnp.bfloat16)


def prepare_call(tables, slots):
    return pl.pallas_call(
        prepare_kernel,
        out_shape=[
            jax.ShapeDtypeStruct((HEADS * 16, 2 * BUCKETS * 16), jnp.bfloat16),
            jax.ShapeDtypeStruct((HEADS, BIAS_TILE, 640), jnp.float32),
        ],
        name="prepare",
        **params_for(1e9, 6e6),
    )(tables, jnp.asarray(rel_marks(slots, 256)).astype(jnp.bfloat16))


def bias_kernel(first, ix_ref, iy_ref, lhs_ref, skew_ref, *rest):
    bias_ref, marks_ref = rest[-2:]
    block = pl.program_id(0) + first
    slots = ix_ref.shape[1]

    def body(t, carry):
        r0 = pl.multiple_of(t * 16, 16)
        write_marks(marks_ref, ix_ref[pl.ds(r0, 16), :], iy_ref[pl.ds(r0, 16), :])
        out = jnp.dot(lhs_ref[...], marks_ref[...], preferred_element_type=jnp.float32)
        for c in range(slots // 128):
            shift = pl.multiple_of((jnp.clip(c - block, -2, 2) + 2) * 128, 128)
            cols = slice(c * 128, c * 128 + 128)
            for h in range(HEADS):
                bias_ref[h, pl.ds(r0, 16), cols] = (
                    out[h * 16 : h * 16 + 16, cols]
                    + skew_ref[h, pl.ds(r0, 16), pl.ds(shift, 128)]
                )
        return carry

    lax.fori_loop(0, BIAS_TILE // 16, body, 0)


def bias_call(ix, iy, lhs, skew, begin, end, held=None):
    slots = ix.shape[0]
    tile = pl.BlockSpec((BIAS_TILE, slots), lambda i: (i + begin, 0))
    in_specs = [
        tile,
        tile,
        pl.BlockSpec(lhs.shape, lambda i: (0, 0)),
        pl.BlockSpec(skew.shape, lambda i: (0, 0, 0)),
    ]
    args = [ix, iy, lhs, skew]
    aliases = {}
    if held is not None:
        in_specs.append(pl.BlockSpec(memory_space=pl.ANY))
        args.append(held)
        aliases = {4: 0}
    share = (end - begin) * BIAS_TILE / slots
    return pl.pallas_call(
        functools.partial(bias_kernel, begin),
        grid=(end - begin,),
        in_specs=in_specs,
        out_specs=pl.BlockSpec((HEADS, BIAS_TILE, slots), lambda i: (0, i + begin, 0)),
        out_shape=jax.ShapeDtypeStruct((HEADS, slots, slots), jnp.float32),
        scratch_shapes=[pltpu.VMEM((2 * BUCKETS * 16, slots), jnp.bfloat16)],
        input_output_aliases=aliases,
        name="bias",
        **params_for(34e9 * share, 72e6 * share),
    )(*args)


def own_lanes(h):
    left = lax.broadcasted_iota(jnp.int32, (1, 128), 1) < HEAD_DIM
    return left if h == 0 else jnp.logical_not(left)


def attend_kernel(q_ref, k_ref, v_ref, bias_ref, probs_ref, mixed_ref):
    q, k, v = q_ref[...], k_ref[...], v_ref[...]
    outs = []
    for h in range(2):
        q_own = jnp.where(own_lanes(h), q, jnp.zeros_like(q))
        scores = lax.dot_general(
            q_own, k, (((1,), (1,)), ((), ())), preferred_element_type=jnp.float32
        )
        strips = []
        for r in range(0, q.shape[0], STRIP):
            strip = scores[r : r + STRIP] + bias_ref[h, r : r + STRIP, :]
            top = jnp.max(strip, axis=1, keepdims=True)
            weights = jnp.exp(strip - top)
            total = jnp.sum(weights, axis=1, keepdims=True)
            strips.append((weights * (1.0 / total)).astype(jnp.bfloat16))
        probs = jnp.concatenate(strips, axis=0)
        probs_ref[h] = probs
        outs.append(jnp.dot(probs, v, preferred_element_type=jnp.float32))
    mixed_ref[...] = jnp.where(own_lanes(0), outs[0], outs[1]).astype(jnp.bfloat16)


def attend_call(query, key_rows, value_rows, bias):
    slots, inner = query.shape
    pairs = inner // 128
    tile = min(ROW_TILE, slots)
    rows = pl.BlockSpec((tile, 128), lambda p, i: (i, p))
    square = pl.BlockSpec((2, tile, slots), lambda p, i: (p, i, 0))
    return pl.pallas_call(
        attend_kernel,
        grid=(pairs, slots // tile),
        in_specs=[
            rows,
            pl.BlockSpec((slots, 128), lambda p, i: (0, p)),
            pl.BlockSpec((slots, 128), lambda p, i: (0, p)),
            square,
        ],
        out_specs=[square, rows],
        out_shape=[
            jax.ShapeDtypeStruct((HEADS, slots, slots), jnp.bfloat16),
            jax.ShapeDtypeStruct((slots, inner), jnp.bfloat16),
        ],
        name="attend",
        **params_for(34e9, 100e6),
    )(query, key_rows, value_rows, bias)


def attend_back_kernel(q_ref, k_ref, v_ref, grad_ref, probs_ref, *rest):
    ds_ref, dq_ref, dk_ref, dv_ref, k_sum, v_sum = rest[-6:]
    step = pl.program_id(1)
    q, k, v, grad = q_ref[...], k_ref[...], v_ref[...], grad_ref[...]
    q_turned, grad_turned = q.T, grad.T

    @pl.when(step == 0)
    def _():
        k_sum[...] = jnp.zeros_like(k_sum)
        v_sum[...] = jnp.zeros_like(v_sum)

    outs = []
    for h in range(2):
        grad_own = jnp.where(own_lanes(h), grad, jnp.zeros_like(grad))
        grad_probs = lax.dot_general(
            grad_own, v, (((1,), (1,)), ((), ())), preferred_element_type=jnp.float32
        )
        strips = []
        for r in range(0, q.shape[0], STRIP):
            probs = probs_ref[h, r : r + STRIP, :].astype(jnp.float32)
            terms = probs * grad_probs[r : r + STRIP]
            delta = jnp.sum(terms, axis=1, keepdims=True)
            strips.append((terms - probs * delta).astype(jnp.bfloat16))
        ds = jnp.concatenate(strips, axis=0)
        ds_ref[h] = ds
        outs.append(jnp.dot(ds, k, preferred_element_type=jnp.float32))
        own = slice(h * HEAD_DIM, (h + 1) * HEAD_DIM)
        k_sum[own, :] += jnp.dot(q_turned[own], ds, preferred_element_type=jnp.float32)
        v_sum[own, :] += jnp.dot(
            grad_turned[own], probs_ref[h], preferred_element_type=jnp.float32
        )
    dq_ref[...] = jnp.where(own_lanes(0), outs[0], outs[1]).astype(jnp.bfloat16)

    @pl.when(step == pl.num_programs(1) - 1)
    def _():
        dk_ref[...] = k_sum[...].T.astype(jnp.bfloat16)
        dv_ref[...] = v_sum[...].T.astype(jnp.bfloat16)


def attend_back_call(query, key_rows, value_rows, grad_mixed, probs, begin, end, held=None):
    slots, inner = query.shape
    tile = min(ROW_TILE, slots)
    rows = pl.BlockSpec((tile, 128), lambda p, i: (i, p + begin))
    whole = pl.BlockSpec((slots, 128), lambda p, i: (0, p + begin))
    square = pl.BlockSpec((2, tile, slots), lambda p, i: (p + begin, i, 0))
    args = [query, key_rows, value_rows, grad_mixed, probs]
    in_specs = [rows, whole, whole, rows, square]
    aliases = {}
    if held is not None:
        aliases = {len(args) + at: at for at in range(len(held))}
        in_specs += [pl.BlockSpec(memory_space=pl.ANY)] * len(held)
        args += list(held)
    share = (end - begin) * 128 / inner
    return pl.pallas_call(
        attend_back_kernel,
        grid=(end - begin, slots // tile),
        in_specs=in_specs,
        out_specs=[square, rows, whole, whole],
        out_shape=[jax.ShapeDtypeStruct((HEADS, slots, slots), jnp.bfloat16)]
        + [jax.ShapeDtypeStruct((slots, inner), jnp.bfloat16)] * 3,
        scratch_shapes=[pltpu.VMEM((128, slots), jnp.float32)] * 2,
        input_output_aliases=aliases,
        name="attend_back",
        **params_for(34e9 * share, 72e6 * share),
    )(*args)


def table_kernel(
    first, ds_ref, ix_ref, iy_ref, layout_ref, rel_ref, layout_sum, rel_sum, marks_ref
):
    step = pl.program_id(0)
    block = step + first
    slots = ix_ref.shape[1]

    @pl.when(step == 0)
    def _():
        layout_sum[...] = jnp.zeros_like(layout_sum)
        rel_sum[...] = jnp.zeros_like(rel_sum)

    def body(t, carry):
        r0 = pl.multiple_of(t * 16, 16)
        write_marks(marks_ref, ix_ref[pl.ds(r0, 16), :], iy_ref[pl.ds(r0, 16), :])
        ds = ds_ref[:, pl.ds(r0, 16), :].reshape(HEADS * 16, slots)
        layout_sum[...] += lax.dot_general(
            marks_ref[...], ds, (((1,), (1,)), ((), ())), preferred_element_type=jnp.float32
        )
        for c in range(slots // 128):
            shift = pl.multiple_of((jnp.clip(c - block, -2, 2) + 2) * 128, 128)
            cols = slice(c * 128, c * 128 + 128)
            for h in range(HEADS):
                rel_sum[h, pl.ds(r0, 16), pl.ds(shift, 128)] += ds_ref[
                    h, pl.ds(r0, 16), cols
                ].astype(jnp.float32)
        return carry

    lax.fori_loop(0, BIAS_TILE // 16, body, 0)

    @pl.when(step == pl.num_programs(0) - 1)
    def _():
        shape = layout_sum.shape
        same = (
            lax.broadcasted_iota(jnp.int32, shape, 0) % 16
            == lax.broadcasted_iota(jnp.int32, shape, 1) % 16
        )
        kept = jnp.where(same, layout_sum[...], 0.0)
        layout_ref[...] = kept.reshape(2 * BUCKETS, 16, HEADS * 16).sum(axis=1)
        tall = (BIAS_TILE, BIAS_TILE)
        flip = (
            lax.broadcasted_iota(jnp.int32, tall, 0) + lax.broadcasted_iota(jnp.int32, tall, 1)
            == BIAS_TILE - 1
        ).astype(jnp.float32)
        for h in range(HEADS):
            upside = jnp.dot(
                flip,
                rel_sum[h],
                precision=lax.Precision.HIGHEST,
                preferred_element_type=jnp.float32,
            )
            padded = jnp.concatenate(
                [upside, jnp.zeros((BIAS_TILE, slots - 640), jnp.float32)], axis=1
            )
            back = pltpu.roll(padded, 0, 1, stride=1, stride_axis=0)
            rel_ref[h : h + 1, :] = jnp.sum(back, axis=0, keepdims=True)


def table_call(ds, ix, iy, begin, end):
    slots = ix.shape[0]
    tile = pl.BlockSpec((BIAS_TILE, slots), lambda i: (i + begin, 0))
    share = (end - begin) * BIAS_TILE / slots
    return pl.pallas_call(
        functools.partial(table_kernel, begin),
        grid=(end - begin,),
        in_specs=[
            pl.BlockSpec((HEADS, BIAS_TILE, slots), lambda i: (0, i + begin, 0)),
            tile,
            tile,
        ],
        out_specs=[
            pl.BlockSpec((2 * BUCKETS, HEADS * 16), lambda i: (0, 0)),
            pl.BlockSpec((HEADS, slots), lambda i: (0, 0)),
        ],
        out_shape=[
            jax.ShapeDtypeStruct((2 * BUCKETS, HEADS * 16), jnp.float32),
            jax.ShapeDtypeStruct((HEADS, slots), jnp.float32),
        ],
        scratch_shapes=[
            pltpu.VMEM((2 * BUCKETS * 16, HEADS * 16), jnp.float32),
            pltpu.VMEM((HEADS, BIAS_TILE, 640), jnp.float32),
            pltpu.VMEM((2 * BUCKETS * 16, slots), jnp.bfloat16),
        ],
        name="table_back",
        **params_for(34e9 * share, 36e6 * share),
    )(ds, ix, iy)


def table_finish(parts, slots):
    layout = sum(part[0] for part in parts)
    rel = sum(part[1] for part in parts)
    layout = layout.reshape(2 * BUCKETS, HEADS, 16).sum(axis=2).T
    rel = lax.dot_general(
        rel,
        jnp.asarray(rel_marks(slots, 383)).astype(jnp.float32),
        (((1,), (1,)), ((), ())),
        precision=lax.Precision.HIGHEST,
        preferred_element_type=jnp.float32,
    )
    return rel, layout[:, :BUCKETS], layout[:, BUCKETS:]


def ffn_kernel(
    n_ref, turned_ref, seed_ref, hidden_ref, gate_ref, up_ref, down_ref,
    out_ref, dn_ref, dgate_ref, dup_ref, ddown_ref, out_sum, dn_sum,
):
    step = pl.program_id(0)

    @pl.when(step == 0)
    def _():
        out_sum[...] = hidden_ref[...]
        dn_sum[...] = jnp.zeros_like(dn_sum)

    seed = seed_ref[...]
    w_gate, w_up, w_down = gate_ref[...], up_ref[...], down_ref[...]
    gate = jnp.dot(n_ref[...], w_gate, preferred_element_type=jnp.float32)
    upper = jnp.dot(n_ref[...], w_up, preferred_element_type=jnp.float32)
    grad_act = lax.dot_general(
        seed, w_down, (((1,), (1,)), ((), ())), preferred_element_type=jnp.float32
    )
    square = gate * gate
    tanh = jnp.tanh(gelu_scale * (gate + 0.044715 * gate * square))
    cdf = 0.5 * (1.0 + tanh)
    gelu = gate * cdf
    slope = cdf + 0.5 * gate * (1.0 - tanh * tanh) * gelu_scale * (1.0 + 3 * 0.044715 * square)
    activated = (gelu * upper).astype(jnp.bfloat16)
    grad_gate = (grad_act * upper * slope).astype(jnp.bfloat16)
    grad_upper = (grad_act * gelu).astype(jnp.bfloat16)
    out_sum[...] += jnp.dot(activated, w_down, preferred_element_type=jnp.float32)
    dn_sum[...] += lax.dot_general(
        grad_gate, w_gate, (((1,), (1,)), ((), ())), preferred_element_type=jnp.float32
    ) + lax.dot_general(
        grad_upper, w_up, (((1,), (1,)), ((), ())), preferred_element_type=jnp.float32
    )
    dgate_ref[...] = jnp.dot(
        turned_ref[...], grad_gate, preferred_element_type=jnp.float32
    ).astype(jnp.bfloat16)
    dup_ref[...] = jnp.dot(
        turned_ref[...], grad_upper, preferred_element_type=jnp.float32
    ).astype(jnp.bfloat16)
    ddown_ref[...] = lax.dot_general(
        activated, seed, (((0,), (0,)), ((), ())), preferred_element_type=jnp.float32
    ).astype(jnp.bfloat16)

    @pl.when(step == pl.num_programs(0) - 1)
    def _():
        out_ref[...] = out_sum[...].astype(jnp.bfloat16)
        dn_ref[...] = dn_sum[...]


def ffn_call(normed, turned, seed, hidden, packed, first, w_down):
    slots, width = normed.shape
    ff = w_down.shape[0]
    tile = 256
    count = ff // tile
    full = pl.BlockSpec((slots, width), lambda f: (0, 0))
    turned_full = pl.BlockSpec((width, slots), lambda f: (0, 0))
    column = pl.BlockSpec((width, tile), lambda f: (0, f))
    return pl.pallas_call(
        ffn_kernel,
        grid=(count,),
        in_specs=[
            full,
            turned_full,
            full,
            full,
            pl.BlockSpec((width, tile), lambda f: (0, f + first)),
            pl.BlockSpec((width, tile), lambda f: (0, f + first + count)),
            pl.BlockSpec((tile, width), lambda f: (f, 0)),
        ],
        out_specs=[full, full, column, column, pl.BlockSpec((tile, width), lambda f: (f, 0))],
        out_shape=[
            jax.ShapeDtypeStruct((slots, width), jnp.bfloat16),
            jax.ShapeDtypeStruct((slots, width), jnp.float32),
            jax.ShapeDtypeStruct((width, ff), jnp.bfloat16),
            jax.ShapeDtypeStruct((width, ff), jnp.bfloat16),
            jax.ShapeDtypeStruct((ff, width), jnp.bfloat16),
        ],
        scratch_shapes=[pltpu.VMEM((slots, width), jnp.float32)] * 2,
        name="ffn",
        **params_for(18 * slots * width * ff, 50e6),
    )(normed, turned, seed, hidden, packed, packed, w_down)


def unpack_kernel(down_rows, part_rows, packed_ref, out_ref):
    width = out_ref.shape[1]
    for at in range(out_ref.shape[0] // down_rows):
        for group in range(-(-down_rows // part_rows)):
            count = min(part_rows, down_rows - group * part_rows)
            here = at * down_rows + group * part_rows
            out_ref[here : here + count, :] = packed_ref[
                at * part_rows : at * part_rows + count, group * width : (group + 1) * width
            ]


def unpack_call(packed, first, down_rows, part_rows, width):
    count = packed.shape[0] // part_rows
    groups = -(-down_rows // part_rows)
    joint = 1
    while (joint * down_rows) % 16 or (joint * part_rows) % 16:
        joint *= 2
    return pl.pallas_call(
        functools.partial(unpack_kernel, down_rows, part_rows),
        grid=(count // joint,),
        in_specs=[
            pl.BlockSpec(
                (joint * part_rows, groups * width), lambda d: (d, first // (groups * width))
            )
        ],
        out_specs=pl.BlockSpec((joint * down_rows, width), lambda d: (d, 0)),
        out_shape=jax.ShapeDtypeStruct((count * down_rows, width), jnp.bfloat16),
        name="unpack",
        **params_for(1e6, 12e6),
    )(packed)


class Exchange:
    def __init__(self, mesh):
        self.count = mesh.shape["wide"] * mesh.shape["narrow"]
        self.bits = self.count.bit_length() - 1
        assert self.count == 1 << self.bits
        one, two, three, *tail = [b for b in range(self.bits) if b != CORE_BIT]
        self.orders = (
            [CORE_BIT, one, two] + tail + [three],
            [CORE_BIT, two, three, one] + tail,
            [CORE_BIT, three, one, two] + tail,
        )

    def mine(self, bit):
        return (lax.axis_index(AXES) >> bit) & 1

    def swap(self, value, bit):
        pairs = [(d, d ^ (1 << bit)) for d in range(self.count)]
        return lax.ppermute(value, AXES, pairs)

    def spread(self, shard):
        copies = jnp.broadcast_to(shard[None, :], (self.count, shard.shape[0]))
        return lax.all_to_all(copies, AXES, 0, 0, tiled=True)

    def sum_small(self, terms):
        return jnp.sum(lax.all_to_all(terms, AXES, 0, 0, tiled=True), axis=0)


class Gather:
    def __init__(self, exchange, shard, order):
        self.exchange = exchange
        self.value = shard
        self.steps = list(reversed(exchange.orders[order]))
        self.held = []
        self.flight = None

    def done(self):
        return not self.steps

    def go(self):
        self.flight = self.exchange.swap(self.value, self.steps[0])

    def land(self):
        bit = self.steps.pop(0)
        other, self.flight = self.flight, None
        spot = sum(b > bit for b in self.held)
        high = self.exchange.mine(bit) == 1
        self.value = jnp.stack(
            [jnp.where(high, other, self.value), jnp.where(high, self.value, other)], axis=spot
        )
        self.held.append(bit)


class Scatter:
    def __init__(self, exchange, terms, order):
        self.exchange = exchange
        rows = terms.shape[0] // exchange.count
        self.value = terms.reshape((2,) * exchange.bits + (rows,) + terms.shape[1:])
        self.steps = list(exchange.orders[order])
        self.held = list(range(exchange.bits - 1, -1, -1))
        self.flight = None

    def done(self):
        return not self.steps

    def go(self):
        bit = self.steps[0]
        self.spot = self.held.index(bit)
        away = lax.dynamic_index_in_dim(
            self.value, 1 - self.exchange.mine(bit), self.spot, keepdims=False
        )
        self.flight = self.exchange.swap(away, bit)

    def land(self):
        bit = self.steps.pop(0)
        other, self.flight = self.flight, None
        stay = lax.dynamic_index_in_dim(
            self.value, self.exchange.mine(bit), self.spot, keepdims=False
        )
        value = stay.astype(jnp.float32) + other.astype(jnp.float32)
        if self.steps:
            value = value.astype(jnp.bfloat16)
        self.value = value
        self.held.pop(self.spot)


class Traffic:
    limit = 5

    def __init__(self):
        self.tasks = []

    def add(self, *tasks):
        self.tasks += tasks
        self.send()

    def send(self):
        busy = sum(task.flight is not None for task in self.tasks)
        for task in self.tasks:
            if task.flight is None and busy < self.limit:
                task.go()
                busy += 1

    def step(self, *work):
        flying = [task for task in self.tasks if task.flight is not None]
        work, flights = lax.optimization_barrier((work, [task.flight for task in flying]))
        for task, flight in zip(flying, flights):
            task.flight = flight
            task.land()
        self.tasks = [task for task in self.tasks if not task.done()]
        self.send()
        return work[0] if len(work) == 1 else work


def norm_apply(values, gain):
    return values * lax.rsqrt(jnp.mean(values * values, axis=-1, keepdims=True) + epsilon) * gain


def plain_product(left, right):
    return jnp.dot(left, right, preferred_element_type=jnp.float32)


def left_transposed(left, right):
    return lax.dot_general(
        left, right, (((0,), (0,)), ((), ())), preferred_element_type=jnp.float32
    )


def right_transposed(left, right):
    return lax.dot_general(
        left, right, (((1,), (1,)), ((), ())), preferred_element_type=jnp.float32
    )


def layer(
    exchange, inputs, norm_first, w_query, w_key, w_value, w_out, rel_table, x_table, y_table,
    norm_second, w_gate, w_up, w_down, lengths, boxes, cotangent,
):
    seq_count, slots, width = inputs.shape
    inner = w_query.shape[1]
    count = exchange.count
    entries = rel_table.shape[0]
    span = norm_first.shape[0]

    rows = inputs.reshape(slots, width).astype(jnp.float32)
    seed = cotangent.reshape(slots, width)
    traffic = Traffic()
    qkv_tasks = [
        Gather(exchange, shard, order) for order, shard in enumerate((w_query, w_key, w_value))
    ]
    traffic.add(*qkv_tasks)
    small = exchange.spread(
        jnp.concatenate([norm_first, norm_second, rel_table, x_table, y_table])
    )
    down_rows, part_rows = w_down.shape[0], w_out.shape[0]
    groups = -(-down_rows // part_rows)
    down_pad = jnp.pad(w_down, ((0, groups * part_rows - down_rows), (0, 0)))
    down_pad = [down_pad[at * part_rows : (at + 1) * part_rows] for at in range(groups)]
    packed = lax.all_gather(
        jnp.concatenate(down_pad + [w_out, w_gate, w_up], axis=1), AXES, axis=0, tiled=True
    )
    ix, iy = index_call(lengths, boxes[0])
    gain_one = small[:, :span].reshape(-1).astype(jnp.float32)
    gain_two = small[:, span : 2 * span].reshape(-1).astype(jnp.float32)
    tables = jnp.concatenate(
        [
            small[:, 2 * span + at * entries : 2 * span + (at + 1) * entries].reshape(
                HEADS, BUCKETS
            )
            for at in range(3)
        ],
        axis=1,
    )
    lhs, skew = prepare_call(tables, slots)
    blocks = slots // BIAS_TILE
    pieces = exchange.bits - 1
    bias = None
    for piece in range(pieces):
        begin, end = piece * blocks // pieces, (piece + 1) * blocks // pieces
        if bias is None:
            lhs = traffic.step(lhs)
        else:
            lhs, bias = traffic.step(lhs, bias)
        if end > begin:
            bias = bias_call(ix, iy, lhs, skew, begin, end, bias)
    normed_one = norm_apply(rows, gain_one).astype(jnp.bfloat16)
    normed_one, bias = traffic.step(normed_one, bias)
    query_full, key_full, value_full = (
        task.value.reshape(-1, task.value.shape[-1]) for task in qkv_tasks
    )
    query = plain_product(normed_one, query_full).astype(jnp.bfloat16)
    key_rows = plain_product(normed_one, key_full).astype(jnp.bfloat16)
    value_rows = plain_product(normed_one, value_full).astype(jnp.bfloat16)
    probs, mixed = attend_call(query, key_rows, value_rows, bias)
    first = groups * width
    out_full = packed[:, first : first + width]
    down_full = unpack_call(packed, 0, down_rows, part_rows, width)
    hidden = rows + plain_product(mixed, out_full)
    normed_two = norm_apply(hidden, gain_two).astype(jnp.bfloat16)
    output, grad_normed_two, d_gate, d_up, d_down = ffn_call(
        normed_two, normed_two.T, seed, hidden, packed, (first + width) // 256, down_full
    )
    ffn_tasks = [Scatter(exchange, part, at) for at, part in enumerate((d_gate, d_up, d_down))]
    traffic.add(*ffn_tasks)
    unused_two, norm_two_pull = jax.vjp(norm_apply, hidden, gain_two)
    hidden_part, grad_gain_two = norm_two_pull(grad_normed_two)
    grad_hidden = seed.astype(jnp.float32) + hidden_part
    branch_low = grad_hidden.astype(jnp.bfloat16)
    d_out = left_transposed(mixed, branch_low).astype(jnp.bfloat16)
    grad_mixed = right_transposed(branch_low, out_full).astype(jnp.bfloat16)
    grad_mixed, d_out = traffic.step(grad_mixed, d_out)
    out_task = Scatter(exchange, d_out, 0)
    traffic.add(out_task)
    pairs = inner // 128
    cuts = (0, pairs // 2, pairs)
    back = None
    for begin, end in zip(cuts[:-1], cuts[1:]):
        back = attend_back_call(
            query, key_rows, value_rows, grad_mixed, probs, begin, end, back
        )
        back = traffic.step(back)
    ds, dq, dk, dv = back
    d_weights = [left_transposed(normed_one, part).astype(jnp.bfloat16) for part in (dq, dk, dv)]
    dq, d_weights = traffic.step(dq, d_weights)
    w_tasks = [Scatter(exchange, part, at) for at, part in enumerate(d_weights)]
    traffic.add(*w_tasks)
    grad_normed_one = (
        right_transposed(dq, query_full)
        + right_transposed(dk, key_full)
        + right_transposed(dv, value_full)
    )
    unused_one, norm_one_pull = jax.vjp(norm_apply, rows, gain_one)
    rows_part, grad_gain_one = norm_one_pull(grad_normed_one)
    grad_inputs = (grad_hidden + rows_part).reshape(inputs.shape)
    parts = []
    pieces = 3
    grad_inputs, ix = traffic.step(grad_inputs, ix)
    for piece in range(pieces):
        begin, end = piece * blocks // pieces, (piece + 1) * blocks // pieces
        parts.append(table_call(ds, ix, iy, begin, end))
        ix, parts = traffic.step(ix, parts)
    grad_rel, grad_x, grad_y = table_finish(parts, slots)
    g_small = exchange.sum_small(
        jnp.concatenate(
            [
                part.reshape(count, -1)
                for part in (grad_gain_one, grad_gain_two, grad_rel, grad_x, grad_y)
            ],
            axis=1,
        )
    )
    while traffic.tasks:
        g_small = traffic.step(g_small)
    g_gate, g_up, g_down = (task.value for task in ffn_tasks)
    edges = [0, span, 2 * span, 2 * span + entries, 2 * span + 2 * entries, g_small.shape[0]]
    g_small = [g_small[a:b] for a, b in zip(edges[:-1], edges[1:])]
    return (
        output.reshape(inputs.shape),
        grad_inputs,
        g_small[0],
        w_tasks[0].value,
        w_tasks[1].value,
        w_tasks[2].value,
        out_task.value,
        g_small[2],
        g_small[3],
        g_small[4],
        g_small[1],
        g_gate,
        g_up,
        g_down,
    )


def solution(mesh):
    exchange = Exchange(mesh)
    vector, matrix, cube = P(AXES), P(AXES, None), P(AXES, None, None)
    in_specs = (
        (cube, vector)
        + (matrix,) * 4
        + (vector,) * 4
        + (matrix,) * 3
        + (vector, cube, cube)
    )
    out_specs = (cube, cube, vector) + (matrix,) * 4 + (vector,) * 4 + (matrix,) * 3

    def local(*args):
        return layer(exchange, *args)

    return jax.shard_map(local, mesh=mesh, in_specs=in_specs, out_specs=out_specs, check_vma=False)
```

time: 1910 us -> 672 us (0.35)
  matrix products: 748 us -> 41.7 us
  waiting for transfers between devices: 625 us -> 37.9 us
  Pallas kernels: 0 us -> 370 us
  local copies, waits for them, and re-layouts: 302 us -> 70 us
  blocking collectives: 84.4 us -> 0 us
  starting transfers between devices: 1.14 us -> 58.8 us
  other arithmetic: 119 us -> 66.6 us
    reduce_scatter x7 -> x0, waiting for transfers between devices: 621 us -> none  [the longest x1 253 us: local(): lax.psum_scatter(grad_w_gate, ('wide', 'narrow'), scatter_dimension=0, ti...]
    dot_general x44 -> x1, matrix products: 578 us -> 0.14 us  [table_finish(): lax.dot_general(rel, jnp.asarray(rel_marks(slots, 383)).astype(jnp.float3...]
    pallas_call x0 -> x14, Pallas kernels: none -> 370 us  [the longest x3 80.3 us: table_call(): pl.pallas_call(functools.partial(table_kernel, begin), grid=(end - begin,...]
    unnamed x567 -> x169, local copies, waits for them, and re-layouts: 250 us -> 23.3 us
    unnamed x2 -> x0, blocking collectives: 84.4 us -> none
    mul x2 -> x0, other arithmetic: 67.2 us -> none  [attend_backward(): probs * (grad_probs - jnp.sum(probs * grad_probs, axis=-1, keepdims=True))]
    ppermute x0 -> x50, starting transfers between devices: none -> 48.9 us  [swap(): return lax.ppermute(value, AXES, pairs)]
    dot_general x7 -> x4, matrix products: 58.3 us -> 12.1 us  [left_transposed(): lax.dot_general(left, right, (((0,), (0,)), ((), ())), preferred_element_...]
  transfers between devices with their start and end apart: 14 -> 53, of which waited for: 3 -> 9; matrix products, arithmetic and copies ran while one was open for 58% -> 18% of each run, Pallas kernels for 0% -> 44%
where the time goes in v1:
time: 672 us; the launch traced here: 661 us
  Pallas kernels  370 us (55%)
  local copies, waits for them, and re-layouts  70 us (10%)
  other arithmetic  66.6 us (10%)
  starting transfers between devices  58.8 us (9%)
  matrix products  41.7 us (6%)
  waiting for transfers between devices  37.9 us (6%)
  between operations  16.7 us (2%)
    pallas_call x3, Pallas kernels, table_call(): pl.pallas_call(functools.partial(table_kernel, begin), grid=(end - begin,...  80.3 us
    pallas_call x4, Pallas kernels, bias_call(): pl.pallas_call(functools.partial(bias_kernel, begin), grid=(end - begin,)...  70.8 us
    pallas_call x1, Pallas kernels, ffn_call(): pl.pallas_call(ffn_kernel, grid=(count,), in_specs=[full, turned_full, fu...  69.9 us
    pallas_call x2, Pallas kernels, attend_back_call(): pl.pallas_call(attend_back_kernel, grid=(end - begin, slots // tile), in_...  62 us
    pallas_call x1, Pallas kernels, attend_call(): pl.pallas_call(attend_kernel, grid=(pairs, slots // tile), in_specs=[rows...  58.7 us
    ppermute x50, starting transfers between devices, swap(): return lax.ppermute(value, AXES, pairs)  48.9 us
    ppermute x50, waiting for transfers between devices, swap(): return lax.ppermute(value, AXES, pairs)  31.4 us
    convert_element_type x28, other arithmetic, land(): value = value.astype(jnp.bfloat16)  25.1 us
  transfers between devices with their start and end apart: 53, of which 9 were waited for; matrix products, arithmetic and copies ran while one was open for 18% of the time, Pallas kernels for 44%

profile of v1, /device:TPU:0, one launch (start us, length us, event | category | flops | bytes accessed | tf_op | source)
XLA Modules:
  0.0 661.5 jit_solution(10418884894226783388)
XLA Ops:
  13.4 3.4 concatenate.12
  17.5 7.3 %all-to-all-start = ((bf16[32,1,112]{2,1,0:T(2,128)(2,1)}), bf16[32,1,112]{2,1,0:T(2,128)(2,1)S(1)}, u32[]{:S(2)}, u32[]{:S(2)}) async-start(bf16[32,1,112]{2,1,0:T(2,128)(2,1)} %broadcast_in_dim.6), calls=%async_computation | async-start | bytes 32768 | tf_op jit(solution)/shard_map/all_to_all | solution.py:565
  26.6 2.4 collective-permute-start.1
  32.5 12.0 %index.1 = (bf16[1024,1024]{1,0:T(8,128)(2,1)}, bf16[1024,1024]{1,0:T(8,128)(2,1)}) custom-call(s32[1]{0:T(128)S(6)} %copy.207.len_ref, s32[2,1024]{1,0:T(2,128)} %copy.120.box_ref, s32[1024,2]{1,0:T(8,128)} %bitcast.342), custom_call_target="tpu_custom_call" | custom-call | flops 1000000000 | bytes 4000000 | tf_op jit(solution)/shard_map/index/pallas_call | solution.py:102
  46.3 5.2 prepare.1
  51.6 2.5 collective-permute-start.3
  57.2 17.6 %bias.4.rest_0_ = f32[16,1024,1024]{2,1,0:T(8,128)} custom-call(bf16[1024,1024]{1,0:T(8,128)(2,1)} %get-tuple-element.216.ix_ref, bf16[1024,1024]{1,0:T(8,128)(2,1)} %get-tuple-element.131.iy_ref, bf16[256,1024]{1,0:T(8,128)(2,1)} %get-tuple-element.148.lhs_ref, f32[16,128,640]{2,1,0:T(8,128)} %get-tuple-element.134.skew_ref), custom_call_target="tpu_custom_call" | custom-call | flops 8499999744 | bytes 18000000 | tf_op jit(solution)/shard_map/bias/pallas_call | solution.py:197
  76.8 17.7 %bias.5.rest_0_ = f32[16,1024,1024]{2,1,0:T(8,128)} custom-call(bf16[1024,1024]{1,0:T(8,128)(2,1)} %get-tuple-element.216.ix_ref, bf16[1024,1024]{1,0:T(8,128)(2,1)} %get-tuple-element.131.iy_ref, bf16[256,1024]{1,0:T(8,128)(2,1)} %get-tuple-element.148.lhs_ref, f32[16,128,640]{2,1,0:T(8,128)} %get-tuple-element.134.skew_ref, ...), custom_call_target="tpu_custom_call", output_to_operand_aliasing={{}: (4, {})} | custom-call | flops 8499999744 | bytes 18000000 | tf_op jit(solution)/shard_map/bias/pallas_call | solution.py:197
  103.0 17.6 %bias.6.rest_0_ = f32[16,1024,1024]{2,1,0:T(8,128)} custom-call(bf16[1024,1024]{1,0:T(8,128)(2,1)} %get-tuple-element.216.ix_ref, bf16[1024,1024]{1,0:T(8,128)(2,1)} %get-tuple-element.131.iy_ref, bf16[256,1024]{1,0:T(8,128)(2,1)} %get-tuple-element.148.lhs_ref, f32[16,128,640]{2,1,0:T(8,128)} %get-tuple-element.134.skew_ref, ...), custom_call_target="tpu_custom_call", output_to_operand_aliasing={{}: (4, {})} | custom-call | flops 8499999744 | bytes 18000000 | tf_op jit(solution)/shard_map/bias/pallas_call | solution.py:197
  120.7 10.9 %collective-permute-done.11 = bf16[2,2,2,32,1024]{4,3,2,1,0:T(8,128)(2,1)} collective-permute-done((bf16[2,2,2,32,1024]{4,3,2,1,0:T(8,128)(2,1)}, bf16[2,2,2,32,1024]{4,3,2,1,0:T(8,128)(2,1)}, u32[]{:S(2)}, u32[]{:S(2)}) %collective-permute-start.11) | collective-permute-done | bytes 524320 | tf_op jit(solution)/shard_map/ppermute | solution.py:561
  141.5 17.9 %bias.7.bias_ref = f32[16,1024,1024]{2,1,0:T(8,128)} custom-call(bf16[1024,1024]{1,0:T(8,128)(2,1)} %get-tuple-element.216.ix_ref, bf16[1024,1024]{1,0:T(8,128)(2,1)} %get-tuple-element.131.iy_ref, bf16[256,1024]{1,0:T(8,128)(2,1)} %get-tuple-element.148.lhs_ref, f32[16,128,640]{2,1,0:T(8,128)} %get-tuple-element.134.skew_ref, ...), custom_call_target="tpu_custom_call", output_to_operand_aliasing={{}: (4, {})} | custom-call | flops 8499999744 | bytes 18000000 | tf_op jit(solution)/shard_map/bias/pallas_call | solution.py:197
  167.9 2.2 copy-done.39
  170.1 3.7 convolution_convert_fusion.5.v_ref
  173.8 3.7 convolution_convert_fusion.6.k_ref
  177.5 3.7 convolution_convert_fusion.7.q_ref
  181.1 58.7 %attend.1 = (bf16[16,1024,1024]{2,1,0:T(8,128)(2,1)}, bf16[1024,1024]{1,0:T(8,128)(2,1)}) custom-call(bf16[1024,1024]{1,0:T(8,128)(2,1)} %convolution_convert_fusion.7.q_ref, bf16[1024,1024]{1,0:T(8,128)(2,1)} %convolution_convert_fusion.6.k_ref, bf16[1024,1024]{1,0:T(8,128)(2,1)} %convolution_convert_fusion.5.v_ref, f32[16,1024,1024]{2,1,0:T(8,128)} %bias.7.bias_ref), custom_call_target="tpu_custom_call" | custom-call | flops 33999998976 | bytes 100000000 | tf_op jit(solution)/shard_map/attend/pallas_call | solution.py:242
  239.8 4.7 multiply_reduce_fusion.2
  248.3 2.6 copy.132.turned_ref
  250.8 10.9 %unpack.1.down_ref = bf16[2816,1024]{1,0:T(8,128)(2,1)} custom-call(bf16[1024,9728]{1,0:T(8,128)(2,1)} %all-gather.2.cloned.1.call-done.packed_ref.gate_ref.up_ref), custom_call_target="tpu_custom_call" | custom-call | flops 1000000 | bytes 12000000 | tf_op jit(solution)/shard_map/unpack/pallas_call | solution.py:529
  261.7 69.9 %ffn.1 = (bf16[1024,1024]{1,0:T(8,128)(2,1)}, f32[1024,1024]{1,0:T(8,128)}, bf16[1024,2816]{1,0:T(8,128)(2,1)}, bf16[1024,2816]{1,0:T(8,128)(2,1)}, bf16[2816,1024]{1,0:T(8,128)(2,1)}) custom-call(bf16[1024,1024]{1,0:T(8,128)(2,1)} %multiply_convert_fusion.n_ref, bf16[1024,1024]{1,0:T(8,128)(2,1)} %copy.132.turned_ref, bf16[1024,1024]{1,0:T(8,128)(2,1)} %bitcast.343, ...), custom_call_target="tpu_custom_call" | custom-call | flops 53150220288 | bytes 50000000 | tf_op jit(solution)/shard_map/ffn/pallas_call | solution.py:486
  331.7 5.0 constant_dynamic-slice_fusion.10
  343.6 2.6 constant_dynamic-slice_fusion.8
  348.2 4.5 multiply_reduce_fusion
  353.3 4.9 fusion.7
  358.3 2.5 convolution_convert_fusion.3
  360.7 5.5 convolution_convert_fusion.4.grad_ref
  367.8 3.2 fusion
  373.4 2.8 fusion.1
  384.2 30.8 %attend_back.2 = (bf16[16,1024,1024]{2,1,0:T(8,128)(2,1)}, bf16[1024,1024]{1,0:T(8,128)(2,1)}, bf16[1024,1024]{1,0:T(8,128)(2,1)}, bf16[1024,1024]{1,0:T(8,128)(2,1)}) custom-call(bf16[1024,1024]{1,0:T(8,128)(2,1)} %convolution_convert_fusion.7.q_ref, bf16[1024,1024]{1,0:T(8,128)(2,1)} %convolution_convert_fusion.6.k_ref, ...), custom_call_target="tpu_custom_call" | custom-call | flops 16999999488 | bytes 36000000 | tf_op jit(solution)/shard_map/attend_back/pallas_call | solution.py:314
  432.5 31.2 %attend_back.3 = (bf16[16,1024,1024]{2,1,0:T(8,128)(2,1)}, bf16[1024,1024]{1,0:T(8,128)(2,1)}, bf16[1024,1024]{1,0:T(8,128)(2,1)}, bf16[1024,1024]{1,0:T(8,128)(2,1)}) custom-call(bf16[1024,1024]{1,0:T(8,128)(2,1)} %convolution_convert_fusion.7.q_ref, ...), custom_call_target="tpu_custom_call", output_to_operand_aliasing={{0}: (5, {}), {1}: (6, {}), {2}: (7, {}), {3}: (8, {})} | custom-call | flops 16999999488 | bytes 36000000 | tf_op jit(solution)/shard_map/attend_back/pallas_call | solution.py:314
  463.8 4.8 convolution_convert_fusion.1
  468.6 2.4 fusion.52
  479.0 2.4 convolution_convert_fusion
  481.5 2.4 convolution_convert_fusion.2
  483.9 2.3 collective-permute-done.28
  486.3 8.3 %collective-permute-done.26 = bf16[2,32,2816]{2,1,0:T(8,128)(2,1)S(1)} collective-permute-done((bf16[2,32,2816]{2,1,0:T(8,128)(2,1)S(1)}, bf16[2,32,2816]{2,1,0:T(8,128)(2,1)S(1)}, u32[]{:S(2)}, u32[]{:S(2)}) %collective-permute-start.26) | collective-permute-done | bytes 360480 | tf_op jit(solution)/shard_map/ppermute | solution.py:561
  496.9 2.9 collective-permute-start.32
  503.5 2.6 fusion.51
  508.8 3.4 fusion.6
  512.2 2.6 fusion.9
  525.2 22.2 %table_back.3 = (f32[64,256]{1,0:T(8,128)}, f32[16,1024]{1,0:T(8,128)}) custom-call(bf16[16,1024,1024]{2,1,0:T(8,128)(2,1)} %get-tuple-element.201.ds_ref, bf16[1024,1024]{1,0:T(8,128)(2,1)} %get-tuple-element.216.ix_ref, bf16[1024,1024]{1,0:T(8,128)(2,1)} %get-tuple-element.131.iy_ref), custom_call_target="tpu_custom_call" | custom-call | flops 8499999744 | bytes 9000000 | tf_op jit(solution)/shard_map/table_back/pallas_call | solution.py:390
  551.9 2.5 collective-permute-done.35
  562.7 28.9 %table_back.4 = (f32[64,256]{1,0:T(8,128)}, f32[16,1024]{1,0:T(8,128)}) custom-call(bf16[16,1024,1024]{2,1,0:T(8,128)(2,1)} %get-tuple-element.201.ds_ref, bf16[1024,1024]{1,0:T(8,128)(2,1)} %get-tuple-element.216.ix_ref, bf16[1024,1024]{1,0:T(8,128)(2,1)} %get-tuple-element.131.iy_ref), custom_call_target="tpu_custom_call" | custom-call | flops 12750000128 | bytes 13500000 | tf_op jit(solution)/shard_map/table_back/pallas_call | solution.py:390
  598.2 29.2 %table_back.5 = (f32[64,256]{1,0:T(8,128)}, f32[16,1024]{1,0:T(8,128)}) custom-call(bf16[16,1024,1024]{2,1,0:T(8,128)(2,1)} %get-tuple-element.201.ds_ref, bf16[1024,1024]{1,0:T(8,128)(2,1)} %get-tuple-element.216.ix_ref, bf16[1024,1024]{1,0:T(8,128)(2,1)} %get-tuple-element.131.iy_ref), custom_call_target="tpu_custom_call" | custom-call | flops 12750000128 | bytes 13500000 | tf_op jit(solution)/shard_map/table_back/pallas_call | solution.py:390
  633.5 2.5 all-to-all-start.1
  636.8 6.4 all-to-all-done.1
  643.9 2.5 collective-permute-start.48
  647.1 3.9 collective-permute-done.49
  (402 shorter events, 145.1 us)
Async XLA Ops:
  7.2 232.6 %all-gather.2.cloned.1.call-start = ((), (), s32[]{:S(2)}) async-start(), calls=%async_computation.2 | async-start | bytes 20545536 | tf_op jit(solution)/shard_map/all_gather | solution.py:701
  17.5 27.0 %all-to-all-start = ((bf16[32,1,112]{2,1,0:T(2,128)(2,1)}), bf16[32,1,112]{2,1,0:T(2,128)(2,1)S(1)}, u32[]{:S(2)}, u32[]{:S(2)}) async-start(bf16[32,1,112]{2,1,0:T(2,128)(2,1)} %broadcast_in_dim.6), calls=%async_computation | async-start | bytes 32768 | tf_op jit(solution)/shard_map/all_to_all | solution.py:565
  24.8 26.7 %collective-permute-start = (bf16[32,1024]{1,0:T(8,128)(2,1)}, bf16[32,1024]{1,0:T(8,128)(2,1)S(1)}, u32[]{:S(2)}, u32[]{:S(2)}) collective-permute-start(bf16[32,1024]{1,0:T(8,128)(2,1)} %param.20), channel_id=1, source_target_pairs={{0,8},{1,9},{2,10},{3,11},{4,12},{5,13},{6,14},{7,15},{8,0},{9,1},... | collective-permute-start | bytes 196616 | tf_op jit(solution)/shard_map/ppermute | solution.py:561
  26.6 24.9 %collective-permute-start.1 = (bf16[32,1024]{1,0:T(8,128)(2,1)}, bf16[32,1024]{1,0:T(8,128)(2,1)S(1)}, u32[]{:S(2)}, u32[]{:S(2)}) collective-permute-start(bf16[32,1024]{1,0:T(8,128)(2,1)} %param.21), channel_id=1, source_target_pairs={{0,16},{1,17},{2,18},{3,19},{4,20},{5,21},{6,22},{7,23},{8,24},{9,... | collective-permute-start | bytes 196616 | tf_op jit(solution)/shard_map/ppermute | solution.py:561
  29.0 22.5 %collective-permute-start.2 = (bf16[32,1024]{1,0:T(8,128)(2,1)}, bf16[32,1024]{1,0:T(8,128)(2,1)S(1)}, u32[]{:S(2)}, u32[]{:S(2)}) collective-permute-start(bf16[32,1024]{1,0:T(8,128)(2,1)} %param.22), channel_id=1, source_target_pairs={{0,16},{1,17},{2,18},{3,19},{4,20},{5,21},{6,22},{7,23},{8,24},{9,... | collective-permute-start | bytes 196616 | tf_op jit(solution)/shard_map/ppermute | solution.py:561
  51.6 23.3 %collective-permute-start.3 = (bf16[2,32,1024]{2,1,0:T(8,128)(2,1)S(1)}, bf16[2,32,1024]{2,1,0:T(8,128)(2,1)S(1)}, u32[]{:S(2)}, u32[]{:S(2)}) collective-permute-start(bf16[2,32,1024]{2,1,0:T(8,128)(2,1)S(1)} %pad_maximum_fusion.12), channel_id=1, source_target_pairs={{0,16},{1,17},{2,18},{3,19},{4,20},{5,21},{6,22},{7,23},{8,24},{9,... | collective-permute-start | bytes 393224 | tf_op jit(solution)/shard_map/ppermute | solution.py:561
  54.1 20.8 %collective-permute-start.4 = (bf16[2,32,1024]{2,1,0:T(8,128)(2,1)S(1)}, bf16[2,32,1024]{2,1,0:T(8,128)(2,1)S(1)}, u32[]{:S(2)}, u32[]{:S(2)}) collective-permute-start(bf16[2,32,1024]{2,1,0:T(8,128)(2,1)S(1)} %pad_maximum_fusion.13), channel_id=1, source_target_pairs={{0,1},{1,0},{2,3},{3,2},{4,5},{5,4},{6,7},{7,6},{8,9},{9,8},{10,11... | collective-permute-start | bytes 393224 | tf_op jit(solution)/shard_map/ppermute | solution.py:561
  55.7 19.2 %collective-permute-start.5 = (bf16[2,32,1024]{2,1,0:T(8,128)(2,1)S(1)}, bf16[2,32,1024]{2,1,0:T(8,128)(2,1)S(1)}, u32[]{:S(2)}, u32[]{:S(2)}) collective-permute-start(bf16[2,32,1024]{2,1,0:T(8,128)(2,1)S(1)} %pad_maximum_fusion.14), channel_id=1, source_target_pairs={{0,4},{1,5},{2,6},{3,7},{4,0},{5,1},{6,2},{7,3},{8,12},{9,13},{10,... | collective-permute-start | bytes 393224 | tf_op jit(solution)/shard_map/ppermute | solution.py:561
  74.9 19.6 %collective-permute-start.8 = (bf16[2,2,32,1024]{3,2,1,0:T(8,128)(2,1)S(1)}, bf16[2,2,32,1024]{3,2,1,0:T(8,128)(2,1)S(1)}, u32[]{:S(2)}, u32[]{:S(2)}) collective-permute-start(bf16[2,2,32,1024]{3,2,1,0:T(8,128)(2,1)S(1)} %pad_maximum_fusion.11), channel_id=1, source_target_pairs={{0,1},{1,0},{2,3},{3,2},{4,5},{5,4},{6,7},{7,6},{8,9},{9,8},{10,11... | collective-permute-start | bytes 786440 | tf_op jit(solution)/shard_map/ppermute | solution.py:561
  75.6 18.9 %collective-permute-start.7 = (bf16[2,2,32,1024]{3,2,0,1:T(8,128)(2,1)S(1)}, bf16[2,2,32,1024]{3,2,0,1:T(8,128)(2,1)}, u32[]{:S(2)}, u32[]{:S(2)}) collective-permute-start(bf16[2,2,32,1024]{3,2,0,1:T(8,128)(2,1)S(1)} %pad_maximum_fusion.10), channel_id=1, source_target_pairs={{0,8},{1,9},{2,10},{3,11},{4,12},{5,13},{6,14},{7,15},{8,0},{9,1},... | collective-permute-start | bytes 786440 | tf_op jit(solution)/shard_map/ppermute | solution.py:561
  76.2 18.3 %collective-permute-start.6 = (bf16[2,2,32,1024]{3,2,1,0:T(8,128)(2,1)S(1)}, bf16[2,2,32,1024]{3,2,1,0:T(8,128)(2,1)}, u32[]{:S(2)}, u32[]{:S(2)}) collective-permute-start(bf16[2,2,32,1024]{3,2,1,0:T(8,128)(2,1)S(1)} %pad_maximum_fusion.9), channel_id=1, source_target_pairs={{0,4},{1,5},{2,6},{3,7},{4,0},{5,1},{6,2},{7,3},{8,12},{9,13},{10,... | collective-permute-start | bytes 786440 | tf_op jit(solution)/shard_map/ppermute | solution.py:561
  95.4 36.2 %collective-permute-start.11 = (bf16[2,2,2,32,1024]{4,3,2,1,0:T(8,128)(2,1)}, bf16[2,2,2,32,1024]{4,3,2,1,0:T(8,128)(2,1)}, u32[]{:S(2)}, u32[]{:S(2)}) collective-permute-start(bf16[2,2,2,32,1024]{4,3,2,1,0:T(8,128)(2,1)} %pad_maximum_fusion.8), channel_id=1, source_target_pairs={{0,8},{1,9},{2,10},{3,11},{4,12},{5,13},{6,14},{7,15},{8,0},{9,1},... | collective-permute-start | bytes 1572872 | tf_op jit(solution)/shard_map/ppermute | solution.py:561
  98.8 32.8 %collective-permute-start.10 = (bf16[2,2,2,32,1024]{4,3,0,2,1:T(8,128)(2,1)}, bf16[2,2,2,32,1024]{4,3,0,2,1:T(8,128)(2,1)}, u32[]{:S(2)}, u32[]{:S(2)}) collective-permute-start(bf16[2,2,2,32,1024]{4,3,0,2,1:T(8,128)(2,1)} %pad_maximum_fusion.7), channel_id=1, source_target_pairs={{0,4},{1,5},{2,6},{3,7},{4,0},{5,1},{6,2},{7,3},{8,12},{9,13},{10,... | collective-permute-start | bytes 1572872 | tf_op jit(solution)/shard_map/ppermute | solution.py:561
  101.4 30.2 %collective-permute-start.9 = (bf16[2,2,2,32,1024]{4,3,2,1,0:T(8,128)(2,1)S(1)}, bf16[2,2,2,32,1024]{4,3,2,1,0:T(8,128)(2,1)}, u32[]{:S(2)}, u32[]{:S(2)}) collective-permute-start(bf16[2,2,2,32,1024]{4,3,2,1,0:T(8,128)(2,1)S(1)} %pad_maximum_fusion.6), channel_id=1, source_target_pairs={{0,1},{1,0},{2,3},{3,2},{4,5},{5,4},{6,7},{7,6},{8,9},{9,8},{10,11... | collective-permute-start | bytes 1572872 | tf_op jit(solution)/shard_map/ppermute | solution.py:561
  133.8 25.6 %collective-permute-start.14 = (bf16[2,2,2,2,32,1024]{5,4,3,2,1,0:T(8,128)(2,1)}, bf16[2,2,2,2,32,1024]{5,4,3,2,1,0:T(8,128)(2,1)}, u32[]{:S(2)}, u32[]{:S(2)}) collective-permute-start(bf16[2,2,2,2,32,1024]{5,4,3,2,1,0:T(8,128)(2,1)} %pad_maximum_fusion.5), channel_id=1, source_target_pairs={{0,2},{1,3},{2,0},{3,1},{4,6},{5,7},{6,4},{7,5},{8,10},{9,11},{10,... | collective-permute-start | bytes 3145736 | tf_op jit(solution)/shard_map/ppermute | solution.py:561
  136.1 23.3 %collective-permute-start.13 = (bf16[2,2,2,2,32,1024]{5,4,0,3,1,2:T(8,128)(2,1)}, bf16[2,2,2,2,32,1024]{5,4,0,3,1,2:T(8,128)(2,1)}, u32[]{:S(2)}, u32[]{:S(2)}) collective-permute-start(bf16[2,2,2,2,32,1024]{5,4,0,3,1,2:T(8,128)(2,1)} %pad_maximum_fusion.4), channel_id=1, source_target_pairs={{0,2},{1,3},{2,0},{3,1},{4,6},{5,7},{6,4},{7,5},{8,10},{9,11},{10,... | collective-permute-start | bytes 3145736 | tf_op jit(solution)/shard_map/ppermute | solution.py:561
  139.5 19.9 %collective-permute-start.12 = (bf16[2,2,2,2,32,1024]{5,4,3,2,1,0:T(8,128)(2,1)}, bf16[2,2,2,2,32,1024]{5,4,3,2,1,0:T(8,128)(2,1)}, u32[]{:S(2)}, u32[]{:S(2)}) collective-permute-start(bf16[2,2,2,2,32,1024]{5,4,3,2,1,0:T(8,128)(2,1)} %pad_maximum_fusion.3), channel_id=1, source_target_pairs={{0,2},{1,3},{2,0},{3,1},{4,6},{5,7},{6,4},{7,5},{8,10},{9,11},{10,... | collective-permute-start | bytes 3145736 | tf_op jit(solution)/shard_map/ppermute | solution.py:561
  338.4 27.8 %collective-permute-start.15 = (bf16[2,2,2,2,32,2816]{5,4,1,0,2,3:T(8,128)(2,1)}, bf16[2,2,2,2,32,2816]{5,4,1,0,2,3:T(8,128)(2,1)S(1)}, u32[]{:S(2)}, u32[]{:S(2)}) collective-permute-start(bf16[2,2,2,2,32,2816]{5,4,1,0,2,3:T(8,128)(2,1)} %bitcast.318), channel_id=1, source_target_pairs={{0,2},{1,3},{2,0},{3,1},{4,6},{5,7},{6,4},{7,5},{8,10},{9,11},{10,... | collective-permute-start | bytes 8650760 | tf_op jit(solution)/shard_map/ppermute | solution.py:561
  343.1 23.2 %collective-permute-start.16 = (bf16[2,2,2,2,32,2816]{5,4,0,3,1,2:T(8,128)(2,1)}, bf16[2,2,2,2,32,2816]{5,4,0,3,1,2:T(8,128)(2,1)}, u32[]{:S(2)}, u32[]{:S(2)}) collective-permute-start(bf16[2,2,2,2,32,2816]{5,4,0,3,1,2:T(8,128)(2,1)} %bitcast.317), channel_id=1, source_target_pairs={{0,2},{1,3},{2,0},{3,1},{4,6},{5,7},{6,4},{7,5},{8,10},{9,11},{10,... | collective-permute-start | bytes 8650760 | tf_op jit(solution)/shard_map/ppermute | solution.py:561
  348.1 18.1 %collective-permute-start.17 = (bf16[2,2,2,2,88,1024]{5,4,0,2,3,1:T(8,128)(2,1)}, bf16[2,2,2,2,88,1024]{5,4,0,2,3,1:T(8,128)(2,1)}, u32[]{:S(2)}, u32[]{:S(2)}) collective-permute-start(bf16[2,2,2,2,88,1024]{5,4,0,2,3,1:T(8,128)(2,1)} %bitcast.316), channel_id=1, source_target_pairs={{0,2},{1,3},{2,0},{3,1},{4,6},{5,7},{6,4},{7,5},{8,10},{9,11},{10,... | collective-permute-start | bytes 8650760 | tf_op jit(solution)/shard_map/ppermute | solution.py:561
  372.3 42.7 %collective-permute-start.20 = (bf16[2,2,2,88,1024]{4,3,0,1,2:T(8,128)(2,1)}, bf16[2,2,2,88,1024]{4,3,0,1,2:T(8,128)(2,1)}, u32[]{:S(2)}, u32[]{:S(2)}) collective-permute-start(bf16[2,2,2,88,1024]{4,3,0,1,2:T(8,128)(2,1)} %dynamic-slice_bitcast_fusion), channel_id=1, source_target_pairs={{0,8},{1,9},{2,10},{3,11},{4,12},{5,13},{6,14},{7,15},{8,0},{9,1},... | collective-permute-start | bytes 4325384 | tf_op jit(solution)/shard_map/ppermute | solution.py:561
  377.4 37.7 %collective-permute-start.19 = (bf16[2,2,2,32,2816]{4,3,0,2,1:T(8,128)(2,1)}, bf16[2,2,2,32,2816]{4,3,0,2,1:T(8,128)(2,1)}, u32[]{:S(2)}, u32[]{:S(2)}) collective-permute-start(bf16[2,2,2,32,2816]{4,3,0,2,1:T(8,128)(2,1)} %dynamic-slice_bitcast_fusion.1), channel_id=1, source_target_pairs={{0,4},{1,5},{2,6},{3,7},{4,0},{5,1},{6,2},{7,3},{8,12},{9,13},{10,... | collective-permute-start | bytes 4325384 | tf_op jit(solution)/shard_map/ppermute | solution.py:561
  381.7 34.3 %collective-permute-start.18 = (bf16[2,2,2,32,2816]{4,3,1,0,2:T(8,128)(2,1)}, bf16[2,2,2,32,2816]{4,3,1,0,2:T(8,128)(2,1)}, u32[]{:S(2)}, u32[]{:S(2)}) collective-permute-start(bf16[2,2,2,32,2816]{4,3,1,0,2:T(8,128)(2,1)} %dynamic-slice_bitcast_fusion.2), channel_id=1, source_target_pairs={{0,1},{1,0},{2,3},{3,2},{4,5},{5,4},{6,7},{7,6},{8,9},{9,8},{10,11... | collective-permute-start | bytes 4325384 | tf_op jit(solution)/shard_map/ppermute | solution.py:561
  384.1 30.9 %collective-permute-start.21 = (bf16[2,2,2,2,32,1024]{5,4,1,0,2,3:T(8,128)(2,1)}, bf16[2,2,2,2,32,1024]{5,4,1,0,2,3:T(8,128)(2,1)}, u32[]{:S(2)}, u32[]{:S(2)}) collective-permute-start(bf16[2,2,2,2,32,1024]{5,4,1,0,2,3:T(8,128)(2,1)} %bitcast.322), channel_id=1, source_target_pairs={{0,2},{1,3},{2,0},{3,1},{4,6},{5,7},{6,4},{7,5},{8,10},{9,11},{10,... | collective-permute-start | bytes 3145736 | tf_op jit(solution)/shard_map/ppermute | solution.py:561
  418.8 44.9 %collective-permute-start.25 = (bf16[2,2,2,32,1024]{4,3,1,0,2:T(8,128)(2,1)}, bf16[2,2,2,32,1024]{4,3,1,0,2:T(8,128)(2,1)S(1)}, u32[]{:S(2)}, u32[]{:S(2)}) collective-permute-start(bf16[2,2,2,32,1024]{4,3,1,0,2:T(8,128)(2,1)} %dynamic-slice_bitcast_fusion.9), channel_id=1, source_target_pairs={{0,1},{1,0},{2,3},{3,2},{4,5},{5,4},{6,7},{7,6},{8,9},{9,8},{10,11... | collective-permute-start | bytes 1572872 | tf_op jit(solution)/shard_map/ppermute | solution.py:561
  423.9 39.8 %collective-permute-start.24 = (bf16[2,2,88,1024]{3,2,0,1:T(8,128)(2,1)}, bf16[2,2,88,1024]{3,2,0,1:T(8,128)(2,1)S(1)}, u32[]{:S(2)}, u32[]{:S(2)}) collective-permute-start(bf16[2,2,88,1024]{3,2,0,1:T(8,128)(2,1)} %dynamic-slice_bitcast_fusion.3), channel_id=1, source_target_pairs={{0,1},{1,0},{2,3},{3,2},{4,5},{5,4},{6,7},{7,6},{8,9},{9,8},{10,11... | collective-permute-start | bytes 2162696 | tf_op jit(solution)/shard_map/ppermute | solution.py:561
  427.6 36.2 %collective-permute-start.23 = (bf16[2,2,32,2816]{3,2,0,1:T(8,128)(2,1)}, bf16[2,2,32,2816]{3,2,0,1:T(8,128)(2,1)}, u32[]{:S(2)}, u32[]{:S(2)}) collective-permute-start(bf16[2,2,32,2816]{3,2,0,1:T(8,128)(2,1)} %dynamic-slice_bitcast_fusion.4), channel_id=1, source_target_pairs={{0,8},{1,9},{2,10},{3,11},{4,12},{5,13},{6,14},{7,15},{8,0},{9,1},... | collective-permute-start | bytes 2162696 | tf_op jit(solution)/shard_map/ppermute | solution.py:561
  430.9 32.8 %collective-permute-start.22 = (bf16[2,2,32,2816]{3,2,1,0:T(8,128)(2,1)}, bf16[2,2,32,2816]{3,2,1,0:T(8,128)(2,1)}, u32[]{:S(2)}, u32[]{:S(2)}) collective-permute-start(bf16[2,2,32,2816]{3,2,1,0:T(8,128)(2,1)} %dynamic-slice_bitcast_fusion.5), channel_id=1, source_target_pairs={{0,4},{1,5},{2,6},{3,7},{4,0},{5,1},{6,2},{7,3},{8,12},{9,13},{10,... | collective-permute-start | bytes 2162696 | tf_op jit(solution)/shard_map/ppermute | solution.py:561
  471.2 12.7 %collective-permute-start.29 = (bf16[2,2,32,1024]{3,2,1,0:T(8,128)(2,1)S(1)}, bf16[2,2,32,1024]{3,2,1,0:T(8,128)(2,1)S(1)}, u32[]{:S(2)}, u32[]{:S(2)}) collective-permute-start(bf16[2,2,32,1024]{3,2,1,0:T(8,128)(2,1)S(1)} %dynamic-slice_bitcast_fusion.16), channel_id=1, source_target_pairs={{0,4},{1,5},{2,6},{3,7},{4,0},{5,1},{6,2},{7,3},{8,12},{9,13},{10,... | collective-permute-start | bytes 786440 | tf_op jit(solution)/shard_map/ppermute | solution.py:561
  472.7 13.6 %collective-permute-start.28 = (bf16[2,88,1024]{2,1,0:T(8,128)(2,1)S(1)}, bf16[2,88,1024]{2,1,0:T(8,128)(2,1)S(1)}, u32[]{:S(2)}, u32[]{:S(2)}) collective-permute-start(bf16[2,88,1024]{2,1,0:T(8,128)(2,1)S(1)} %dynamic-slice_bitcast_fusion.10), channel_id=1, source_target_pairs={{0,4},{1,5},{2,6},{3,7},{4,0},{5,1},{6,2},{7,3},{8,12},{9,13},{10,... | collective-permute-start | bytes 1081352 | tf_op jit(solution)/shard_map/ppermute | solution.py:561
  477.8 16.8 %collective-permute-start.26 = (bf16[2,32,2816]{2,1,0:T(8,128)(2,1)S(1)}, bf16[2,32,2816]{2,1,0:T(8,128)(2,1)S(1)}, u32[]{:S(2)}, u32[]{:S(2)}) collective-permute-start(bf16[2,32,2816]{2,1,0:T(8,128)(2,1)S(1)} %dynamic-slice_bitcast_fusion.12), channel_id=1, source_target_pairs={{0,16},{1,17},{2,18},{3,19},{4,20},{5,21},{6,22},{7,23},{8,24},{9,... | collective-permute-start | bytes 1081352 | tf_op jit(solution)/shard_map/ppermute | solution.py:561
  496.1 21.3 %collective-permute-start.33 = (bf16[2,32,1024]{2,1,0:T(8,128)(2,1)}, bf16[2,32,1024]{2,1,0:T(8,128)(2,1)}, u32[]{:S(2)}, u32[]{:S(2)}) collective-permute-start(bf16[2,32,1024]{2,1,0:T(8,128)(2,1)} %dynamic-slice_bitcast_fusion.23), channel_id=1, source_target_pairs={{0,16},{1,17},{2,18},{3,19},{4,20},{5,21},{6,22},{7,23},{8,24},{9,... | collective-permute-start | bytes 393224 | tf_op jit(solution)/shard_map/ppermute | solution.py:561
  496.9 20.6 %collective-permute-start.32 = (bf16[88,1024]{1,0:T(8,128)(2,1)}, bf16[88,1024]{1,0:T(8,128)(2,1)}, u32[]{:S(2)}, u32[]{:S(2)}) collective-permute-start(bf16[88,1024]{1,0:T(8,128)(2,1)} %dynamic-slice_bitcast_fusion.17), channel_id=1, source_target_pairs={{0,16},{1,17},{2,18},{3,19},{4,20},{5,21},{6,22},{7,23},{8,24},{9,... | collective-permute-start | bytes 540680 | tf_op jit(solution)/shard_map/ppermute | solution.py:561
  500.7 18.3 %collective-permute-start.31 = (bf16[32,2816]{1,0:T(8,128)(2,1)}, bf16[32,2816]{1,0:T(8,128)(2,1)}, u32[]{:S(2)}, u32[]{:S(2)}) collective-permute-start(bf16[32,2816]{1,0:T(8,128)(2,1)} %dynamic-slice_bitcast_fusion.18), channel_id=1, source_target_pairs={{0,16},{1,17},{2,18},{3,19},{4,20},{5,21},{6,22},{7,23},{8,24},{9,... | collective-permute-start | bytes 540680 | tf_op jit(solution)/shard_map/ppermute | solution.py:561
  501.5 17.4 %collective-permute-start.30 = (bf16[32,2816]{1,0:T(8,128)(2,1)}, bf16[32,2816]{1,0:T(8,128)(2,1)}, u32[]{:S(2)}, u32[]{:S(2)}) collective-permute-start(bf16[32,2816]{1,0:T(8,128)(2,1)} %dynamic-slice_bitcast_fusion.19), channel_id=1, source_target_pairs={{0,8},{1,9},{2,10},{3,11},{4,12},{5,13},{6,14},{7,15},{8,0},{9,1},... | collective-permute-start | bytes 540680 | tf_op jit(solution)/shard_map/ppermute | solution.py:561
  507.5 11.5 %collective-permute-start.34 = (bf16[2,2,2,2,32,1024]{5,4,1,0,2,3:T(8,128)(2,1)}, bf16[2,2,2,2,32,1024]{5,4,1,0,2,3:T(8,128)(2,1)}, u32[]{:S(2)}, u32[]{:S(2)}) collective-permute-start(bf16[2,2,2,2,32,1024]{5,4,1,0,2,3:T(8,128)(2,1)} %bitcast.321), channel_id=1, source_target_pairs={{0,2},{1,3},{2,0},{3,1},{4,6},{5,7},{6,4},{7,5},{8,10},{9,11},{10,... | collective-permute-start | bytes 3145736 | tf_op jit(solution)/shard_map/ppermute | solution.py:561
  517.4 34.5 %collective-permute-start.37 = (bf16[2,2,2,2,32,1024]{5,4,0,3,1,2:T(8,128)(2,1)}, bf16[2,2,2,2,32,1024]{5,4,0,3,1,2:T(8,128)(2,1)}, u32[]{:S(2)}, u32[]{:S(2)}) collective-permute-start(bf16[2,2,2,2,32,1024]{5,4,0,3,1,2:T(8,128)(2,1)} %bitcast.344), channel_id=1, source_target_pairs={{0,2},{1,3},{2,0},{3,1},{4,6},{5,7},{6,4},{7,5},{8,10},{9,11},{10,... | collective-permute-start | bytes 3145736 | tf_op jit(solution)/shard_map/ppermute | solution.py:561
  517.4 34.5 %collective-permute-start.38 = (bf16[2,2,2,2,32,1024]{5,4,0,2,3,1:T(8,128)(2,1)}, bf16[2,2,2,2,32,1024]{5,4,0,2,3,1:T(8,128)(2,1)}, u32[]{:S(2)}, u32[]{:S(2)}) collective-permute-start(bf16[2,2,2,2,32,1024]{5,4,0,2,3,1:T(8,128)(2,1)} %bitcast.345), channel_id=1, source_target_pairs={{0,2},{1,3},{2,0},{3,1},{4,6},{5,7},{6,4},{7,5},{8,10},{9,11},{10,... | collective-permute-start | bytes 3145736 | tf_op jit(solution)/shard_map/ppermute | solution.py:561
  524.2 30.2 %collective-permute-start.36 = (bf16[2,2,2,32,1024]{4,3,1,0,2:T(8,128)(2,1)}, bf16[2,2,2,32,1024]{4,3,1,0,2:T(8,128)(2,1)S(1)}, u32[]{:S(2)}, u32[]{:S(2)}) collective-permute-start(bf16[2,2,2,32,1024]{4,3,1,0,2:T(8,128)(2,1)} %dynamic-slice_bitcast_fusion.8), channel_id=1, source_target_pairs={{0,1},{1,0},{2,3},{3,2},{4,5},{5,4},{6,7},{7,6},{8,9},{9,8},{10,11... | collective-permute-start | bytes 1572872 | tf_op jit(solution)/shard_map/ppermute | solution.py:561
  557.7 33.9 %collective-permute-start.41 = (bf16[2,2,2,32,1024]{4,3,0,1,2:T(8,128)(2,1)}, bf16[2,2,2,32,1024]{4,3,0,1,2:T(8,128)(2,1)S(1)}, u32[]{:S(2)}, u32[]{:S(2)}) collective-permute-start(bf16[2,2,2,32,1024]{4,3,0,1,2:T(8,128)(2,1)} %dynamic-slice_bitcast_fusion.6), channel_id=1, source_target_pairs={{0,8},{1,9},{2,10},{3,11},{4,12},{5,13},{6,14},{7,15},{8,0},{9,1},... | collective-permute-start | bytes 1572872 | tf_op jit(solution)/shard_map/ppermute | solution.py:561
  560.4 31.3 %collective-permute-start.40 = (bf16[2,2,2,32,1024]{4,3,0,2,1:T(8,128)(2,1)}, bf16[2,2,2,32,1024]{4,3,0,2,1:T(8,128)(2,1)S(1)}, u32[]{:S(2)}, u32[]{:S(2)}) collective-permute-start(bf16[2,2,2,32,1024]{4,3,0,2,1:T(8,128)(2,1)} %dynamic-slice_bitcast_fusion.7), channel_id=1, source_target_pairs={{0,4},{1,5},{2,6},{3,7},{4,0},{5,1},{6,2},{7,3},{8,12},{9,13},{10,... | collective-permute-start | bytes 1572872 | tf_op jit(solution)/shard_map/ppermute | solution.py:561
  561.8 29.8 %collective-permute-start.39 = (bf16[2,2,32,1024]{3,2,1,0:T(8,128)(2,1)S(1)}, bf16[2,2,32,1024]{3,2,1,0:T(8,128)(2,1)}, u32[]{:S(2)}, u32[]{:S(2)}) collective-permute-start(bf16[2,2,32,1024]{3,2,1,0:T(8,128)(2,1)S(1)} %dynamic-slice_bitcast_fusion.15), channel_id=1, source_target_pairs={{0,4},{1,5},{2,6},{3,7},{4,0},{5,1},{6,2},{7,3},{8,12},{9,13},{10,... | collective-permute-start | bytes 786440 | tf_op jit(solution)/shard_map/ppermute | solution.py:561
  592.7 34.8 %collective-permute-start.44 = (bf16[2,2,32,1024]{3,2,0,1:T(8,128)(2,1)S(1)}, bf16[2,2,32,1024]{3,2,0,1:T(8,128)(2,1)S(1)}, u32[]{:S(2)}, u32[]{:S(2)}) collective-permute-start(bf16[2,2,32,1024]{3,2,0,1:T(8,128)(2,1)S(1)} %dynamic-slice_bitcast_fusion.13), channel_id=1, source_target_pairs={{0,1},{1,0},{2,3},{3,2},{4,5},{5,4},{6,7},{7,6},{8,9},{9,8},{10,11... | collective-permute-start | bytes 786440 | tf_op jit(solution)/shard_map/ppermute | solution.py:561
  594.0 33.5 %collective-permute-start.43 = (bf16[2,2,32,1024]{3,2,0,1:T(8,128)(2,1)S(1)}, bf16[2,2,32,1024]{3,2,0,1:T(8,128)(2,1)S(1)}, u32[]{:S(2)}, u32[]{:S(2)}) collective-permute-start(bf16[2,2,32,1024]{3,2,0,1:T(8,128)(2,1)S(1)} %dynamic-slice_bitcast_fusion.14), channel_id=1, source_target_pairs={{0,8},{1,9},{2,10},{3,11},{4,12},{5,13},{6,14},{7,15},{8,0},{9,1},... | collective-permute-start | bytes 786440 | tf_op jit(solution)/shard_map/ppermute | solution.py:561
  597.1 30.4 %collective-permute-start.42 = (bf16[2,32,1024]{2,1,0:T(8,128)(2,1)S(1)}, bf16[2,32,1024]{2,1,0:T(8,128)(2,1)S(1)}, u32[]{:S(2)}, u32[]{:S(2)}) collective-permute-start(bf16[2,32,1024]{2,1,0:T(8,128)(2,1)S(1)} %dynamic-slice_bitcast_fusion.22), channel_id=1, source_target_pairs={{0,16},{1,17},{2,18},{3,19},{4,20},{5,21},{6,22},{7,23},{8,24},{9,... | collective-permute-start | bytes 393224 | tf_op jit(solution)/shard_map/ppermute | solution.py:561
  627.6 15.6 %collective-permute-start.47 = (bf16[2,32,1024]{2,1,0:T(8,128)(2,1)S(1)}, bf16[2,32,1024]{2,1,0:T(8,128)(2,1)S(1)}, u32[]{:S(2)}, u32[]{:S(2)}) collective-permute-start(bf16[2,32,1024]{2,1,0:T(8,128)(2,1)S(1)} %dynamic-slice_bitcast_fusion.20), channel_id=1, source_target_pairs={{0,4},{1,5},{2,6},{3,7},{4,0},{5,1},{6,2},{7,3},{8,12},{9,13},{10,... | collective-permute-start | bytes 393224 | tf_op jit(solution)/shard_map/ppermute | solution.py:561
  629.1 14.1 %collective-permute-start.46 = (bf16[2,32,1024]{2,1,0:T(8,128)(2,1)S(1)}, bf16[2,32,1024]{2,1,0:T(8,128)(2,1)S(1)}, u32[]{:S(2)}, u32[]{:S(2)}) collective-permute-start(bf16[2,32,1024]{2,1,0:T(8,128)(2,1)S(1)} %dynamic-slice_bitcast_fusion.21), channel_id=1, source_target_pairs={{0,1},{1,0},{2,3},{3,2},{4,5},{5,4},{6,7},{7,6},{8,9},{9,8},{10,11... | collective-permute-start | bytes 393224 | tf_op jit(solution)/shard_map/ppermute | solution.py:561
  630.1 13.2 %collective-permute-start.45 = (bf16[32,1024]{1,0:T(8,128)(2,1)S(1)}, bf16[32,1024]{1,0:T(8,128)(2,1)S(1)}, u32[]{:S(2)}, u32[]{:S(2)}) collective-permute-start(bf16[32,1024]{1,0:T(8,128)(2,1)S(1)} %dynamic-slice_bitcast_fusion.26), channel_id=1, source_target_pairs={{0,8},{1,9},{2,10},{3,11},{4,12},{5,13},{6,14},{7,15},{8,0},{9,1},... | collective-permute-start | bytes 196616 | tf_op jit(solution)/shard_map/ppermute | solution.py:561
  (86 other events, 655.8 us)
Sparse Core Ops, SparseCore 0:
  13.5 157.8 all-gather.1

commit v2 on v1

--- a/solution.py
+++ b/solution.py
@@ -21,11 +21,12 @@
 gelu_scale = 0.7978845608028654
 
 VMEM_LIMIT = 60 * 2**20
-ROW_TILE = 256
+ROW_TILE = 1024
 STRIP = 16
 BIAS_TILE = 128
 DEAD_BUCKET = 16
 CORE_BIT = 1
+TABLE_JOINT = 4
 
 
 def params_for(flops, moved):
@@ -34,6 +35,22 @@
         cost_estimate=pl.CostEstimate(
             flops=int(flops), bytes_accessed=int(moved), transcendentals=0
         ),
+    )
+
+
+def plain_product(left, right):
+    return jnp.dot(left, right, preferred_element_type=jnp.float32)
+
+
+def left_transposed(left, right):
+    return lax.dot_general(
+        left, right, (((0,), (0,)), ((), ())), preferred_element_type=jnp.float32
+    )
+
+
+def right_transposed(left, right):
+    return lax.dot_general(
+        left, right, (((1,), (1,)), ((), ())), preferred_element_type=jnp.float32
     )
 
 
@@ -79,12 +96,13 @@
     return table[offset + slots - 1][None, :] == np.arange(BUCKETS)[:, None]
 
 
-def write_marks(marks_ref, x_tile, y_tile):
+def write_marks(marks_ref, x_tile, y_tile, begin=0):
     one = jnp.ones(x_tile.shape, jnp.bfloat16)
     zero = jnp.zeros(x_tile.shape, jnp.bfloat16)
+    cols = slice(begin, begin + x_tile.shape[1])
     for b in range(BUCKETS):
-        marks_ref[b * 16 : b * 16 + 16, :] = jnp.where(x_tile == b, one, zero)
-        marks_ref[512 + b * 16 : 512 + b * 16 + 16, :] = jnp.where(y_tile == b, one, zero)
+        marks_ref[b * 16 : b * 16 + 16, cols] = jnp.where(x_tile == b, one, zero)
+        marks_ref[512 + b * 16 : 512 + b * 16 + 16, cols] = jnp.where(y_tile == b, one, zero)
 
 
 def index_kernel(len_ref, box_ref, turned_ref, ix_ref, iy_ref):
@@ -122,7 +140,8 @@
     )
     for h in range(HEADS):
         wide = jnp.broadcast_to(rel_row[h : h + 1, :], (BIAS_TILE, slots))
-        skew_ref[h] = pltpu.roll(wide, 0, 1, stride=1, stride_axis=0)[:, :640]
+        skew = pltpu.roll(wide, 0, 1, stride=1, stride_axis=0)[:, :640]
+        skew_ref[h] = skew.astype(jnp.bfloat16)
     tall, long = HEADS * 16, 2 * BUCKETS * 16
     layout = tables[:, BUCKETS:]
     dead = lax.broadcasted_iota(jnp.int32, layout.shape, 1) == DEAD_BUCKET
@@ -149,33 +168,51 @@
         prepare_kernel,
         out_shape=[
             jax.ShapeDtypeStruct((HEADS * 16, 2 * BUCKETS * 16), jnp.bfloat16),
-            jax.ShapeDtypeStruct((HEADS, BIAS_TILE, 640), jnp.float32),
+            jax.ShapeDtypeStruct((HEADS, BIAS_TILE, 640), jnp.bfloat16),
         ],
         name="prepare",
         **params_for(1e9, 6e6),
     )(tables, jnp.asarray(rel_marks(slots, 256)).astype(jnp.bfloat16))
 
 
+def two_at_a_time(ix_ref, iy_ref, first_ref, second_ref, use, joint=1):
+    rows, slots = ix_ref.shape
+    step = 16 * joint
+
+    def write(ref, r0):
+        for at in range(joint):
+            here = pl.multiple_of(jnp.minimum(r0 + 16 * at, rows - 16), 16)
+            write_marks(ref, ix_ref[pl.ds(here, 16), :], iy_ref[pl.ds(here, 16), :], at * slots)
+
+    write(first_ref, 0)
+
+    def body(t, carry):
+        r0 = pl.multiple_of(t * 2 * step, 2 * step)
+        write(second_ref, r0 + step)
+        use(r0, first_ref)
+        write(first_ref, r0 + 2 * step)
+        use(pl.multiple_of(r0 + step, step), second_ref)
+        return carry
+
+    lax.fori_loop(0, rows // (2 * step), body, 0)
+
+
 def bias_kernel(first, ix_ref, iy_ref, lhs_ref, skew_ref, *rest):
-    bias_ref, marks_ref = rest[-2:]
+    bias_ref, first_ref, second_ref = rest[-3:]
     block = pl.program_id(0) + first
     slots = ix_ref.shape[1]
 
-    def body(t, carry):
-        r0 = pl.multiple_of(t * 16, 16)
-        write_marks(marks_ref, ix_ref[pl.ds(r0, 16), :], iy_ref[pl.ds(r0, 16), :])
+    def use(r0, marks_ref):
         out = jnp.dot(lhs_ref[...], marks_ref[...], preferred_element_type=jnp.float32)
         for c in range(slots // 128):
             shift = pl.multiple_of((jnp.clip(c - block, -2, 2) + 2) * 128, 128)
             cols = slice(c * 128, c * 128 + 128)
             for h in range(HEADS):
-                bias_ref[h, pl.ds(r0, 16), cols] = (
-                    out[h * 16 : h * 16 + 16, cols]
-                    + skew_ref[h, pl.ds(r0, 16), pl.ds(shift, 128)]
-                )
-        return carry
-
-    lax.fori_loop(0, BIAS_TILE // 16, body, 0)
+                bias_ref[h, pl.ds(r0, 16), cols] = out[
+                    h * 16 : h * 16 + 16, cols
+                ] + skew_ref[h, pl.ds(r0, 16), pl.ds(shift, 128)].astype(jnp.float32)
+
+    two_at_a_time(ix_ref, iy_ref, first_ref, second_ref, use)
 
 
 def bias_call(ix, iy, lhs, skew, begin, end, held=None):
@@ -200,7 +237,7 @@
         in_specs=in_specs,
         out_specs=pl.BlockSpec((HEADS, BIAS_TILE, slots), lambda i: (0, i + begin, 0)),
         out_shape=jax.ShapeDtypeStruct((HEADS, slots, slots), jnp.float32),
-        scratch_shapes=[pltpu.VMEM((2 * BUCKETS * 16, slots), jnp.bfloat16)],
+        scratch_shapes=[pltpu.VMEM((2 * BUCKETS * 16, slots), jnp.bfloat16)] * 2,
         input_output_aliases=aliases,
         name="bias",
         **params_for(34e9 * share, 72e6 * share),
@@ -325,68 +362,76 @@
     )(*args)
 
 
+def rel_near_marks(slots):
+    row = np.arange(BIAS_TILE)[:, None]
+    offset = np.arange(640)[None, :] - 256 - row
+    bucket = bucket_table(slots - 1, BUCKETS, token_reach)[offset + slots - 1]
+    marks = bucket[None, :, :] == np.arange(BUCKETS)[:, None, None]
+    marks = marks.reshape(BUCKETS, BIAS_TILE // 16, 16, 640).transpose(1, 0, 2, 3)
+    return marks.reshape(BIAS_TILE // 16, BUCKETS * 16, 640)
+
+
 def table_kernel(
-    first, ds_ref, ix_ref, iy_ref, layout_ref, rel_ref, layout_sum, rel_sum, marks_ref
+    first, ds_ref, ix_ref, iy_ref, near_ref, out_ref, total, rel_total, first_ref, second_ref
 ):
     step = pl.program_id(0)
     block = step + first
     slots = ix_ref.shape[1]
+    blocks = slots // BIAS_TILE
+    heads = ds_ref.shape[0]
 
     @pl.when(step == 0)
     def _():
-        layout_sum[...] = jnp.zeros_like(layout_sum)
-        rel_sum[...] = jnp.zeros_like(rel_sum)
-
-    def body(t, carry):
-        r0 = pl.multiple_of(t * 16, 16)
-        write_marks(marks_ref, ix_ref[pl.ds(r0, 16), :], iy_ref[pl.ds(r0, 16), :])
-        ds = ds_ref[:, pl.ds(r0, 16), :].reshape(HEADS * 16, slots)
-        layout_sum[...] += lax.dot_general(
-            marks_ref[...], ds, (((1,), (1,)), ((), ())), preferred_element_type=jnp.float32
+        total[...] = jnp.zeros_like(total)
+        rel_total[...] = jnp.zeros_like(rel_total)
+
+    begin = jnp.clip(block - 1, 0, blocks - 3)
+    lanes = pl.ds(pl.multiple_of(begin * BIAS_TILE, BIAS_TILE), 3 * BIAS_TILE)
+    source = pl.ds(
+        pl.multiple_of((begin - block + 2) * BIAS_TILE, BIAS_TILE), 3 * BIAS_TILE
+    )
+    place = lax.broadcasted_iota(jnp.int32, (16, TABLE_JOINT * slots), 1) % slots
+    low = (place < begin * BIAS_TILE).astype(jnp.float32).astype(jnp.bfloat16)
+    high = (place >= (begin + 3) * BIAS_TILE).astype(jnp.float32).astype(jnp.bfloat16)
+    for ref in (first_ref, second_ref):
+        ref[2 * BUCKETS * 16 : 2 * BUCKETS * 16 + 16, :] = low
+        ref[2 * BUCKETS * 16 + 16 :, :] = high
+
+    def use(r0, marks_ref):
+        ds, close, near = [], [], []
+        for at in range(TABLE_JOINT):
+            here = pl.ds(pl.multiple_of(r0 + 16 * at, 16), 16)
+            ds.append(ds_ref[:, here, :].reshape(heads * 16, slots))
+            close.append(ds_ref[:, here, lanes].reshape(heads * 16, 3 * BIAS_TILE))
+            near.append(near_ref[r0 // 16 + at, :, source])
+        total[...] += right_transposed(marks_ref[...], jnp.concatenate(ds, axis=1))
+        rel_total[...] += right_transposed(
+            jnp.concatenate(near, axis=1), jnp.concatenate(close, axis=1)
         )
-        for c in range(slots // 128):
-            shift = pl.multiple_of((jnp.clip(c - block, -2, 2) + 2) * 128, 128)
-            cols = slice(c * 128, c * 128 + 128)
-            for h in range(HEADS):
-                rel_sum[h, pl.ds(r0, 16), pl.ds(shift, 128)] += ds_ref[
-                    h, pl.ds(r0, 16), cols
-                ].astype(jnp.float32)
-        return carry
-
-    lax.fori_loop(0, BIAS_TILE // 16, body, 0)
+
+    two_at_a_time(ix_ref, iy_ref, first_ref, second_ref, use, TABLE_JOINT)
 
     @pl.when(step == pl.num_programs(0) - 1)
     def _():
-        shape = layout_sum.shape
-        same = (
-            lax.broadcasted_iota(jnp.int32, shape, 0) % 16
-            == lax.broadcasted_iota(jnp.int32, shape, 1) % 16
-        )
-        kept = jnp.where(same, layout_sum[...], 0.0)
-        layout_ref[...] = kept.reshape(2 * BUCKETS, 16, HEADS * 16).sum(axis=1)
-        tall = (BIAS_TILE, BIAS_TILE)
-        flip = (
-            lax.broadcasted_iota(jnp.int32, tall, 0) + lax.broadcasted_iota(jnp.int32, tall, 1)
-            == BIAS_TILE - 1
-        ).astype(jnp.float32)
-        for h in range(HEADS):
-            upside = jnp.dot(
-                flip,
-                rel_sum[h],
-                precision=lax.Precision.HIGHEST,
-                preferred_element_type=jnp.float32,
+        at = 0
+        for ref in (total, rel_total):
+            shape = ref.shape
+            same = (
+                lax.broadcasted_iota(jnp.int32, shape, 0) % 16
+                == lax.broadcasted_iota(jnp.int32, shape, 1) % 16
             )
-            padded = jnp.concatenate(
-                [upside, jnp.zeros((BIAS_TILE, slots - 640), jnp.float32)], axis=1
-            )
-            back = pltpu.roll(padded, 0, 1, stride=1, stride_axis=0)
-            rel_ref[h : h + 1, :] = jnp.sum(back, axis=0, keepdims=True)
+            kept = jnp.where(same, ref[...], 0.0).reshape(shape[0] // 16, 16, shape[1])
+            out_ref[at : at + shape[0] // 16, :] = kept.sum(axis=1)
+            at += shape[0] // 16
+        out_ref[at:, :] = jnp.zeros((out_ref.shape[0] - at, out_ref.shape[1]), jnp.float32)
 
 
 def table_call(ds, ix, iy, begin, end):
     slots = ix.shape[0]
     tile = pl.BlockSpec((BIAS_TILE, slots), lambda i: (i + begin, 0))
     share = (end - begin) * BIAS_TILE / slots
+    near = jnp.asarray(rel_near_marks(slots)).astype(jnp.bfloat16)
+    marked = (2 * BUCKETS + 2) * 16
     return pl.pallas_call(
         functools.partial(table_kernel, begin),
         grid=(end - begin,),
@@ -394,57 +439,59 @@
             pl.BlockSpec((HEADS, BIAS_TILE, slots), lambda i: (0, i + begin, 0)),
             tile,
             tile,
+            pl.BlockSpec(near.shape, lambda i: (0, 0, 0)),
         ],
-        out_specs=[
-            pl.BlockSpec((2 * BUCKETS, HEADS * 16), lambda i: (0, 0)),
-            pl.BlockSpec((HEADS, slots), lambda i: (0, 0)),
-        ],
-        out_shape=[
-            jax.ShapeDtypeStruct((2 * BUCKETS, HEADS * 16), jnp.float32),
-            jax.ShapeDtypeStruct((HEADS, slots), jnp.float32),
-        ],
+        out_specs=pl.BlockSpec((104, HEADS * 16), lambda i: (0, 0)),
+        out_shape=jax.ShapeDtypeStruct((104, HEADS * 16), jnp.float32),
         scratch_shapes=[
-            pltpu.VMEM((2 * BUCKETS * 16, HEADS * 16), jnp.float32),
-            pltpu.VMEM((HEADS, BIAS_TILE, 640), jnp.float32),
-            pltpu.VMEM((2 * BUCKETS * 16, slots), jnp.bfloat16),
+            pltpu.VMEM((marked, HEADS * 16), jnp.float32),
+            pltpu.VMEM((BUCKETS * 16, HEADS * 16), jnp.float32),
+            pltpu.VMEM((marked, TABLE_JOINT * slots), jnp.bfloat16),
+            pltpu.VMEM((marked, TABLE_JOINT * slots), jnp.bfloat16),
         ],
         name="table_back",
-        **params_for(34e9 * share, 36e6 * share),
-    )(ds, ix, iy)
-
-
-def table_finish(parts, slots):
-    layout = sum(part[0] for part in parts)
-    rel = sum(part[1] for part in parts)
-    layout = layout.reshape(2 * BUCKETS, HEADS, 16).sum(axis=2).T
-    rel = lax.dot_general(
-        rel,
-        jnp.asarray(rel_marks(slots, 383)).astype(jnp.float32),
-        (((1,), (1,)), ((), ())),
-        precision=lax.Precision.HIGHEST,
-        preferred_element_type=jnp.float32,
-    )
-    return rel, layout[:, :BUCKETS], layout[:, BUCKETS:]
+        **params_for(40e9 * share, 40e6 * share),
+    )(ds, ix, iy, near)
+
+
+def table_finish(parts):
+    sums = sum(parts).reshape(104, HEADS, 16).sum(axis=2).T
+    near = sums[:, 66:98]
+    left, right = BUCKETS // 2 - 1, BUCKETS - 1
+    column = jnp.arange(BUCKETS)[None, :]
+    rel = near + jnp.where(column == left, sums[:, 64:65], 0.0)
+    rel = rel + jnp.where(column == right, sums[:, 65:66], 0.0)
+    return rel, sums[:, :BUCKETS], sums[:, BUCKETS : 2 * BUCKETS]
 
 
 def ffn_kernel(
-    n_ref, turned_ref, seed_ref, hidden_ref, gate_ref, up_ref, down_ref,
-    out_ref, dn_ref, dgate_ref, dup_ref, ddown_ref, out_sum, dn_sum,
+    unit, core_ref, n_ref, seed_ref, hidden_ref, gate_ref, up_ref, down_ref,
+    out_ref, dn_ref, gate_away_ref, gate_stay_ref, up_away_ref, up_stay_ref, ddown_ref,
+    out_sum, turned_ref,
 ):
     step = pl.program_id(0)
+    width = n_ref.shape[1]
+    half = width // 2
 
     @pl.when(step == 0)
     def _():
         out_sum[...] = hidden_ref[...]
-        dn_sum[...] = jnp.zeros_like(dn_sum)
+        dn_ref[...] = jnp.zeros_like(dn_ref)
+        core = core_ref[0]
+        for lanes in range(0, width, 128):
+            turned = n_ref[:, lanes : lanes + 128].T
+            for part in range(128 // unit):
+                group = lanes // unit + part
+                first = jnp.where(core == group % 2, half, 0) + group // 2 * unit
+                turned_ref[pl.ds(pl.multiple_of(first, 16), unit), :] = turned[
+                    part * unit : (part + 1) * unit
+                ]
 
     seed = seed_ref[...]
     w_gate, w_up, w_down = gate_ref[...], up_ref[...], down_ref[...]
-    gate = jnp.dot(n_ref[...], w_gate, preferred_element_type=jnp.float32)
-    upper = jnp.dot(n_ref[...], w_up, preferred_element_type=jnp.float32)
-    grad_act = lax.dot_general(
-        seed, w_down, (((1,), (1,)), ((), ())), preferred_element_type=jnp.float32
-    )
+    gate = plain_product(n_ref[...], w_gate)
+    upper = plain_product(n_ref[...], w_up)
+    grad_act = right_transposed(seed, w_down)
     square = gate * gate
     tanh = jnp.tanh(gelu_scale * (gate + 0.044715 * gate * square))
     cdf = 0.5 * (1.0 + tanh)
@@ -453,92 +500,55 @@
     activated = (gelu * upper).astype(jnp.bfloat16)
     grad_gate = (grad_act * upper * slope).astype(jnp.bfloat16)
     grad_upper = (grad_act * gelu).astype(jnp.bfloat16)
-    out_sum[...] += jnp.dot(activated, w_down, preferred_element_type=jnp.float32)
-    dn_sum[...] += lax.dot_general(
-        grad_gate, w_gate, (((1,), (1,)), ((), ())), preferred_element_type=jnp.float32
-    ) + lax.dot_general(
-        grad_upper, w_up, (((1,), (1,)), ((), ())), preferred_element_type=jnp.float32
-    )
-    dgate_ref[...] = jnp.dot(
-        turned_ref[...], grad_gate, preferred_element_type=jnp.float32
-    ).astype(jnp.bfloat16)
-    dup_ref[...] = jnp.dot(
-        turned_ref[...], grad_upper, preferred_element_type=jnp.float32
-    ).astype(jnp.bfloat16)
-    ddown_ref[...] = lax.dot_general(
-        activated, seed, (((0,), (0,)), ((), ())), preferred_element_type=jnp.float32
-    ).astype(jnp.bfloat16)
+    out_sum[...] += plain_product(activated, w_down)
+    dn_ref[...] += right_transposed(grad_gate, w_gate) + right_transposed(grad_upper, w_up)
+    d_gate = plain_product(turned_ref[...], grad_gate).astype(jnp.bfloat16)
+    gate_away_ref[...] = d_gate[:half]
+    gate_stay_ref[...] = d_gate[half:]
+    d_up = plain_product(turned_ref[...], grad_upper).astype(jnp.bfloat16)
+    up_away_ref[...] = d_up[:half]
+    up_stay_ref[...] = d_up[half:]
+    ddown_ref[...] = left_transposed(activated, seed).astype(jnp.bfloat16)
 
     @pl.when(step == pl.num_programs(0) - 1)
     def _():
         out_ref[...] = out_sum[...].astype(jnp.bfloat16)
-        dn_ref[...] = dn_sum[...]
-
-
-def ffn_call(normed, turned, seed, hidden, packed, first, w_down):
+
+
+def ffn_call(core, unit, normed, seed, hidden, packed, w_down):
     slots, width = normed.shape
     ff = w_down.shape[0]
     tile = 256
     count = ff // tile
     full = pl.BlockSpec((slots, width), lambda f: (0, 0))
-    turned_full = pl.BlockSpec((width, slots), lambda f: (0, 0))
-    column = pl.BlockSpec((width, tile), lambda f: (0, f))
+    column = pl.BlockSpec((width // 2, tile), lambda f: (0, f))
+    row = pl.BlockSpec((tile, width), lambda f: (f, 0))
     return pl.pallas_call(
-        ffn_kernel,
+        functools.partial(ffn_kernel, unit),
         grid=(count,),
         in_specs=[
-            full,
-            turned_full,
+            pl.BlockSpec(memory_space=pltpu.SMEM),
             full,
             full,
-            pl.BlockSpec((width, tile), lambda f: (0, f + first)),
-            pl.BlockSpec((width, tile), lambda f: (0, f + first + count)),
-            pl.BlockSpec((tile, width), lambda f: (f, 0)),
+            full,
+            pl.BlockSpec((width, tile), lambda f: (0, f)),
+            pl.BlockSpec((width, tile), lambda f: (0, f + count)),
+            row,
         ],
-        out_specs=[full, full, column, column, pl.BlockSpec((tile, width), lambda f: (f, 0))],
+        out_specs=[full, full, column, column, column, column, row],
         out_shape=[
             jax.ShapeDtypeStruct((slots, width), jnp.bfloat16),
             jax.ShapeDtypeStruct((slots, width), jnp.float32),
-            jax.ShapeDtypeStruct((width, ff), jnp.bfloat16),
-            jax.ShapeDtypeStruct((width, ff), jnp.bfloat16),
-            jax.ShapeDtypeStruct((ff, width), jnp.bfloat16),
+        ]
+        + [jax.ShapeDtypeStruct((width // 2, ff), jnp.bfloat16)] * 4
+        + [jax.ShapeDtypeStruct((ff, width), jnp.bfloat16)],
+        scratch_shapes=[
+            pltpu.VMEM((slots, width), jnp.float32),
+            pltpu.VMEM((width, slots), jnp.bfloat16),
         ],
-        scratch_shapes=[pltpu.VMEM((slots, width), jnp.float32)] * 2,
         name="ffn",
         **params_for(18 * slots * width * ff, 50e6),
-    )(normed, turned, seed, hidden, packed, packed, w_down)
-
-
-def unpack_kernel(down_rows, part_rows, packed_ref, out_ref):
-    width = out_ref.shape[1]
-    for at in range(out_ref.shape[0] // down_rows):
-        for group in range(-(-down_rows // part_rows)):
-            count = min(part_rows, down_rows - group * part_rows)
-            here = at * down_rows + group * part_rows
-            out_ref[here : here + count, :] = packed_ref[
-                at * part_rows : at * part_rows + count, group * width : (group + 1) * width
-            ]
-
-
-def unpack_call(packed, first, down_rows, part_rows, width):
-    count = packed.shape[0] // part_rows
-    groups = -(-down_rows // part_rows)
-    joint = 1
-    while (joint * down_rows) % 16 or (joint * part_rows) % 16:
-        joint *= 2
-    return pl.pallas_call(
-        functools.partial(unpack_kernel, down_rows, part_rows),
-        grid=(count // joint,),
-        in_specs=[
-            pl.BlockSpec(
-                (joint * part_rows, groups * width), lambda d: (d, first // (groups * width))
-            )
-        ],
-        out_specs=pl.BlockSpec((joint * down_rows, width), lambda d: (d, 0)),
-        out_shape=jax.ShapeDtypeStruct((count * down_rows, width), jnp.bfloat16),
-        name="unpack",
-        **params_for(1e6, 12e6),
-    )(packed)
+    )(core, normed, seed, hidden, packed, packed, w_down)
 
 
 class Exchange:
@@ -553,8 +563,11 @@
             [CORE_BIT, three, one, two] + tail,
         )
 
+    def me(self):
+        return lax.axis_index(AXES)
+
     def mine(self, bit):
-        return (lax.axis_index(AXES) >> bit) & 1
+        return (self.me() >> bit) & 1
 
     def swap(self, value, bit):
         pairs = [(d, d ^ (1 << bit)) for d in range(self.count)]
@@ -571,9 +584,9 @@
 class Gather:
     def __init__(self, exchange, shard, order):
         self.exchange = exchange
-        self.value = shard
+        self.value = shard[None]
         self.steps = list(reversed(exchange.orders[order]))
-        self.held = []
+        self.offsets = [0]
         self.flight = None
 
     def done(self):
@@ -585,21 +598,81 @@
     def land(self):
         bit = self.steps.pop(0)
         other, self.flight = self.flight, None
-        spot = sum(b > bit for b in self.held)
-        high = self.exchange.mine(bit) == 1
-        self.value = jnp.stack(
-            [jnp.where(high, other, self.value), jnp.where(high, self.value, other)], axis=spot
-        )
-        self.held.append(bit)
+        self.offsets += [offset | 1 << bit for offset in self.offsets]
+        if self.steps:
+            self.value = jnp.concatenate([self.value, other], axis=0)
+        else:
+            self.other = other
+
+
+def project_kernel(offsets, me_ref, x_ref, *refs):
+    count = len(offsets)
+    halves, outs, scratch = refs[: 2 * count], refs[2 * count : 4 * count], refs[4 * count]
+    me = me_ref[0]
+    for at in range(count):
+        value_ref, other_ref = halves[2 * at : 2 * at + 2]
+        out_ref, full_ref = outs[2 * at : 2 * at + 2]
+        places, rows, _ = value_ref.shape
+        for place, offset in enumerate(offsets[at]):
+            part = value_ref[place] if place < places else other_ref[place - places]
+            begin = pl.multiple_of((me ^ offset) * rows, rows)
+            scratch[at, pl.ds(begin, rows), :] = part
+        full_ref[...] = scratch[at]
+        out_ref[...] = plain_product(x_ref[...], scratch[at]).astype(jnp.bfloat16)
+
+
+def project_call(exchange, normed, tasks):
+    places, rows, inner = tasks[0].value.shape
+    slots, width = normed.shape
+    if rows % 16:
+        fulls, outs = [], []
+        for task in tasks:
+            held = jnp.concatenate([task.value, task.other], axis=0)
+            place_of = np.argsort(np.asarray(task.offsets))
+            spots = jnp.asarray(place_of)[exchange.me() ^ jnp.arange(exchange.count)]
+            fulls.append(jnp.take(held, spots, axis=0).reshape(width, inner))
+            outs.append(plain_product(normed, fulls[-1]).astype(jnp.bfloat16))
+        return outs, fulls
+    tile = 256
+    part = pl.BlockSpec((places, rows, tile), lambda n: (0, 0, n))
+    column = pl.BlockSpec((slots, tile), lambda n: (0, n))
+    full = pl.BlockSpec((width, tile), lambda n: (0, n))
+    results = pl.pallas_call(
+        functools.partial(project_kernel, tuple(tuple(task.offsets) for task in tasks)),
+        grid=(inner // tile,),
+        in_specs=[
+            pl.BlockSpec(memory_space=pltpu.SMEM),
+            pl.BlockSpec((slots, width), lambda n: (0, 0)),
+        ]
+        + [part] * (2 * len(tasks)),
+        out_specs=[column, full] * len(tasks),
+        out_shape=[
+            jax.ShapeDtypeStruct((slots, inner), jnp.bfloat16),
+            jax.ShapeDtypeStruct((width, inner), jnp.bfloat16),
+        ]
+        * len(tasks),
+        scratch_shapes=[pltpu.VMEM((len(tasks), width, tile), jnp.bfloat16)],
+        name="project",
+        **params_for(2 * len(tasks) * slots * width * inner, 20e6),
+    )(
+        exchange.me().astype(jnp.int32).reshape(1),
+        normed,
+        *[half for task in tasks for half in (task.value, task.other)],
+    )
+    return results[0::2], results[1::2]
 
 
 class Scatter:
-    def __init__(self, exchange, terms, order):
+    def __init__(self, exchange, terms, order, away=None):
         self.exchange = exchange
-        rows = terms.shape[0] // exchange.count
-        self.value = terms.reshape((2,) * exchange.bits + (rows,) + terms.shape[1:])
+        self.held = list(range(exchange.bits - 1, -1, -1))
+        if away is not None:
+            self.held.remove(CORE_BIT)
+        dims = (2,) * len(self.held)
+        rows = terms.shape[0] >> len(self.held)
+        self.value = terms.reshape(dims + (rows,) + terms.shape[1:])
+        self.away = None if away is None else away.reshape(self.value.shape)
         self.steps = list(exchange.orders[order])
-        self.held = list(range(exchange.bits - 1, -1, -1))
         self.flight = None
 
     def done(self):
@@ -607,6 +680,9 @@
 
     def go(self):
         bit = self.steps[0]
+        if self.away is not None:
+            self.flight = self.exchange.swap(self.away, bit)
+            return
         self.spot = self.held.index(bit)
         away = lax.dynamic_index_in_dim(
             self.value, 1 - self.exchange.mine(bit), self.spot, keepdims=False
@@ -616,14 +692,17 @@
     def land(self):
         bit = self.steps.pop(0)
         other, self.flight = self.flight, None
-        stay = lax.dynamic_index_in_dim(
-            self.value, self.exchange.mine(bit), self.spot, keepdims=False
-        )
+        stay = self.value
+        if self.away is None:
+            stay = lax.dynamic_index_in_dim(
+                self.value, self.exchange.mine(bit), self.spot, keepdims=False
+            )
+            self.held.pop(self.spot)
+        self.away = None
         value = stay.astype(jnp.float32) + other.astype(jnp.float32)
         if self.steps:
             value = value.astype(jnp.bfloat16)
         self.value = value
-        self.held.pop(self.spot)
 
 
 class Traffic:
@@ -658,22 +737,6 @@
     return values * lax.rsqrt(jnp.mean(values * values, axis=-1, keepdims=True) + epsilon) * gain
 
 
-def plain_product(left, right):
-    return jnp.dot(left, right, preferred_element_type=jnp.float32)
-
-
-def left_transposed(left, right):
-    return lax.dot_general(
-        left, right, (((0,), (0,)), ((), ())), preferred_element_type=jnp.float32
-    )
-
-
-def right_transposed(left, right):
-    return lax.dot_general(
-        left, right, (((1,), (1,)), ((), ())), preferred_element_type=jnp.float32
-    )
-
-
 def layer(
     exchange, inputs, norm_first, w_query, w_key, w_value, w_out, rel_table, x_table, y_table,
     norm_second, w_gate, w_up, w_down, lengths, boxes, cotangent,
@@ -694,13 +757,10 @@
     small = exchange.spread(
         jnp.concatenate([norm_first, norm_second, rel_table, x_table, y_table])
     )
-    down_rows, part_rows = w_down.shape[0], w_out.shape[0]
-    groups = -(-down_rows // part_rows)
-    down_pad = jnp.pad(w_down, ((0, groups * part_rows - down_rows), (0, 0)))
-    down_pad = [down_pad[at * part_rows : (at + 1) * part_rows] for at in range(groups)]
     packed = lax.all_gather(
-        jnp.concatenate(down_pad + [w_out, w_gate, w_up], axis=1), AXES, axis=0, tiled=True
-    )
+        jnp.concatenate([w_gate, w_up, w_out], axis=1), AXES, axis=0, tiled=True
+    )
+    down_full = lax.all_gather(w_down, AXES, axis=0, tiled=True)
     ix, iy = index_call(lengths, boxes[0])
     gain_one = small[:, :span].reshape(-1).astype(jnp.float32)
     gain_two = small[:, span : 2 * span].reshape(-1).astype(jnp.float32)
@@ -727,22 +787,23 @@
             bias = bias_call(ix, iy, lhs, skew, begin, end, bias)
     normed_one = norm_apply(rows, gain_one).astype(jnp.bfloat16)
     normed_one, bias = traffic.step(normed_one, bias)
-    query_full, key_full, value_full = (
-        task.value.reshape(-1, task.value.shape[-1]) for task in qkv_tasks
-    )
-    query = plain_product(normed_one, query_full).astype(jnp.bfloat16)
-    key_rows = plain_product(normed_one, key_full).astype(jnp.bfloat16)
-    value_rows = plain_product(normed_one, value_full).astype(jnp.bfloat16)
+    projected, fulls = project_call(exchange, normed_one, qkv_tasks)
+    query, key_rows, value_rows = projected
+    query_full, key_full, value_full = fulls
     probs, mixed = attend_call(query, key_rows, value_rows, bias)
-    first = groups * width
-    out_full = packed[:, first : first + width]
-    down_full = unpack_call(packed, 0, down_rows, part_rows, width)
+    out_full = packed[:, 2 * w_gate.shape[1] :]
     hidden = rows + plain_product(mixed, out_full)
     normed_two = norm_apply(hidden, gain_two).astype(jnp.bfloat16)
-    output, grad_normed_two, d_gate, d_up, d_down = ffn_call(
-        normed_two, normed_two.T, seed, hidden, packed, (first + width) // 256, down_full
-    )
-    ffn_tasks = [Scatter(exchange, part, at) for at, part in enumerate((d_gate, d_up, d_down))]
+    core = exchange.mine(CORE_BIT).astype(jnp.int32).reshape(1)
+    unit = width // count << CORE_BIT
+    output, grad_normed_two, gate_away, gate_stay, up_away, up_stay, d_down = ffn_call(
+        core, unit, normed_two, seed, hidden, packed, down_full
+    )
+    ffn_tasks = [
+        Scatter(exchange, gate_stay, 0, gate_away),
+        Scatter(exchange, up_stay, 1, up_away),
+        Scatter(exchange, d_down, 2),
+    ]
     traffic.add(*ffn_tasks)
     unused_two, norm_two_pull = jax.vjp(norm_apply, hidden, gain_two)
     hidden_part, grad_gain_two = norm_two_pull(grad_normed_two)
@@ -754,7 +815,7 @@
     out_task = Scatter(exchange, d_out, 0)
     traffic.add(out_task)
     pairs = inner // 128
-    cuts = (0, pairs // 2, pairs)
+    cuts = (0, 3 * pairs // 8, 6 * pairs // 8, pairs)
     back = None
     for begin, end in zip(cuts[:-1], cuts[1:]):
         back = attend_back_call(
@@ -771,17 +832,18 @@
         + right_transposed(dk, key_full)
         + right_transposed(dv, value_full)
     )
+    grad_normed_one, ix = traffic.step(grad_normed_one, ix)
     unused_one, norm_one_pull = jax.vjp(norm_apply, rows, gain_one)
     rows_part, grad_gain_one = norm_one_pull(grad_normed_one)
     grad_inputs = (grad_hidden + rows_part).reshape(inputs.shape)
     parts = []
-    pieces = 3
-    grad_inputs, ix = traffic.step(grad_inputs, ix)
+    pieces = 4
     for piece in range(pieces):
         begin, end = piece * blocks // pieces, (piece + 1) * blocks // pieces
         parts.append(table_call(ds, ix, iy, begin, end))
-        ix, parts = traffic.step(ix, parts)
-    grad_rel, grad_x, grad_y = table_finish(parts, slots)
+        if piece + 1 < pieces:
+            ix, parts = traffic.step(ix, parts)
+    grad_rel, grad_x, grad_y = table_finish(parts)
     g_small = exchange.sum_small(
         jnp.concatenate(
             [

time: 672 us -> 590 us (0.88)
  Pallas kernels: 370 us -> 325 us
  waiting for transfers between devices: 37.9 us -> 18.6 us
  matrix products: 41.7 us -> 29.1 us
  starting transfers between devices: 58.8 us -> 66.5 us
  local copies, waits for them, and re-layouts: 70 us -> 62.8 us
    ppermute x50, waiting for transfers between devices: 31.4 us -> 12.1 us  [swap(): return lax.ppermute(value, AXES, pairs)]
    another operation x30 -> x0, other arithmetic: 16.9 us -> none  [land(): jnp.stack([jnp.where(high, other, self.value), jnp.where(high, self.value...]
    pallas_call x3 -> x4, Pallas kernels: 80.3 us -> 65 us  [table_call(): pl.pallas_call(functools.partial(table_kernel, begin), grid=(end - begin,...]
    pallas_call x1, Pallas kernels: 58.7 us -> 45.1 us  [attend_call(): pl.pallas_call(attend_kernel, grid=(pairs, slots // tile), in_specs=[rows...]
    dot_general x4 -> x1, matrix products: 15.7 us -> 4.89 us  [plain_product(): return jnp.dot(left, right, preferred_element_type=jnp.float32)]
    pallas_call x2 -> x3, Pallas kernels: 62 us -> 52.3 us  [attend_back_call(): pl.pallas_call(attend_back_kernel, grid=(end - begin, slots // tile), in_...]
    unnamed x169 -> x127, local copies, waits for them, and re-layouts: 23.3 us -> 22.7 us
  transfers between devices with their start and end apart: 53 -> 54, of which waited for: 9 -> 6; matrix products, arithmetic and copies ran while one was open for 18% -> 20% of each run, Pallas kernels for 44% -> 44%
where the time goes in v2:
time: 590 us; the launch traced here: 580 us
  Pallas kernels  325 us (55%)
  starting transfers between devices  66.5 us (11%)
  local copies, waits for them, and re-layouts  62.8 us (11%)
  other arithmetic  61.3 us (10%)
  matrix products  29.1 us (5%)
  waiting for transfers between devices  18.6 us (3%)
  between operations  16.1 us (3%)
    pallas_call x1, Pallas kernels, ffn_call(): pl.pallas_call(functools.partial(ffn_kernel, unit), grid=(count,), in_spe...  69.3 us
    pallas_call x4, Pallas kernels, bias_call(): pl.pallas_call(functools.partial(bias_kernel, begin), grid=(end - begin,)...  65.4 us
    pallas_call x4, Pallas kernels, table_call(): pl.pallas_call(functools.partial(table_kernel, begin), grid=(end - begin,...  65 us
    ppermute x50, starting transfers between devices, swap(): return lax.ppermute(value, AXES, pairs)  54.5 us
    pallas_call x3, Pallas kernels, attend_back_call(): pl.pallas_call(attend_back_kernel, grid=(end - begin, slots // tile), in_...  52.3 us
    pallas_call x1, Pallas kernels, attend_call(): pl.pallas_call(attend_kernel, grid=(pairs, slots // tile), in_specs=[rows...  45.1 us
    convert_element_type x28, other arithmetic, land(): value = value.astype(jnp.bfloat16)  29.2 us
    unnamed x127, local copies, waits for them, and re-layouts  22.7 us
  transfers between devices with their start and end apart: 54, of which 6 were waited for; matrix products, arithmetic and copies ran while one was open for 20% of the time, Pallas kernels for 44%

profile of v2, /device:TPU:0, one launch (start us, length us, event | category | flops | bytes accessed | tf_op | source)
XLA Modules:
  0.0 579.6 jit_solution(11984385292446893881)
XLA Ops:
  9.2 3.4 concatenate.57
  13.3 7.3 %all-to-all-start = ((bf16[32,1,112]{2,1,0:T(2,128)(2,1)}), bf16[32,1,112]{2,1,0:T(2,128)(2,1)S(1)}, u32[]{:S(2)}, u32[]{:S(2)}) async-start(bf16[32,1,112]{2,1,0:T(2,128)(2,1)} %broadcast_in_dim.65), calls=%async_computation | async-start | bytes 32768 | tf_op jit(solution)/shard_map/all_to_all | solution.py:578
  22.5 2.4 collective-permute-start.1
  32.8 12.0 %index.1 = (bf16[1024,1024]{1,0:T(8,128)(2,1)}, bf16[1024,1024]{1,0:T(8,128)(2,1)}) custom-call(s32[1]{0:T(128)S(6)} %copy.198.len_ref, s32[2,1024]{1,0:T(2,128)} %copy.118.box_ref, s32[1024,2]{1,0:T(8,128)} %bitcast.246), custom_call_target="tpu_custom_call" | custom-call | flops 1000000000 | bytes 4000000 | tf_op jit(solution)/shard_map/index/pallas_call | solution.py:120
  46.6 3.6 prepare.1
  50.2 2.5 collective-permute-start.3
  55.9 16.2 %bias.4.rest_0_ = f32[16,1024,1024]{2,1,0:T(8,128)} custom-call(bf16[1024,1024]{1,0:T(8,128)(2,1)} %get-tuple-element.242.ix_ref, bf16[1024,1024]{1,0:T(8,128)(2,1)} %get-tuple-element.135.iy_ref, bf16[256,1024]{1,0:T(8,128)(2,1)} %get-tuple-element.152.lhs_ref, bf16[16,128,640]{2,1,0:T(8,128)(2,1)} %get-tuple-element.138.skew_ref), custom_call_target="tpu_custom_call" | custom-call | flops 8499999744 | bytes 18000000 | tf_op jit(solution)/shard_map/bias/pallas_call | solution.py:234
  76.5 16.3 %bias.5.rest_0_ = f32[16,1024,1024]{2,1,0:T(8,128)} custom-call(bf16[1024,1024]{1,0:T(8,128)(2,1)} %get-tuple-element.242.ix_ref, bf16[1024,1024]{1,0:T(8,128)(2,1)} %get-tuple-element.135.iy_ref, bf16[256,1024]{1,0:T(8,128)(2,1)} %get-tuple-element.152.lhs_ref, bf16[16,128,640]{2,1,0:T(8,128)(2,1)} %get-tuple-element.138.skew_ref, ...), custom_call_target="tpu_custom_call", output_to_operand_aliasing={{}: (4, {})} | custom-call | flops 8499999744 | bytes 18000000 | tf_op jit(solution)/shard_map/bias/pallas_call | solution.py:234
  104.1 16.3 %bias.6.rest_0_ = f32[16,1024,1024]{2,1,0:T(8,128)} custom-call(bf16[1024,1024]{1,0:T(8,128)(2,1)} %get-tuple-element.242.ix_ref, bf16[1024,1024]{1,0:T(8,128)(2,1)} %get-tuple-element.135.iy_ref, bf16[256,1024]{1,0:T(8,128)(2,1)} %get-tuple-element.152.lhs_ref, bf16[16,128,640]{2,1,0:T(8,128)(2,1)} %get-tuple-element.138.skew_ref, ...), custom_call_target="tpu_custom_call", output_to_operand_aliasing={{}: (4, {})} | custom-call | flops 8499999744 | bytes 18000000 | tf_op jit(solution)/shard_map/bias/pallas_call | solution.py:234
  127.5 16.5 %bias.7.bias_ref = f32[16,1024,1024]{2,1,0:T(8,128)} custom-call(bf16[1024,1024]{1,0:T(8,128)(2,1)} %get-tuple-element.242.ix_ref, bf16[1024,1024]{1,0:T(8,128)(2,1)} %get-tuple-element.135.iy_ref, bf16[256,1024]{1,0:T(8,128)(2,1)} %get-tuple-element.152.lhs_ref, bf16[16,128,640]{2,1,0:T(8,128)(2,1)} %get-tuple-element.138.skew_ref, ...), custom_call_target="tpu_custom_call", output_to_operand_aliasing={{}: (4, {})} | custom-call | flops 8499999744 | bytes 18000000 | tf_op jit(solution)/shard_map/bias/pallas_call | solution.py:234
  144.0 12.5 %project.1 = (bf16[1024,1024]{1,0:T(8,128)(2,1)}, bf16[1024,1024]{1,0:T(8,128)(2,1)}, bf16[1024,1024]{1,0:T(8,128)(2,1)}, bf16[1024,1024]{1,0:T(8,128)(2,1)}, bf...) custom-call(s32[1]{0:T(128)} %bitcast.2.me_ref, bf16[1024,1024]{1,0:T(8,128)(2,1)} %fusion.5.x_ref, ...), custom_call_target="tpu_custom_call" | custom-call | flops 6442450944 | bytes 20000000 | tf_op jit(solution)/shard_map/project/pallas_call | solution.py:640
  156.5 45.1 %attend.1 = (bf16[16,1024,1024]{2,1,0:T(8,128)(2,1)}, bf16[1024,1024]{1,0:T(8,128)(2,1)}) custom-call(bf16[1024,1024]{1,0:T(8,128)(2,1)} %get-tuple-element.161.q_ref, bf16[1024,1024]{1,0:T(8,128)(2,1)} %get-tuple-element.162.k_ref, bf16[1024,1024]{1,0:T(8,128)(2,1)} %get-tuple-element.163.v_ref, f32[16,1024,1024]{2,1,0:T(8,128)} %bias.7.bias_ref), custom_call_target="tpu_custom_call" | custom-call | flops 33999998976 | bytes 100000000 | tf_op jit(solution)/shard_map/attend/pallas_call | solution.py:279
  201.7 4.9 multiply_reduce_fusion.2
  210.3 69.3 %ffn.1 = (bf16[1024,1024]{1,0:T(8,128)(2,1)}, f32[1024,1024]{1,0:T(8,128)}, bf16[512,2816]{1,0:T(8,128)(2,1)}, bf16[512,2816]{1,0:T(8,128)(2,1)}, bf16[512,2816]...) custom-call(s32[1]{0:T(128)} %bitcast.core_ref, ...), custom_call_target="tpu_custom_call" | custom-call | flops 53150220288 | bytes 50000000 | tf_op jit(solution)/shard_map/ffn/pallas_call | solution.py:526
  279.6 5.3 constant_dynamic-slice_fusion.8
  292.6 4.6 multiply_reduce_fusion
  298.5 2.9 fusion.7
  301.5 3.8 convolution_convert_fusion.3
  305.3 5.5 convolution_convert_fusion.4.grad_ref
  312.4 3.2 fusion
  318.0 2.8 fusion.1
  322.0 4.1 collective-permute-start.19
  331.7 2.7 constant_dynamic-slice_fusion.6
  335.5 19.3 %attend_back.3 = (bf16[16,1024,1024]{2,1,0:T(8,128)(2,1)}, bf16[1024,1024]{1,0:T(8,128)(2,1)}, bf16[1024,1024]{1,0:T(8,128)(2,1)}, bf16[1024,1024]{1,0:T(8,128)(2,1)}) custom-call(bf16[1024,1024]{1,0:T(8,128)(2,1)} %get-tuple-element.161.q_ref, bf16[1024,1024]{1,0:T(8,128)(2,1)} %get-tuple-element.162.k_ref, bf16[1024,1024]{1,0:T(8,128)(2,1)} %get-tuple-element.163.v_ref, ...), custom_call_target="tpu_custom_call" | custom-call | flops 12750000128 | bytes 27000000 | tf_op jit(solution)/shard_map/attend_back/pallas_call | solution.py:351
  354.8 3.5 collective-permute-done.19
  358.4 4.3 collective-permute-done.18
  379.2 2.4 collective-permute-start.22
  381.6 19.0 %attend_back.4 = (bf16[16,1024,1024]{2,1,0:T(8,128)(2,1)}, bf16[1024,1024]{1,0:T(8,128)(2,1)}, bf16[1024,1024]{1,0:T(8,128)(2,1)}, bf16[1024,1024]{1,0:T(8,128)(2,1)}) custom-call(bf16[1024,1024]{1,0:T(8,128)(2,1)} %get-tuple-element.161.q_ref, ...), custom_call_target="tpu_custom_call", output_to_operand_aliasing={{0}: (5, {}), {1}: (6, {}), {2}: (7, {}), {3}: (8, {})} | custom-call | flops 12750000128 | bytes 27000000 | tf_op jit(solution)/shard_map/attend_back/pallas_call | solution.py:351
  410.2 2.1 collective-permute-start.26
  412.3 14.1 %attend_back.5 = (bf16[16,1024,1024]{2,1,0:T(8,128)(2,1)}, bf16[1024,1024]{1,0:T(8,128)(2,1)}, bf16[1024,1024]{1,0:T(8,128)(2,1)}, bf16[1024,1024]{1,0:T(8,128)(2,1)}) custom-call(bf16[1024,1024]{1,0:T(8,128)(2,1)} %get-tuple-element.161.q_ref, ...), custom_call_target="tpu_custom_call", output_to_operand_aliasing={{0}: (5, {}), {1}: (6, {}), {2}: (7, {}), {3}: (8, {})} | custom-call | flops 8499999744 | bytes 18000000 | tf_op jit(solution)/shard_map/attend_back/pallas_call | solution.py:351
  429.6 2.1 collective-permute-start.32
  434.9 2.3 collective-permute-start.30
  437.2 2.4 convolution_convert_fusion
  439.7 2.4 convolution_convert_fusion.1
  442.1 2.4 convolution_convert_fusion.2
  444.6 2.4 fusion.49
  448.0 2.7 collective-permute-done.31
  455.3 2.8 fusion.48
  458.1 2.4 add_add_fusion.2
  470.6 16.2 %table_back.4 = f32[104,256]{1,0:T(8,128)} custom-call(bf16[16,1024,1024]{2,1,0:T(8,128)(2,1)} %get-tuple-element.224.ds_ref, bf16[1024,1024]{1,0:T(8,128)(2,1)} %get-tuple-element.242.ix_ref, bf16[1024,1024]{1,0:T(8,128)(2,1)} %get-tuple-element.135.iy_ref, bf16[8,512,640]{2,1,0:T(8,128)(2,1)} %constant.228.near_ref), custom_call_target="tpu_custom_call" | custom-call | flops 10000000000 | bytes 10000000 | tf_op jit(solution)/shard_map/table_back/pallas_call | solution.py:435
  486.7 5.4 fusion.9
  498.9 16.3 %table_back.5 = f32[104,256]{1,0:T(8,128)} custom-call(bf16[16,1024,1024]{2,1,0:T(8,128)(2,1)} %get-tuple-element.224.ds_ref, bf16[1024,1024]{1,0:T(8,128)(2,1)} %get-tuple-element.242.ix_ref, bf16[1024,1024]{1,0:T(8,128)(2,1)} %get-tuple-element.135.iy_ref, bf16[8,512,640]{2,1,0:T(8,128)(2,1)} %constant.228.near_ref), custom_call_target="tpu_custom_call" | custom-call | flops 10000000000 | bytes 10000000 | tf_op jit(solution)/shard_map/table_back/pallas_call | solution.py:435
  517.2 2.1 collective-permute-start.44
  519.3 16.2 %table_back.6 = f32[104,256]{1,0:T(8,128)} custom-call(bf16[16,1024,1024]{2,1,0:T(8,128)(2,1)} %get-tuple-element.224.ds_ref, bf16[1024,1024]{1,0:T(8,128)(2,1)} %get-tuple-element.242.ix_ref, bf16[1024,1024]{1,0:T(8,128)(2,1)} %get-tuple-element.135.iy_ref, bf16[8,512,640]{2,1,0:T(8,128)(2,1)} %constant.228.near_ref), custom_call_target="tpu_custom_call" | custom-call | flops 10000000000 | bytes 10000000 | tf_op jit(solution)/shard_map/table_back/pallas_call | solution.py:435
  536.5 2.1 collective-permute-start.48
  538.9 16.4 %table_back.7 = f32[104,256]{1,0:T(8,128)} custom-call(bf16[16,1024,1024]{2,1,0:T(8,128)(2,1)} %get-tuple-element.224.ds_ref, bf16[1024,1024]{1,0:T(8,128)(2,1)} %get-tuple-element.242.ix_ref, bf16[1024,1024]{1,0:T(8,128)(2,1)} %get-tuple-element.135.iy_ref, bf16[8,512,640]{2,1,0:T(8,128)(2,1)} %constant.228.near_ref), custom_call_target="tpu_custom_call" | custom-call | flops 10000000000 | bytes 10000000 | tf_op jit(solution)/shard_map/table_back/pallas_call | solution.py:435
  557.5 4.7 all-to-all-start.1
  562.9 6.4 %all-to-all-done.1 = f32[32,1,112]{2,1,0:T(1,128)S(1)} async-done(((f32[32,1,112]{2,1,0:T(1,128)}), f32[32,1,112]{2,1,0:T(1,128)S(1)}, u32[]{:S(2)}, u32[]{:S(2)}) %all-to-all-start.1) | async-done | bytes 14368 | tf_op jit(solution)/shard_map/all_to_all | solution.py:581
  (339 shorter events, 127.9 us)
Async XLA Ops:
  7.2 194.5 %all-gather.3.cloned.1.call-start = ((), (), s32[]{:S(2)}) async-start(), calls=%async_computation.2 | async-start | bytes 14057472 | tf_op jit(solution)/shard_map/all_gather | solution.py:760
  13.3 31.4 %all-to-all-start = ((bf16[32,1,112]{2,1,0:T(2,128)(2,1)}), bf16[32,1,112]{2,1,0:T(2,128)(2,1)S(1)}, u32[]{:S(2)}, u32[]{:S(2)}) async-start(bf16[32,1,112]{2,1,0:T(2,128)(2,1)} %broadcast_in_dim.65), calls=%async_computation | async-start | bytes 32768 | tf_op jit(solution)/shard_map/all_to_all | solution.py:578
  20.6 189.7 %all-gather.5.cloned.1.call-start = ((), (), s32[]{:S(2)}) async-start(), calls=%async_computation.3 | async-start | bytes 5947392 | tf_op jit(solution)/shard_map/all_gather | solution.py:763
  20.7 29.5 %collective-permute-start = (bf16[1,32,1024]{2,1,0:T(8,128)(2,1)}, bf16[1,32,1024]{2,1,0:T(8,128)(2,1)S(1)}, u32[]{:S(2)}, u32[]{:S(2)}) collective-permute-start(bf16[1,32,1024]{2,1,0:T(8,128)(2,1)} %bitcast.259), channel_id=1, source_target_pairs={{0,8},{1,9},{2,10},{3,11},{4,12},{5,13},{6,14},{7,15},{8,0},{9,1},... | collective-permute-start | bytes 196616 | tf_op jit(solution)/shard_map/ppermute | solution.py:574
  22.5 27.7 %collective-permute-start.1 = (bf16[1,32,1024]{2,1,0:T(8,128)(2,1)}, bf16[1,32,1024]{2,1,0:T(8,128)(2,1)S(1)}, u32[]{:S(2)}, u32[]{:S(2)}) collective-permute-start(bf16[1,32,1024]{2,1,0:T(8,128)(2,1)} %bitcast.255), channel_id=1, source_target_pairs={{0,16},{1,17},{2,18},{3,19},{4,20},{5,21},{6,22},{7,23},{8,24},{9,... | collective-permute-start | bytes 196616 | tf_op jit(solution)/shard_map/ppermute | solution.py:574
  24.9 25.3 %collective-permute-start.2 = (bf16[1,32,1024]{2,1,0:T(8,128)(2,1)}, bf16[1,32,1024]{2,1,0:T(8,128)(2,1)S(1)}, u32[]{:S(2)}, u32[]{:S(2)}) collective-permute-start(bf16[1,32,1024]{2,1,0:T(8,128)(2,1)} %bitcast.251), channel_id=1, source_target_pairs={{0,16},{1,17},{2,18},{3,19},{4,20},{5,21},{6,22},{7,23},{8,24},{9,... | collective-permute-start | bytes 196616 | tf_op jit(solution)/shard_map/ppermute | solution.py:574
  50.2 23.2 %collective-permute-start.3 = (bf16[2,32,1024]{2,1,0:T(8,128)(2,1)S(1)}, bf16[2,32,1024]{2,1,0:T(8,128)(2,1)S(1)}, u32[]{:S(2)}, u32[]{:S(2)}) collective-permute-start(bf16[2,32,1024]{2,1,0:T(8,128)(2,1)S(1)} %pad_maximum_fusion.7), channel_id=1, source_target_pairs={{0,16},{1,17},{2,18},{3,19},{4,20},{5,21},{6,22},{7,23},{8,24},{9,... | collective-permute-start | bytes 393224 | tf_op jit(solution)/shard_map/ppermute | solution.py:574
  52.8 20.6 %collective-permute-start.4 = (bf16[2,32,1024]{2,1,0:T(8,128)(2,1)S(1)}, bf16[2,32,1024]{2,1,0:T(8,128)(2,1)S(1)}, u32[]{:S(2)}, u32[]{:S(2)}) collective-permute-start(bf16[2,32,1024]{2,1,0:T(8,128)(2,1)S(1)} %pad_maximum_fusion.8), channel_id=1, source_target_pairs={{0,1},{1,0},{2,3},{3,2},{4,5},{5,4},{6,7},{7,6},{8,9},{9,8},{10,11... | collective-permute-start | bytes 393224 | tf_op jit(solution)/shard_map/ppermute | solution.py:574
  54.3 19.1 %collective-permute-start.5 = (bf16[2,32,1024]{2,1,0:T(8,128)(2,1)S(1)}, bf16[2,32,1024]{2,1,0:T(8,128)(2,1)S(1)}, u32[]{:S(2)}, u32[]{:S(2)}) collective-permute-start(bf16[2,32,1024]{2,1,0:T(8,128)(2,1)S(1)} %pad_maximum_fusion.9), channel_id=1, source_target_pairs={{0,4},{1,5},{2,6},{3,7},{4,0},{5,1},{6,2},{7,3},{8,12},{9,13},{10,... | collective-permute-start | bytes 393224 | tf_op jit(solution)/shard_map/ppermute | solution.py:574
  73.5 21.3 %collective-permute-start.6 = (bf16[4,32,1024]{2,1,0:T(8,128)(2,1)S(1)}, bf16[4,32,1024]{2,1,0:T(8,128)(2,1)S(1)}, u32[]{:S(2)}, u32[]{:S(2)}) collective-permute-start(bf16[4,32,1024]{2,1,0:T(8,128)(2,1)S(1)} %pad_maximum_fusion.4), channel_id=1, source_target_pairs={{0,4},{1,5},{2,6},{3,7},{4,0},{5,1},{6,2},{7,3},{8,12},{9,13},{10,... | collective-permute-start | bytes 786440 | tf_op jit(solution)/shard_map/ppermute | solution.py:574
  74.8 20.0 %collective-permute-start.7 = (bf16[4,32,1024]{2,1,0:T(8,128)(2,1)}, bf16[4,32,1024]{2,1,0:T(8,128)(2,1)S(1)}, u32[]{:S(2)}, u32[]{:S(2)}) collective-permute-start(bf16[4,32,1024]{2,1,0:T(8,128)(2,1)} %pad_maximum_fusion.5), channel_id=1, source_target_pairs={{0,8},{1,9},{2,10},{3,11},{4,12},{5,13},{6,14},{7,15},{8,0},{9,1},... | collective-permute-start | bytes 786440 | tf_op jit(solution)/shard_map/ppermute | solution.py:574
  76.0 18.8 %collective-permute-start.8 = (bf16[4,32,1024]{2,1,0:T(8,128)(2,1)}, bf16[4,32,1024]{2,1,0:T(8,128)(2,1)S(1)}, u32[]{:S(2)}, u32[]{:S(2)}) collective-permute-start(bf16[4,32,1024]{2,1,0:T(8,128)(2,1)} %pad_maximum_fusion.6), channel_id=1, source_target_pairs={{0,1},{1,0},{2,3},{3,2},{4,5},{5,4},{6,7},{7,6},{8,9},{9,8},{10,11... | collective-permute-start | bytes 786440 | tf_op jit(solution)/shard_map/ppermute | solution.py:574
  95.7 25.3 %collective-permute-start.11 = (bf16[8,32,1024]{2,1,0:T(8,128)(2,1)}, bf16[8,32,1024]{2,1,0:T(8,128)(2,1)}, u32[]{:S(2)}, u32[]{:S(2)}) collective-permute-start(bf16[8,32,1024]{2,1,0:T(8,128)(2,1)} %pad_maximum_fusion.2), channel_id=1, source_target_pairs={{0,8},{1,9},{2,10},{3,11},{4,12},{5,13},{6,14},{7,15},{8,0},{9,1},... | collective-permute-start | bytes 1572872 | tf_op jit(solution)/shard_map/ppermute | solution.py:574
  98.1 22.8 %collective-permute-start.10 = (bf16[8,32,1024]{2,1,0:T(8,128)(2,1)}, bf16[8,32,1024]{2,1,0:T(8,128)(2,1)}, u32[]{:S(2)}, u32[]{:S(2)}) collective-permute-start(bf16[8,32,1024]{2,1,0:T(8,128)(2,1)} %pad_maximum_fusion.1), channel_id=1, source_target_pairs={{0,4},{1,5},{2,6},{3,7},{4,0},{5,1},{6,2},{7,3},{8,12},{9,13},{10,... | collective-permute-start | bytes 1572872 | tf_op jit(solution)/shard_map/ppermute | solution.py:574
  100.4 20.5 %collective-permute-start.9 = (bf16[8,32,1024]{2,1,0:T(8,128)(2,1)}, bf16[8,32,1024]{2,1,0:T(8,128)(2,1)S(1)}, u32[]{:S(2)}, u32[]{:S(2)}) collective-permute-start(bf16[8,32,1024]{2,1,0:T(8,128)(2,1)} %pad_maximum_fusion), channel_id=1, source_target_pairs={{0,1},{1,0},{2,3},{3,2},{4,5},{5,4},{6,7},{7,6},{8,9},{9,8},{10,11... | collective-permute-start | bytes 1572872 | tf_op jit(solution)/shard_map/ppermute | solution.py:574
  122.8 21.2 %collective-permute-start.14 = (bf16[16,32,1024]{2,1,0:T(8,128)(2,1)}, bf16[16,32,1024]{2,1,0:T(8,128)(2,1)}, u32[]{:S(2)}, u32[]{:S(2)}) collective-permute-start(bf16[16,32,1024]{2,1,0:T(8,128)(2,1)} %constant_dynamic-update-slice_fusion.10.refs_4_), channel_id=1, source_target_pairs={{0,2},{1,3},{2,0},{3,1},{4,6},{5,7},{6,4},{7,5},{8,10},{9,11},{10,... | collective-permute-start | bytes 3145736 | tf_op jit(solution)/shard_map/ppermute | solution.py:574
  124.0 20.0 %collective-permute-start.13 = (bf16[16,32,1024]{2,1,0:T(8,128)(2,1)S(1)}, bf16[16,32,1024]{2,1,0:T(8,128)(2,1)}, u32[]{:S(2)}, u32[]{:S(2)}) collective-permute-start(bf16[16,32,1024]{2,1,0:T(8,128)(2,1)S(1)} %constant_dynamic-update-slice_fusion.5.refs_2_), channel_id=1, source_target_pairs={{0,2},{1,3},{2,0},{3,1},{4,6},{5,7},{6,4},{7,5},{8,10},{9,11},{10,... | collective-permute-start | bytes 3145736 | tf_op jit(solution)/shard_map/ppermute | solution.py:574
  125.3 18.7 %collective-permute-start.12 = (bf16[16,32,1024]{2,1,0:T(8,128)(2,1)}, bf16[16,32,1024]{2,1,0:T(8,128)(2,1)}, u32[]{:S(2)}, u32[]{:S(2)}) collective-permute-start(bf16[16,32,1024]{2,1,0:T(8,128)(2,1)} %constant_dynamic-update-slice_fusion.refs_0_), channel_id=1, source_target_pairs={{0,2},{1,3},{2,0},{3,1},{4,6},{5,7},{6,4},{7,5},{8,10},{9,11},{10,... | collective-permute-start | bytes 3145736 | tf_op jit(solution)/shard_map/ppermute | solution.py:574
  286.9 23.8 %collective-permute-start.17 = (bf16[2,2,2,2,88,1024]{5,4,0,2,3,1:T(8,128)(2,1)}, bf16[2,2,2,2,88,1024]{5,4,0,2,3,1:T(8,128)(2,1)}, u32[]{:S(2)}, u32[]{:S(2)}) collective-permute-start(bf16[2,2,2,2,88,1024]{5,4,0,2,3,1:T(8,128)(2,1)} %bitcast.230), channel_id=1, source_target_pairs={{0,2},{1,3},{2,0},{3,1},{4,6},{5,7},{6,4},{7,5},{8,10},{9,11},{10,... | collective-permute-start | bytes 8650760 | tf_op jit(solution)/shard_map/ppermute | solution.py:574
  289.5 21.2 %collective-permute-start.15 = (bf16[2,2,2,2,32,2816]{5,4,1,0,2,3:T(8,128)(2,1)}, bf16[2,2,2,2,32,2816]{5,4,1,0,2,3:T(8,128)(2,1)S(1)}, u32[]{:S(2)}, u32[]{:S(2)}) collective-permute-start(bf16[2,2,2,2,32,2816]{5,4,1,0,2,3:T(8,128)(2,1)} %copy.120), channel_id=1, source_target_pairs={{0,2},{1,3},{2,0},{3,1},{4,6},{5,7},{6,4},{7,5},{8,10},{9,11},{10,... | collective-permute-start | bytes 8650760 | tf_op jit(solution)/shard_map/ppermute | solution.py:574
  292.4 18.3 %collective-permute-start.16 = (bf16[2,2,2,2,32,2816]{5,4,0,3,1,2:T(8,128)(2,1)}, bf16[2,2,2,2,32,2816]{5,4,0,3,1,2:T(8,128)(2,1)}, u32[]{:S(2)}, u32[]{:S(2)}) collective-permute-start(bf16[2,2,2,2,32,2816]{5,4,0,3,1,2:T(8,128)(2,1)} %copy.121), channel_id=1, source_target_pairs={{0,2},{1,3},{2,0},{3,1},{4,6},{5,7},{6,4},{7,5},{8,10},{9,11},{10,... | collective-permute-start | bytes 8650760 | tf_op jit(solution)/shard_map/ppermute | solution.py:574
  317.0 37.9 %collective-permute-start.20 = (bf16[2,2,2,88,1024]{4,3,0,1,2:T(8,128)(2,1)}, bf16[2,2,2,88,1024]{4,3,0,1,2:T(8,128)(2,1)}, u32[]{:S(2)}, u32[]{:S(2)}) collective-permute-start(bf16[2,2,2,88,1024]{4,3,0,1,2:T(8,128)(2,1)} %dynamic-slice_bitcast_fusion), channel_id=1, source_target_pairs={{0,8},{1,9},{2,10},{3,11},{4,12},{5,13},{6,14},{7,15},{8,0},{9,1},... | collective-permute-start | bytes 4325384 | tf_op jit(solution)/shard_map/ppermute | solution.py:574
  322.0 36.4 %collective-permute-start.19 = (bf16[2,2,2,32,2816]{4,3,0,2,1:T(8,128)(2,1)}, bf16[2,2,2,32,2816]{4,3,0,2,1:T(8,128)(2,1)}, u32[]{:S(2)}, u32[]{:S(2)}) collective-permute-start(bf16[2,2,2,32,2816]{4,3,0,2,1:T(8,128)(2,1)} %dynamic-slice_bitcast_fusion.1), channel_id=1, source_target_pairs={{0,4},{1,5},{2,6},{3,7},{4,0},{5,1},{6,2},{7,3},{8,12},{9,13},{10,... | collective-permute-start | bytes 4325384 | tf_op jit(solution)/shard_map/ppermute | solution.py:574
  328.9 33.8 %collective-permute-start.18 = (bf16[2,2,2,32,2816]{4,3,1,0,2:T(8,128)(2,1)}, bf16[2,2,2,32,2816]{4,3,1,0,2:T(8,128)(2,1)}, u32[]{:S(2)}, u32[]{:S(2)}) collective-permute-start(bf16[2,2,2,32,2816]{4,3,1,0,2:T(8,128)(2,1)} %dynamic-slice_bitcast_fusion.2), channel_id=1, source_target_pairs={{0,1},{1,0},{2,3},{3,2},{4,5},{5,4},{6,7},{7,6},{8,9},{9,8},{10,11... | collective-permute-start | bytes 4325384 | tf_op jit(solution)/shard_map/ppermute | solution.py:574
  335.5 19.3 %collective-permute-start.21 = (bf16[2,2,2,2,32,1024]{5,4,1,0,2,3:T(8,128)(2,1)}, bf16[2,2,2,2,32,1024]{5,4,1,0,2,3:T(8,128)(2,1)}, u32[]{:S(2)}, u32[]{:S(2)}) collective-permute-start(bf16[2,2,2,2,32,1024]{5,4,1,0,2,3:T(8,128)(2,1)} %bitcast.234), channel_id=1, source_target_pairs={{0,2},{1,3},{2,0},{3,1},{4,6},{5,7},{6,4},{7,5},{8,10},{9,11},{10,... | collective-permute-start | bytes 3145736 | tf_op jit(solution)/shard_map/ppermute | solution.py:574
  365.7 34.8 %collective-permute-start.25 = (bf16[2,2,2,32,1024]{4,3,1,0,2:T(8,128)(2,1)}, bf16[2,2,2,32,1024]{4,3,1,0,2:T(8,128)(2,1)}, u32[]{:S(2)}, u32[]{:S(2)}) collective-permute-start(bf16[2,2,2,32,1024]{4,3,1,0,2:T(8,128)(2,1)} %dynamic-slice_bitcast_fusion.9), channel_id=1, source_target_pairs={{0,1},{1,0},{2,3},{3,2},{4,5},{5,4},{6,7},{7,6},{8,9},{9,8},{10,11... | collective-permute-start | bytes 1572872 | tf_op jit(solution)/shard_map/ppermute | solution.py:574
  371.2 29.4 %collective-permute-start.24 = (bf16[2,2,88,1024]{3,2,0,1:T(8,128)(2,1)}, bf16[2,2,88,1024]{3,2,0,1:T(8,128)(2,1)}, u32[]{:S(2)}, u32[]{:S(2)}) collective-permute-start(bf16[2,2,88,1024]{3,2,0,1:T(8,128)(2,1)} %dynamic-slice_bitcast_fusion.3), channel_id=1, source_target_pairs={{0,1},{1,0},{2,3},{3,2},{4,5},{5,4},{6,7},{7,6},{8,9},{9,8},{10,11... | collective-permute-start | bytes 2162696 | tf_op jit(solution)/shard_map/ppermute | solution.py:574
  374.7 25.9 %collective-permute-start.23 = (bf16[2,2,32,2816]{3,2,0,1:T(8,128)(2,1)}, bf16[2,2,32,2816]{3,2,0,1:T(8,128)(2,1)}, u32[]{:S(2)}, u32[]{:S(2)}) collective-permute-start(bf16[2,2,32,2816]{3,2,0,1:T(8,128)(2,1)} %dynamic-slice_bitcast_fusion.4), channel_id=1, source_target_pairs={{0,8},{1,9},{2,10},{3,11},{4,12},{5,13},{6,14},{7,15},{8,0},{9,1},... | collective-permute-start | bytes 2162696 | tf_op jit(solution)/shard_map/ppermute | solution.py:574
  379.2 21.4 %collective-permute-start.22 = (bf16[2,2,32,2816]{3,2,1,0:T(8,128)(2,1)}, bf16[2,2,32,2816]{3,2,1,0:T(8,128)(2,1)}, u32[]{:S(2)}, u32[]{:S(2)}) collective-permute-start(bf16[2,2,32,2816]{3,2,1,0:T(8,128)(2,1)} %dynamic-slice_bitcast_fusion.5), channel_id=1, source_target_pairs={{0,4},{1,5},{2,6},{3,7},{4,0},{5,1},{6,2},{7,3},{8,12},{9,13},{10,... | collective-permute-start | bytes 2162696 | tf_op jit(solution)/shard_map/ppermute | solution.py:574
  402.8 23.6 %collective-permute-start.29 = (bf16[2,2,32,1024]{3,2,1,0:T(8,128)(2,1)}, bf16[2,2,32,1024]{3,2,1,0:T(8,128)(2,1)}, u32[]{:S(2)}, u32[]{:S(2)}) collective-permute-start(bf16[2,2,32,1024]{3,2,1,0:T(8,128)(2,1)} %dynamic-slice_bitcast_fusion.16), channel_id=1, source_target_pairs={{0,4},{1,5},{2,6},{3,7},{4,0},{5,1},{6,2},{7,3},{8,12},{9,13},{10,... | collective-permute-start | bytes 786440 | tf_op jit(solution)/shard_map/ppermute | solution.py:574
  404.4 21.9 %collective-permute-start.28 = (bf16[2,88,1024]{2,1,0:T(8,128)(2,1)S(1)}, bf16[2,88,1024]{2,1,0:T(8,128)(2,1)}, u32[]{:S(2)}, u32[]{:S(2)}) collective-permute-start(bf16[2,88,1024]{2,1,0:T(8,128)(2,1)S(1)} %dynamic-slice_bitcast_fusion.10), channel_id=1, source_target_pairs={{0,4},{1,5},{2,6},{3,7},{4,0},{5,1},{6,2},{7,3},{8,12},{9,13},{10,... | collective-permute-start | bytes 1081352 | tf_op jit(solution)/shard_map/ppermute | solution.py:574
  407.6 18.8 %collective-permute-start.27 = (bf16[2,32,2816]{2,1,0:T(8,128)(2,1)S(1)}, bf16[2,32,2816]{2,1,0:T(8,128)(2,1)}, u32[]{:S(2)}, u32[]{:S(2)}) collective-permute-start(bf16[2,32,2816]{2,1,0:T(8,128)(2,1)S(1)} %dynamic-slice_bitcast_fusion.11), channel_id=1, source_target_pairs={{0,1},{1,0},{2,3},{3,2},{4,5},{5,4},{6,7},{7,6},{8,9},{9,8},{10,11... | collective-permute-start | bytes 1081352 | tf_op jit(solution)/shard_map/ppermute | solution.py:574
  410.2 16.2 %collective-permute-start.26 = (bf16[2,32,2816]{2,1,0:T(8,128)(2,1)S(1)}, bf16[2,32,2816]{2,1,0:T(8,128)(2,1)}, u32[]{:S(2)}, u32[]{:S(2)}) collective-permute-start(bf16[2,32,2816]{2,1,0:T(8,128)(2,1)S(1)} %dynamic-slice_bitcast_fusion.12), channel_id=1, source_target_pairs={{0,16},{1,17},{2,18},{3,19},{4,20},{5,21},{6,22},{7,23},{8,24},{9,... | collective-permute-start | bytes 1081352 | tf_op jit(solution)/shard_map/ppermute | solution.py:574
  427.6 19.4 %collective-permute-start.33 = (bf16[2,32,1024]{2,1,0:T(8,128)(2,1)S(1)}, bf16[2,32,1024]{2,1,0:T(8,128)(2,1)S(1)}, u32[]{:S(2)}, u32[]{:S(2)}) collective-permute-start(bf16[2,32,1024]{2,1,0:T(8,128)(2,1)S(1)} %dynamic-slice_bitcast_fusion.23), channel_id=1, source_target_pairs={{0,16},{1,17},{2,18},{3,19},{4,20},{5,21},{6,22},{7,23},{8,24},{9,... | collective-permute-start | bytes 393224 | tf_op jit(solution)/shard_map/ppermute | solution.py:574
  429.6 18.3 %collective-permute-start.32 = (bf16[88,1024]{1,0:T(8,128)(2,1)S(1)}, bf16[88,1024]{1,0:T(8,128)(2,1)S(1)}, u32[]{:S(2)}, u32[]{:S(2)}) collective-permute-start(bf16[88,1024]{1,0:T(8,128)(2,1)S(1)} %dynamic-slice_bitcast_fusion.17), channel_id=1, source_target_pairs={{0,16},{1,17},{2,18},{3,19},{4,20},{5,21},{6,22},{7,23},{8,24},{9,... | collective-permute-start | bytes 540680 | tf_op jit(solution)/shard_map/ppermute | solution.py:574
  432.9 17.8 %collective-permute-start.31 = (bf16[32,2816]{1,0:T(8,128)(2,1)S(1)}, bf16[32,2816]{1,0:T(8,128)(2,1)S(1)}, u32[]{:S(2)}, u32[]{:S(2)}) collective-permute-start(bf16[32,2816]{1,0:T(8,128)(2,1)S(1)} %dynamic-slice_bitcast_fusion.18), channel_id=1, source_target_pairs={{0,16},{1,17},{2,18},{3,19},{4,20},{5,21},{6,22},{7,23},{8,24},{9,... | collective-permute-start | bytes 540680 | tf_op jit(solution)/shard_map/ppermute | solution.py:574
  462.7 29.5 %collective-permute-start.40 = (bf16[2,2,2,32,1024]{4,3,0,1,2:T(8,128)(2,1)}, bf16[2,2,2,32,1024]{4,3,0,1,2:T(8,128)(2,1)}, u32[]{:S(2)}, u32[]{:S(2)}) collective-permute-start(bf16[2,2,2,32,1024]{4,3,0,1,2:T(8,128)(2,1)} %dynamic-slice_bitcast_fusion.6), channel_id=1, source_target_pairs={{0,8},{1,9},{2,10},{3,11},{4,12},{5,13},{6,14},{7,15},{8,0},{9,1},... | collective-permute-start | bytes 1572872 | tf_op jit(solution)/shard_map/ppermute | solution.py:574
  466.1 26.1 %collective-permute-start.39 = (bf16[2,2,2,32,1024]{4,3,0,2,1:T(8,128)(2,1)}, bf16[2,2,2,32,1024]{4,3,0,2,1:T(8,128)(2,1)}, u32[]{:S(2)}, u32[]{:S(2)}) collective-permute-start(bf16[2,2,2,32,1024]{4,3,0,2,1:T(8,128)(2,1)} %dynamic-slice_bitcast_fusion.7), channel_id=1, source_target_pairs={{0,4},{1,5},{2,6},{3,7},{4,0},{5,1},{6,2},{7,3},{8,12},{9,13},{10,... | collective-permute-start | bytes 1572872 | tf_op jit(solution)/shard_map/ppermute | solution.py:574
  468.0 24.2 %collective-permute-start.38 = (bf16[2,2,2,32,1024]{4,3,1,0,2:T(8,128)(2,1)}, bf16[2,2,2,32,1024]{4,3,1,0,2:T(8,128)(2,1)}, u32[]{:S(2)}, u32[]{:S(2)}) collective-permute-start(bf16[2,2,2,32,1024]{4,3,1,0,2:T(8,128)(2,1)} %dynamic-slice_bitcast_fusion.8), channel_id=1, source_target_pairs={{0,1},{1,0},{2,3},{3,2},{4,5},{5,4},{6,7},{7,6},{8,9},{9,8},{10,11... | collective-permute-start | bytes 1572872 | tf_op jit(solution)/shard_map/ppermute | solution.py:574
  493.6 21.7 %collective-permute-start.43 = (bf16[2,2,32,1024]{3,2,0,1:T(8,128)(2,1)S(1)}, bf16[2,2,32,1024]{3,2,0,1:T(8,128)(2,1)S(1)}, u32[]{:S(2)}, u32[]{:S(2)}) collective-permute-start(bf16[2,2,32,1024]{3,2,0,1:T(8,128)(2,1)S(1)} %dynamic-slice_bitcast_fusion.13), channel_id=1, source_target_pairs={{0,1},{1,0},{2,3},{3,2},{4,5},{5,4},{6,7},{7,6},{8,9},{9,8},{10,11... | collective-permute-start | bytes 786440 | tf_op jit(solution)/shard_map/ppermute | solution.py:574
  496.0 19.3 %collective-permute-start.42 = (bf16[2,2,32,1024]{3,2,0,1:T(8,128)(2,1)S(1)}, bf16[2,2,32,1024]{3,2,0,1:T(8,128)(2,1)S(1)}, u32[]{:S(2)}, u32[]{:S(2)}) collective-permute-start(bf16[2,2,32,1024]{3,2,0,1:T(8,128)(2,1)S(1)} %dynamic-slice_bitcast_fusion.14), channel_id=1, source_target_pairs={{0,8},{1,9},{2,10},{3,11},{4,12},{5,13},{6,14},{7,15},{8,0},{9,1},... | collective-permute-start | bytes 786440 | tf_op jit(solution)/shard_map/ppermute | solution.py:574
  497.3 17.9 %collective-permute-start.41 = (bf16[2,2,32,1024]{3,2,1,0:T(8,128)(2,1)S(1)}, bf16[2,2,32,1024]{3,2,1,0:T(8,128)(2,1)S(1)}, u32[]{:S(2)}, u32[]{:S(2)}) collective-permute-start(bf16[2,2,32,1024]{3,2,1,0:T(8,128)(2,1)S(1)} %dynamic-slice_bitcast_fusion.15), channel_id=1, source_target_pairs={{0,4},{1,5},{2,6},{3,7},{4,0},{5,1},{6,2},{7,3},{8,12},{9,13},{10,... | collective-permute-start | bytes 786440 | tf_op jit(solution)/shard_map/ppermute | solution.py:574
  515.3 20.1 %collective-permute-start.46 = (bf16[2,32,1024]{2,1,0:T(8,128)(2,1)S(1)}, bf16[2,32,1024]{2,1,0:T(8,128)(2,1)S(1)}, u32[]{:S(2)}, u32[]{:S(2)}) collective-permute-start(bf16[2,32,1024]{2,1,0:T(8,128)(2,1)S(1)} %dynamic-slice_bitcast_fusion.20), channel_id=1, source_target_pairs={{0,4},{1,5},{2,6},{3,7},{4,0},{5,1},{6,2},{7,3},{8,12},{9,13},{10,... | collective-permute-start | bytes 393224 | tf_op jit(solution)/shard_map/ppermute | solution.py:574
  516.1 19.4 %collective-permute-start.45 = (bf16[2,32,1024]{2,1,0:T(8,128)(2,1)S(1)}, bf16[2,32,1024]{2,1,0:T(8,128)(2,1)S(1)}, u32[]{:S(2)}, u32[]{:S(2)}) collective-permute-start(bf16[2,32,1024]{2,1,0:T(8,128)(2,1)S(1)} %dynamic-slice_bitcast_fusion.21), channel_id=1, source_target_pairs={{0,1},{1,0},{2,3},{3,2},{4,5},{5,4},{6,7},{7,6},{8,9},{9,8},{10,11... | collective-permute-start | bytes 393224 | tf_op jit(solution)/shard_map/ppermute | solution.py:574
  517.2 18.3 %collective-permute-start.44 = (bf16[2,32,1024]{2,1,0:T(8,128)(2,1)S(1)}, bf16[2,32,1024]{2,1,0:T(8,128)(2,1)S(1)}, u32[]{:S(2)}, u32[]{:S(2)}) collective-permute-start(bf16[2,32,1024]{2,1,0:T(8,128)(2,1)S(1)} %dynamic-slice_bitcast_fusion.22), channel_id=1, source_target_pairs={{0,16},{1,17},{2,18},{3,19},{4,20},{5,21},{6,22},{7,23},{8,24},{9,... | collective-permute-start | bytes 393224 | tf_op jit(solution)/shard_map/ppermute | solution.py:574
  535.5 33.8 %collective-permute-start.49 = (bf16[32,1024]{1,0:T(8,128)(2,1)S(1)}, bf16[32,1024]{1,0:T(8,128)(2,1)S(1)}, u32[]{:S(2)}, u32[]{:S(2)}) collective-permute-start(bf16[32,1024]{1,0:T(8,128)(2,1)S(1)} %dynamic-slice_bitcast_fusion.24), channel_id=1, source_target_pairs={{0,16},{1,17},{2,18},{3,19},{4,20},{5,21},{6,22},{7,23},{8,24},{9,... | collective-permute-start | bytes 196616 | tf_op jit(solution)/shard_map/ppermute | solution.py:574
  536.5 32.8 %collective-permute-start.48 = (bf16[32,1024]{1,0:T(8,128)(2,1)S(1)}, bf16[32,1024]{1,0:T(8,128)(2,1)S(1)}, u32[]{:S(2)}, u32[]{:S(2)}) collective-permute-start(bf16[32,1024]{1,0:T(8,128)(2,1)S(1)} %dynamic-slice_bitcast_fusion.25), channel_id=1, source_target_pairs={{0,16},{1,17},{2,18},{3,19},{4,20},{5,21},{6,22},{7,23},{8,24},{9,... | collective-permute-start | bytes 196616 | tf_op jit(solution)/shard_map/ppermute | solution.py:574
  538.8 30.6 %collective-permute-start.47 = (bf16[32,1024]{1,0:T(8,128)(2,1)S(1)}, bf16[32,1024]{1,0:T(8,128)(2,1)S(1)}, u32[]{:S(2)}, u32[]{:S(2)}) collective-permute-start(bf16[32,1024]{1,0:T(8,128)(2,1)S(1)} %dynamic-slice_bitcast_fusion.26), channel_id=1, source_target_pairs={{0,8},{1,9},{2,10},{3,11},{4,12},{5,13},{6,14},{7,15},{8,0},{9,1},... | collective-permute-start | bytes 196616 | tf_op jit(solution)/shard_map/ppermute | solution.py:574
  (63 other events, 665.8 us)
Sparse Core Ops, SparseCore 0:
  10.9 121.2 all-gather.2
  135.1 70.0 all-gather.4

commit v3 on v2

--- a/solution.py
+++ b/solution.py
@@ -83,9 +83,16 @@
     half = BUCKETS // 2
     exact = half // 2
     distance = jnp.abs(offset)
-    magnitude = jnp.minimum(distance, exact)
-    for edge in magnitude_steps(span, reach):
-        magnitude = magnitude + (distance >= edge).astype(jnp.int32)
+    edges = magnitude_steps(span, reach)
+    edges = [exact] + edges + [2 * span] * (exact - 1 - len(edges))
+
+    def search(low, high):
+        if high - low == 1:
+            return low
+        middle = (low + high) // 2
+        return jnp.where(distance >= edges[middle], search(middle, high), search(low, middle))
+
+    magnitude = jnp.where(distance < exact, distance, exact + search(0, len(edges)))
     return magnitude + jnp.where(offset > 0, half, 0)
 
 
@@ -96,27 +103,47 @@
     return table[offset + slots - 1][None, :] == np.arange(BUCKETS)[:, None]
 
 
+def write_pairs(marks_ref, x_rows, y_rows):
+    odd = lax.broadcasted_iota(jnp.int32, (16, 1), 0) >= 8
+    one = jnp.ones((16, x_rows.shape[1]), jnp.bfloat16)
+    zero = jnp.zeros((16, x_rows.shape[1]), jnp.bfloat16)
+    shift = jnp.where(odd, 1.0, 0.0).astype(jnp.bfloat16)
+    for at, rows in enumerate((x_rows, y_rows)):
+        even = rows - shift
+        for b in range(0, BUCKETS, 2):
+            begin = (at * BUCKETS + b) * 8
+            marks_ref[begin : begin + 16, :] = jnp.where(even == b, one, zero)
+
+
 def write_marks(marks_ref, x_tile, y_tile, begin=0):
     one = jnp.ones(x_tile.shape, jnp.bfloat16)
     zero = jnp.zeros(x_tile.shape, jnp.bfloat16)
     cols = slice(begin, begin + x_tile.shape[1])
     for b in range(BUCKETS):
+        if b == DEAD_BUCKET:
+            continue
         marks_ref[b * 16 : b * 16 + 16, cols] = jnp.where(x_tile == b, one, zero)
         marks_ref[512 + b * 16 : 512 + b * 16 + 16, cols] = jnp.where(y_tile == b, one, zero)
 
 
-def index_kernel(len_ref, box_ref, turned_ref, ix_ref, iy_ref):
+def index_kernel(len_ref, box_ref, turned_ref, ix_ref, iy_ref, ix2_ref, iy2_ref):
     place = lax.broadcasted_iota(jnp.int32, ix_ref.shape, 1)
     x_bucket = bucket_index(box_ref[0:1, :] - turned_ref[:, 0:1], coord_top, layout_reach)
     y_bucket = bucket_index(box_ref[1:2, :] - turned_ref[:, 1:2], coord_top, layout_reach)
-    x_bucket = jnp.where(place < len_ref[0], x_bucket, DEAD_BUCKET)
-    ix_ref[...] = x_bucket.astype(jnp.float32).astype(jnp.bfloat16)
-    iy_ref[...] = y_bucket.astype(jnp.float32).astype(jnp.bfloat16)
+    x_bucket = jnp.where(place < len_ref[0], x_bucket, DEAD_BUCKET).astype(jnp.float32)
+    y_bucket = y_bucket.astype(jnp.float32)
+    ix_ref[...] = x_bucket.astype(jnp.bfloat16)
+    iy_ref[...] = y_bucket.astype(jnp.bfloat16)
+    for twice_ref, value in ((ix2_ref, x_bucket), (iy2_ref, y_bucket)):
+        for r in range(0, ix_ref.shape[0], 8):
+            part = value[r : r + 8]
+            twice_ref[2 * r : 2 * r + 16, :] = jnp.concatenate([part, part]).astype(jnp.bfloat16)
 
 
 def index_call(length, box):
     slots = box.shape[1]
     tile = pl.BlockSpec((BIAS_TILE, slots), lambda i: (i, 0))
+    twice = pl.BlockSpec((2 * BIAS_TILE, slots), lambda i: (i, 0))
     return pl.pallas_call(
         index_kernel,
         grid=(slots // BIAS_TILE,),
@@ -125,8 +152,9 @@
             pl.BlockSpec((2, slots), lambda i: (0, 0)),
             pl.BlockSpec((BIAS_TILE, 2), lambda i: (i, 0)),
         ],
-        out_specs=[tile, tile],
-        out_shape=[jax.ShapeDtypeStruct((slots, slots), jnp.bfloat16)] * 2,
+        out_specs=[tile, tile, twice, twice],
+        out_shape=[jax.ShapeDtypeStruct((slots, slots), jnp.bfloat16)] * 2
+        + [jax.ShapeDtypeStruct((2 * slots, slots), jnp.bfloat16)] * 2,
         name="index",
         **params_for(1e9, 4e6),
     )(length, box, box.T)
@@ -141,14 +169,14 @@
     for h in range(HEADS):
         wide = jnp.broadcast_to(rel_row[h : h + 1, :], (BIAS_TILE, slots))
         skew = pltpu.roll(wide, 0, 1, stride=1, stride_axis=0)[:, :640]
-        skew_ref[h] = skew.astype(jnp.bfloat16)
-    tall, long = HEADS * 16, 2 * BUCKETS * 16
+        skew_ref[h] = skew
+    tall, long = HEADS * 8, 2 * BUCKETS * 8
     layout = tables[:, BUCKETS:]
     dead = lax.broadcasted_iota(jnp.int32, layout.shape, 1) == DEAD_BUCKET
     layout = jnp.where(dead, jnp.asarray(masked_score, jnp.bfloat16), layout)
-    head_of = lax.broadcasted_iota(jnp.int32, (tall, HEADS), 0) // 16
+    head_of = lax.broadcasted_iota(jnp.int32, (tall, HEADS), 0) // 8
     pick_head = head_of == lax.broadcasted_iota(jnp.int32, (tall, HEADS), 1)
-    bucket_of = lax.broadcasted_iota(jnp.int32, (2 * BUCKETS, long), 1) // 16
+    bucket_of = lax.broadcasted_iota(jnp.int32, (2 * BUCKETS, long), 1) // 8
     pick_bucket = bucket_of == lax.broadcasted_iota(jnp.int32, (2 * BUCKETS, long), 0)
     by_head = jnp.dot(
         pick_head.astype(jnp.bfloat16), layout, preferred_element_type=jnp.float32
@@ -157,8 +185,8 @@
         by_head, pick_bucket.astype(jnp.bfloat16), preferred_element_type=jnp.float32
     )
     same = (
-        lax.broadcasted_iota(jnp.int32, (tall, long), 0) % 16
-        == lax.broadcasted_iota(jnp.int32, (tall, long), 1) % 16
+        lax.broadcasted_iota(jnp.int32, (tall, long), 0) % 8
+        == lax.broadcasted_iota(jnp.int32, (tall, long), 1) % 8
     )
     lhs_ref[...] = jnp.where(same, full, 0.0).astype(jnp.bfloat16)
 
@@ -167,8 +195,8 @@
     return pl.pallas_call(
         prepare_kernel,
         out_shape=[
-            jax.ShapeDtypeStruct((HEADS * 16, 2 * BUCKETS * 16), jnp.bfloat16),
-            jax.ShapeDtypeStruct((HEADS, BIAS_TILE, 640), jnp.bfloat16),
+            jax.ShapeDtypeStruct((HEADS * 8, 2 * BUCKETS * 8), jnp.bfloat16),
+            jax.ShapeDtypeStruct((HEADS, BIAS_TILE, 640), jnp.float32),
         ],
         name="prepare",
         **params_for(1e9, 6e6),
@@ -201,6 +229,11 @@
     bias_ref, first_ref, second_ref = rest[-3:]
     block = pl.program_id(0) + first
     slots = ix_ref.shape[1]
+    rows = BIAS_TILE
+
+    def write(ref, r0):
+        r0 = pl.multiple_of(jnp.minimum(2 * r0, 2 * rows - 16), 16)
+        write_pairs(ref, ix_ref[pl.ds(r0, 16), :], iy_ref[pl.ds(r0, 16), :])
 
     def use(r0, marks_ref):
         out = jnp.dot(lhs_ref[...], marks_ref[...], preferred_element_type=jnp.float32)
@@ -208,16 +241,26 @@
             shift = pl.multiple_of((jnp.clip(c - block, -2, 2) + 2) * 128, 128)
             cols = slice(c * 128, c * 128 + 128)
             for h in range(HEADS):
-                bias_ref[h, pl.ds(r0, 16), cols] = out[
-                    h * 16 : h * 16 + 16, cols
-                ] + skew_ref[h, pl.ds(r0, 16), pl.ds(shift, 128)].astype(jnp.float32)
-
-    two_at_a_time(ix_ref, iy_ref, first_ref, second_ref, use)
+                bias_ref[h, pl.ds(r0, 8), cols] = out[
+                    h * 8 : h * 8 + 8, cols
+                ] + skew_ref[h, pl.ds(r0, 8), pl.ds(shift, 128)]
+
+    write(first_ref, 0)
+
+    def body(t, carry):
+        r0 = pl.multiple_of(t * 16, 16)
+        write(second_ref, r0 + 8)
+        use(r0, first_ref)
+        write(first_ref, r0 + 16)
+        use(pl.multiple_of(r0 + 8, 8), second_ref)
+        return carry
+
+    lax.fori_loop(0, rows // 16, body, 0)
 
 
 def bias_call(ix, iy, lhs, skew, begin, end, held=None):
-    slots = ix.shape[0]
-    tile = pl.BlockSpec((BIAS_TILE, slots), lambda i: (i + begin, 0))
+    slots = ix.shape[1]
+    tile = pl.BlockSpec((2 * BIAS_TILE, slots), lambda i: (i + begin, 0))
     in_specs = [
         tile,
         tile,
@@ -237,7 +280,7 @@
         in_specs=in_specs,
         out_specs=pl.BlockSpec((HEADS, BIAS_TILE, slots), lambda i: (0, i + begin, 0)),
         out_shape=jax.ShapeDtypeStruct((HEADS, slots, slots), jnp.float32),
-        scratch_shapes=[pltpu.VMEM((2 * BUCKETS * 16, slots), jnp.bfloat16)] * 2,
+        scratch_shapes=[pltpu.VMEM((2 * BUCKETS * 8, slots), jnp.bfloat16)] * 2,
         input_output_aliases=aliases,
         name="bias",
         **params_for(34e9 * share, 72e6 * share),
@@ -394,8 +437,8 @@
     low = (place < begin * BIAS_TILE).astype(jnp.float32).astype(jnp.bfloat16)
     high = (place >= (begin + 3) * BIAS_TILE).astype(jnp.float32).astype(jnp.bfloat16)
     for ref in (first_ref, second_ref):
-        ref[2 * BUCKETS * 16 : 2 * BUCKETS * 16 + 16, :] = low
-        ref[2 * BUCKETS * 16 + 16 :, :] = high
+        ref[DEAD_BUCKET * 16 : DEAD_BUCKET * 16 + 16, :] = low
+        ref[(BUCKETS + DEAD_BUCKET) * 16 : (BUCKETS + DEAD_BUCKET) * 16 + 16, :] = high
 
     def use(r0, marks_ref):
         ds, close, near = [], [], []
@@ -423,7 +466,6 @@
             kept = jnp.where(same, ref[...], 0.0).reshape(shape[0] // 16, 16, shape[1])
             out_ref[at : at + shape[0] // 16, :] = kept.sum(axis=1)
             at += shape[0] // 16
-        out_ref[at:, :] = jnp.zeros((out_ref.shape[0] - at, out_ref.shape[1]), jnp.float32)
 
 
 def table_call(ds, ix, iy, begin, end):
@@ -431,7 +473,7 @@
     tile = pl.BlockSpec((BIAS_TILE, slots), lambda i: (i + begin, 0))
     share = (end - begin) * BIAS_TILE / slots
     near = jnp.asarray(rel_near_marks(slots)).astype(jnp.bfloat16)
-    marked = (2 * BUCKETS + 2) * 16
+    marked = 2 * BUCKETS * 16
     return pl.pallas_call(
         functools.partial(table_kernel, begin),
         grid=(end - begin,),
@@ -441,8 +483,8 @@
             tile,
             pl.BlockSpec(near.shape, lambda i: (0, 0, 0)),
         ],
-        out_specs=pl.BlockSpec((104, HEADS * 16), lambda i: (0, 0)),
-        out_shape=jax.ShapeDtypeStruct((104, HEADS * 16), jnp.float32),
+        out_specs=pl.BlockSpec((3 * BUCKETS, HEADS * 16), lambda i: (0, 0)),
+        out_shape=jax.ShapeDtypeStruct((3 * BUCKETS, HEADS * 16), jnp.float32),
         scratch_shapes=[
             pltpu.VMEM((marked, HEADS * 16), jnp.float32),
             pltpu.VMEM((BUCKETS * 16, HEADS * 16), jnp.float32),
@@ -455,28 +497,37 @@
 
 
 def table_finish(parts):
-    sums = sum(parts).reshape(104, HEADS, 16).sum(axis=2).T
-    near = sums[:, 66:98]
-    left, right = BUCKETS // 2 - 1, BUCKETS - 1
+    sums = sum(parts).reshape(3, BUCKETS, HEADS, 16).sum(axis=3).transpose(0, 2, 1)
     column = jnp.arange(BUCKETS)[None, :]
-    rel = near + jnp.where(column == left, sums[:, 64:65], 0.0)
-    rel = rel + jnp.where(column == right, sums[:, 65:66], 0.0)
-    return rel, sums[:, :BUCKETS], sums[:, BUCKETS : 2 * BUCKETS]
+    far = sums[:2, :, DEAD_BUCKET : DEAD_BUCKET + 1]
+    rel = sums[2] + jnp.where(column == BUCKETS // 2 - 1, far[0], 0.0)
+    rel = rel + jnp.where(column == BUCKETS - 1, far[1], 0.0)
+    layout = jnp.where(column == DEAD_BUCKET, 0.0, sums[:2])
+    return rel, layout[0], layout[1]
 
 
 def ffn_kernel(
-    unit, core_ref, n_ref, seed_ref, hidden_ref, gate_ref, up_ref, down_ref,
-    out_ref, dn_ref, gate_away_ref, gate_stay_ref, up_away_ref, up_stay_ref, ddown_ref,
-    out_sum, turned_ref,
+    unit, spots, core_ref, gain_ref, seed_ref, hidden_ref, gate_ref, up_ref, down_ref,
+    out_ref, grad_ref, low_ref, dgain_ref, gate_away_ref, gate_stay_ref, up_away_ref,
+    up_stay_ref, down_away_ref, down_stay_ref, out_sum, n_ref, turned_ref, ddown_ref,
 ):
     step = pl.program_id(0)
-    width = n_ref.shape[1]
+    slots, width = n_ref.shape
     half = width // 2
+    rows = half // len(spots[0])
+
+    def place(refs, spot, value):
+        for ref, part in zip(refs, (value[:half], value[half:])):
+            for at, to in enumerate(spot):
+                ref[to * rows : (to + 1) * rows, :] = part[at * rows : (at + 1) * rows]
 
     @pl.when(step == 0)
     def _():
-        out_sum[...] = hidden_ref[...]
-        dn_ref[...] = jnp.zeros_like(dn_ref)
+        for r in range(0, slots, 64):
+            rows_now = hidden_ref[r : r + 64, :]
+            out_sum[r : r + 64, :] = rows_now
+            n_ref[r : r + 64, :] = norm_apply(rows_now, gain_ref[...]).astype(jnp.bfloat16)
+        grad_ref[...] = jnp.zeros_like(grad_ref)
         core = core_ref[0]
         for lanes in range(0, width, 128):
             turned = n_ref[:, lanes : lanes + 128].T
@@ -501,54 +552,88 @@
     grad_gate = (grad_act * upper * slope).astype(jnp.bfloat16)
     grad_upper = (grad_act * gelu).astype(jnp.bfloat16)
     out_sum[...] += plain_product(activated, w_down)
-    dn_ref[...] += right_transposed(grad_gate, w_gate) + right_transposed(grad_upper, w_up)
+    grad_ref[...] += right_transposed(
+        jnp.concatenate([grad_gate, grad_upper], axis=1), jnp.concatenate([w_gate, w_up], axis=1)
+    )
     d_gate = plain_product(turned_ref[...], grad_gate).astype(jnp.bfloat16)
-    gate_away_ref[...] = d_gate[:half]
-    gate_stay_ref[...] = d_gate[half:]
+    place((gate_away_ref, gate_stay_ref), spots[0], d_gate)
     d_up = plain_product(turned_ref[...], grad_upper).astype(jnp.bfloat16)
-    up_away_ref[...] = d_up[:half]
-    up_stay_ref[...] = d_up[half:]
-    ddown_ref[...] = left_transposed(activated, seed).astype(jnp.bfloat16)
+    place((up_away_ref, up_stay_ref), spots[1], d_up)
+    tile = w_down.shape[0]
+    ddown_ref[pl.ds(pl.multiple_of(step * tile, tile), tile), :] = left_transposed(
+        activated, seed
+    ).astype(jnp.bfloat16)
 
     @pl.when(step == pl.num_programs(0) - 1)
     def _():
-        out_ref[...] = out_sum[...].astype(jnp.bfloat16)
-
-
-def ffn_call(core, unit, normed, seed, hidden, packed, w_down):
-    slots, width = normed.shape
+        gain = gain_ref[...]
+        gain_sum = jnp.zeros((1, width), jnp.float32)
+        for r in range(0, slots, 64):
+            here = slice(r, r + 64)
+            out_ref[here, :] = out_sum[here, :].astype(jnp.bfloat16)
+            value, grad = hidden_ref[here, :], grad_ref[here, :]
+            scale = lax.rsqrt(jnp.mean(value * value, axis=1, keepdims=True) + epsilon)
+            turn = value * scale
+            gain_sum += jnp.sum(grad * turn, axis=0, keepdims=True)
+            grad = grad * gain
+            shift = jnp.mean(grad * turn, axis=1, keepdims=True)
+            total = seed_ref[here, :].astype(jnp.float32) + scale * (grad - turn * shift)
+            grad_ref[here, :] = total
+            low_ref[here, :] = total.astype(jnp.bfloat16)
+        dgain_ref[...] = gain_sum
+        tall = ddown_ref.shape[0] // (2 * len(spots[2]))
+        low_bits = unit // rows
+        flip = core_ref[0] == 1
+        for at, to in enumerate(spots[2]):
+            first = (at // low_bits * 2 * low_bits + at % low_bits) * tall
+            second = first + low_bits * tall
+            zero = ddown_ref[first : first + tall, :]
+            one = ddown_ref[second : second + tall, :]
+            down_away_ref[to * tall : (to + 1) * tall, :] = jnp.where(flip, zero, one)
+            down_stay_ref[to * tall : (to + 1) * tall, :] = jnp.where(flip, one, zero)
+
+
+def ffn_call(core, unit, spots, gain, seed, hidden, packed, w_down):
+    slots, width = hidden.shape
     ff = w_down.shape[0]
     tile = 256
     count = ff // tile
-    full = pl.BlockSpec((slots, width), lambda f: (0, 0))
+    single = pl.Buffered(1)
+    full = pl.BlockSpec((slots, width), lambda f: (0, 0), pipeline_mode=single)
     column = pl.BlockSpec((width // 2, tile), lambda f: (0, f))
     row = pl.BlockSpec((tile, width), lambda f: (f, 0))
+    down_half = pl.BlockSpec((ff // 2, width), lambda f: (0, 0), pipeline_mode=single)
+    vector = pl.BlockSpec((1, width), lambda f: (0, 0))
     return pl.pallas_call(
-        functools.partial(ffn_kernel, unit),
+        functools.partial(ffn_kernel, unit, spots),
         grid=(count,),
         in_specs=[
             pl.BlockSpec(memory_space=pltpu.SMEM),
-            full,
+            vector,
             full,
             full,
             pl.BlockSpec((width, tile), lambda f: (0, f)),
             pl.BlockSpec((width, tile), lambda f: (0, f + count)),
             row,
         ],
-        out_specs=[full, full, column, column, column, column, row],
+        out_specs=[full, full, full, vector] + [column] * 4 + [down_half] * 2,
         out_shape=[
             jax.ShapeDtypeStruct((slots, width), jnp.bfloat16),
             jax.ShapeDtypeStruct((slots, width), jnp.float32),
+            jax.ShapeDtypeStruct((slots, width), jnp.bfloat16),
+            jax.ShapeDtypeStruct((1, width), jnp.float32),
         ]
         + [jax.ShapeDtypeStruct((width // 2, ff), jnp.bfloat16)] * 4
-        + [jax.ShapeDtypeStruct((ff, width), jnp.bfloat16)],
+        + [jax.ShapeDtypeStruct((ff // 2, width), jnp.bfloat16)] * 2,
         scratch_shapes=[
             pltpu.VMEM((slots, width), jnp.float32),
+            pltpu.VMEM((slots, width), jnp.bfloat16),
             pltpu.VMEM((width, slots), jnp.bfloat16),
+            pltpu.VMEM((ff, width), jnp.bfloat16),
         ],
         name="ffn",
         **params_for(18 * slots * width * ff, 50e6),
-    )(core, normed, seed, hidden, packed, packed, w_down)
+    )(core, gain, seed, hidden, packed, packed, w_down)
 
 
 class Exchange:
@@ -573,8 +658,18 @@
         pairs = [(d, d ^ (1 << bit)) for d in range(self.count)]
         return lax.ppermute(value, AXES, pairs)
 
+    def spots(self, order):
+        held = [b for b in range(self.bits - 1, -1, -1) if b != CORE_BIT]
+        steps = self.orders[order][1:]
+        last = len(held) - 1
+        found = []
+        for at in range(1 << len(held)):
+            value = {bit: at >> (last - k) & 1 for k, bit in enumerate(held)}
+            found.append(sum(value[bit] << (last - k) for k, bit in enumerate(steps)))
+        return tuple(found)
+
     def spread(self, shard):
-        copies = jnp.broadcast_to(shard[None, :], (self.count, shard.shape[0]))
+        copies = jnp.broadcast_to(shard[None], (self.count,) + shard.shape)
         return lax.all_to_all(copies, AXES, 0, 0, tiled=True)
 
     def sum_small(self, terms):
@@ -667,7 +762,7 @@
         self.exchange = exchange
         self.held = list(range(exchange.bits - 1, -1, -1))
         if away is not None:
-            self.held.remove(CORE_BIT)
+            self.held = exchange.orders[order][1:]
         dims = (2,) * len(self.held)
         rows = terms.shape[0] >> len(self.held)
         self.value = terms.reshape(dims + (rows,) + terms.shape[1:])
@@ -754,37 +849,36 @@
         Gather(exchange, shard, order) for order, shard in enumerate((w_query, w_key, w_value))
     ]
     traffic.add(*qkv_tasks)
+    longest = max(span, entries)
     small = exchange.spread(
-        jnp.concatenate([norm_first, norm_second, rel_table, x_table, y_table])
-    )
+        jnp.stack(
+            [
+                jnp.pad(part, (0, longest - part.shape[0]))
+                for part in (norm_first, norm_second, rel_table, x_table, y_table)
+            ]
+        )
+    ).reshape(count, 5, longest)
     packed = lax.all_gather(
         jnp.concatenate([w_gate, w_up, w_out], axis=1), AXES, axis=0, tiled=True
     )
     down_full = lax.all_gather(w_down, AXES, axis=0, tiled=True)
-    ix, iy = index_call(lengths, boxes[0])
-    gain_one = small[:, :span].reshape(-1).astype(jnp.float32)
-    gain_two = small[:, span : 2 * span].reshape(-1).astype(jnp.float32)
+    ix, iy, ix_twice, iy_twice = index_call(lengths, traffic.step(boxes)[0])
+    gain_one = small[:, 0, :span].reshape(-1).astype(jnp.float32)
+    gain_two = small[:, 1, :span].reshape(-1).astype(jnp.float32)
     tables = jnp.concatenate(
-        [
-            small[:, 2 * span + at * entries : 2 * span + (at + 1) * entries].reshape(
-                HEADS, BUCKETS
-            )
-            for at in range(3)
-        ],
-        axis=1,
+        [small[:, 2 + at, :entries].reshape(HEADS, BUCKETS) for at in range(3)], axis=1
     )
     lhs, skew = prepare_call(tables, slots)
     blocks = slots // BIAS_TILE
-    pieces = exchange.bits - 1
     bias = None
-    for piece in range(pieces):
-        begin, end = piece * blocks // pieces, (piece + 1) * blocks // pieces
+    cuts = [0, blocks // 4, blocks // 4 * 3, blocks] + [blocks] * (exchange.bits - 5)
+    for begin, end in zip(cuts[:-1], cuts[1:]):
         if bias is None:
             lhs = traffic.step(lhs)
         else:
             lhs, bias = traffic.step(lhs, bias)
         if end > begin:
-            bias = bias_call(ix, iy, lhs, skew, begin, end, bias)
+            bias = bias_call(ix_twice, iy_twice, lhs, skew, begin, end, bias)
     normed_one = norm_apply(rows, gain_one).astype(jnp.bfloat16)
     normed_one, bias = traffic.step(normed_one, bias)
     projected, fulls = project_call(exchange, normed_one, qkv_tasks)
@@ -793,29 +887,21 @@
     probs, mixed = attend_call(query, key_rows, value_rows, bias)
     out_full = packed[:, 2 * w_gate.shape[1] :]
     hidden = rows + plain_product(mixed, out_full)
-    normed_two = norm_apply(hidden, gain_two).astype(jnp.bfloat16)
     core = exchange.mine(CORE_BIT).astype(jnp.int32).reshape(1)
     unit = width // count << CORE_BIT
-    output, grad_normed_two, gate_away, gate_stay, up_away, up_stay, d_down = ffn_call(
-        core, unit, normed_two, seed, hidden, packed, down_full
+    spots = tuple(exchange.spots(order) for order in range(3))
+    output, grad_hidden, branch_low, grad_gain_two, *halves = ffn_call(
+        core, unit, spots, gain_two.reshape(1, -1), seed, hidden, packed, down_full
     )
     ffn_tasks = [
-        Scatter(exchange, gate_stay, 0, gate_away),
-        Scatter(exchange, up_stay, 1, up_away),
-        Scatter(exchange, d_down, 2),
+        Scatter(exchange, halves[2 * at + 1], at, halves[2 * at]) for at in range(3)
     ]
     traffic.add(*ffn_tasks)
-    unused_two, norm_two_pull = jax.vjp(norm_apply, hidden, gain_two)
-    hidden_part, grad_gain_two = norm_two_pull(grad_normed_two)
-    grad_hidden = seed.astype(jnp.float32) + hidden_part
-    branch_low = grad_hidden.astype(jnp.bfloat16)
     d_out = left_transposed(mixed, branch_low).astype(jnp.bfloat16)
     grad_mixed = right_transposed(branch_low, out_full).astype(jnp.bfloat16)
     grad_mixed, d_out = traffic.step(grad_mixed, d_out)
-    out_task = Scatter(exchange, d_out, 0)
-    traffic.add(out_task)
     pairs = inner // 128
-    cuts = (0, 3 * pairs // 8, 6 * pairs // 8, pairs)
+    cuts = (0, pairs)
     back = None
     for begin, end in zip(cuts[:-1], cuts[1:]):
         back = attend_back_call(
@@ -824,25 +910,27 @@
         back = traffic.step(back)
     ds, dq, dk, dv = back
     d_weights = [left_transposed(normed_one, part).astype(jnp.bfloat16) for part in (dq, dk, dv)]
-    dq, d_weights = traffic.step(dq, d_weights)
-    w_tasks = [Scatter(exchange, part, at) for at, part in enumerate(d_weights)]
-    traffic.add(*w_tasks)
     grad_normed_one = (
         right_transposed(dq, query_full)
         + right_transposed(dk, key_full)
         + right_transposed(dv, value_full)
     )
-    grad_normed_one, ix = traffic.step(grad_normed_one, ix)
+    grad_normed_one, d_weights = traffic.step(grad_normed_one, d_weights)
+    half = width // 2
+    d_weights[0] = jnp.concatenate([d_weights[0], d_out[:, :half]], axis=1)
+    d_weights[1] = jnp.concatenate([d_weights[1], d_out[:, half:]], axis=1)
+    w_tasks = [Scatter(exchange, part, at) for at, part in enumerate(d_weights)]
+    traffic.add(*w_tasks)
     unused_one, norm_one_pull = jax.vjp(norm_apply, rows, gain_one)
     rows_part, grad_gain_one = norm_one_pull(grad_normed_one)
     grad_inputs = (grad_hidden + rows_part).reshape(inputs.shape)
+    grad_gain_one, ix = traffic.step(grad_gain_one, ix)
     parts = []
-    pieces = 4
+    pieces = 3
     for piece in range(pieces):
         begin, end = piece * blocks // pieces, (piece + 1) * blocks // pieces
         parts.append(table_call(ds, ix, iy, begin, end))
-        if piece + 1 < pieces:
-            ix, parts = traffic.step(ix, parts)
+        ix, parts = traffic.step(ix, parts)
     grad_rel, grad_x, grad_y = table_finish(parts)
     g_small = exchange.sum_small(
         jnp.concatenate(
@@ -862,10 +950,10 @@
         output.reshape(inputs.shape),
         grad_inputs,
         g_small[0],
-        w_tasks[0].value,
-        w_tasks[1].value,
+        w_tasks[0].value[:, :inner],
+        w_tasks[1].value[:, :inner],
         w_tasks[2].value,
-        out_task.value,
+        jnp.concatenate([task.value[:, inner:] for task in w_tasks[:2]], axis=1),
         g_small[2],
         g_small[3],
         g_small[4],

time: 590 us -> 540 us (0.915)
  Pallas kernels: 325 us -> 300 us
  other arithmetic: 61.3 us -> 44.5 us
  local copies, waits for them, and re-layouts: 62.8 us -> 47.8 us
  waiting for transfers between devices: 18.6 us -> 32 us
  starting transfers between devices: 66.5 us -> 60 us
    ppermute x50 -> x45, waiting for transfers between devices: 12.1 us -> 28 us  [swap(): return lax.ppermute(value, AXES, pairs)]
    pallas_call x4 -> x3, Pallas kernels: 65.4 us -> 49.7 us  [bias_call(): pl.pallas_call(functools.partial(bias_kernel, begin), grid=(end - begin,)...]
    pallas_call x3 -> x1, Pallas kernels: 52.3 us -> 42.5 us  [attend_back_call(): pl.pallas_call(attend_back_kernel, grid=(end - begin, slots // tile), in_...]
    convert_element_type x28 -> x24, other arithmetic: 29.2 us -> 21.1 us  [land(): value = value.astype(jnp.bfloat16)]
    dynamic_slice x5 -> x3, local copies, waits for them, and re-layouts: 8.72 us -> 1.81 us  [land(): lax.dynamic_index_in_dim(self.value, self.exchange.mine(bit), self.spot,...]
    pallas_call x2, Pallas kernels: 72.9 us -> 79.6 us  [the longest x1 74.5 us: ffn_call(): pl.pallas_call(functools.partial(ffn_kernel, unit, spots), grid=(count,),...]
    all_to_all x1, waiting for transfers between devices: 6.45 us -> 0.01 us  [sum_small(): return jnp.sum(lax.all_to_all(terms, AXES, 0, 0, tiled=True), axis=0)]
    pallas_call x4 -> x3, Pallas kernels: 65 us -> 58.6 us  [table_call(): pl.pallas_call(functools.partial(table_kernel, begin), grid=(end - begin,...]
  transfers between devices with their start and end apart: 54 -> 49, of which waited for: 6 -> 11; matrix products, arithmetic and copies ran while one was open for 20% -> 19% of each run, Pallas kernels for 44% -> 42%
where the time goes in v3:
time: 540 us; the launch traced here: 535 us
  Pallas kernels  300 us (56%)
  starting transfers between devices  60 us (11%)
  local copies, waits for them, and re-layouts  47.8 us (9%)
  other arithmetic  44.5 us (8%)
  matrix products  34.5 us (6%)
  waiting for transfers between devices  32 us (6%)
  between operations  15.9 us (3%)
    pallas_call x1, Pallas kernels, ffn_call(): pl.pallas_call(functools.partial(ffn_kernel, unit, spots), grid=(count,),...  74.5 us
    pallas_call x3, Pallas kernels, table_call(): pl.pallas_call(functools.partial(table_kernel, begin), grid=(end - begin,...  58.6 us
    pallas_call x3, Pallas kernels, bias_call(): pl.pallas_call(functools.partial(bias_kernel, begin), grid=(end - begin,)...  49.7 us
    ppermute x45, starting transfers between devices, swap(): return lax.ppermute(value, AXES, pairs)  48.9 us
    pallas_call x1, Pallas kernels, attend_call(): pl.pallas_call(attend_kernel, grid=(pairs, slots // tile), in_specs=[rows...  43.9 us
    pallas_call x1, Pallas kernels, attend_back_call(): pl.pallas_call(attend_back_kernel, grid=(end - begin, slots // tile), in_...  42.5 us
    ppermute x45, waiting for transfers between devices, swap(): return lax.ppermute(value, AXES, pairs)  28 us
    convert_element_type x24, other arithmetic, land(): value = value.astype(jnp.bfloat16)  21.1 us
  transfers between devices with their start and end apart: 49, of which 11 were waited for; matrix products, arithmetic and copies ran while one was open for 19% of the time, Pallas kernels for 42%

profile of v3, /device:TPU:0, one launch (start us, length us, event | category | flops | bytes accessed | tf_op | source)
XLA Modules:
  0.0 535.1 jit_solution(10667557620380135986)
XLA Ops:
  7.2 1.9 pad_maximum_fusion.5
  12.4 7.3 %all-to-all-start = ((bf16[32,5,32]{2,1,0:T(8,128)(2,1)}), bf16[32,5,32]{2,1,0:T(8,128)(2,1)S(1)}, u32[]{:S(2)}, u32[]{:S(2)}) async-start(bf16[32,5,32]{2,1,0:T(8,128)(2,1)} %broadcast_in_dim.82), calls=%async_computation | async-start | bytes 131072 | tf_op jit(solution)/shard_map/all_to_all | solution.py:673
  21.6 2.4 collective-permute-start.1
  29.0 2.1 fusion.9
  33.7 5.1 prepare.1
  39.9 2.5 collective-permute-start.3
  46.8 13.6 %index.1 = (bf16[1024,1024]{1,0:T(8,128)(2,1)}, bf16[1024,1024]{1,0:T(8,128)(2,1)}, bf16[2048,1024]{1,0:T(8,128)(2,1)}, bf16[2048,1024]{1,0:T(8,128)(2,1)}) custom-call(s32[1]{0:T(128)S(6)} %copy.103.len_ref, s32[2,1024]{1,0:T(2,128)} %copy.63.box_ref, s32[1024,2]{1,0:T(8,128)} %bitcast.214), custom_call_target="tpu_custom_call" | custom-call | flops 1000000000 | bytes 4000000 | tf_op jit(solution)/shard_map/index/pallas_call | solution.py:147
  62.9 14.0 %bias.3.rest_0_ = f32[16,1024,1024]{2,1,0:T(8,128)} custom-call(bf16[2048,1024]{1,0:T(8,128)(2,1)} %get-tuple-element.119.ix_ref, bf16[2048,1024]{1,0:T(8,128)(2,1)} %get-tuple-element.120.iy_ref, bf16[128,512]{1,0:T(8,128)(2,1)} %get-tuple-element.135.lhs_ref, f32[16,128,640]{2,1,0:T(8,128)} %get-tuple-element.126.skew_ref), custom_call_target="tpu_custom_call" | custom-call | flops 8499999744 | bytes 18000000 | tf_op jit(solution)/shard_map/bias/pallas_call | solution.py:277
  86.0 21.8 %bias.4.rest_0_ = f32[16,1024,1024]{2,1,0:T(8,128)} custom-call(bf16[2048,1024]{1,0:T(8,128)(2,1)} %get-tuple-element.119.ix_ref, bf16[2048,1024]{1,0:T(8,128)(2,1)} %get-tuple-element.120.iy_ref, bf16[128,512]{1,0:T(8,128)(2,1)} %get-tuple-element.135.lhs_ref, f32[16,128,640]{2,1,0:T(8,128)} %get-tuple-element.126.skew_ref, ...), custom_call_target="tpu_custom_call", output_to_operand_aliasing={{}: (4, {})} | custom-call | flops 16999999488 | bytes 36000000 | tf_op jit(solution)/shard_map/bias/pallas_call | solution.py:277
  110.0 4.0 collective-permute-done.11
  117.1 2.0 constant_dynamic-update-slice_fusion.10.refs_4_
  119.2 1.9 fusion.5.x_ref
  121.1 13.9 %bias.5.bias_ref = f32[16,1024,1024]{2,1,0:T(8,128)} custom-call(bf16[2048,1024]{1,0:T(8,128)(2,1)} %get-tuple-element.119.ix_ref, bf16[2048,1024]{1,0:T(8,128)(2,1)} %get-tuple-element.120.iy_ref, bf16[128,512]{1,0:T(8,128)(2,1)} %get-tuple-element.135.lhs_ref, f32[16,128,640]{2,1,0:T(8,128)} %get-tuple-element.126.skew_ref, ...), custom_call_target="tpu_custom_call", output_to_operand_aliasing={{}: (4, {})} | custom-call | flops 8499999744 | bytes 18000000 | tf_op jit(solution)/shard_map/bias/pallas_call | solution.py:277
  136.0 12.4 %project.1 = (bf16[1024,1024]{1,0:T(8,128)(2,1)}, bf16[1024,1024]{1,0:T(8,128)(2,1)}, bf16[1024,1024]{1,0:T(8,128)(2,1)}, bf16[1024,1024]{1,0:T(8,128)(2,1)}, bf...) custom-call(s32[1]{0:T(128)} %bitcast.8.me_ref, bf16[1024,1024]{1,0:T(8,128)(2,1)} %fusion.5.x_ref, ...), custom_call_target="tpu_custom_call" | custom-call | flops 6442450944 | bytes 20000000 | tf_op jit(solution)/shard_map/project/pallas_call | solution.py:735
  148.4 43.9 %attend.1 = (bf16[16,1024,1024]{2,1,0:T(8,128)(2,1)}, bf16[1024,1024]{1,0:T(8,128)(2,1)}) custom-call(bf16[1024,1024]{1,0:T(8,128)(2,1)} %get-tuple-element.144.q_ref, bf16[1024,1024]{1,0:T(8,128)(2,1)} %get-tuple-element.145.k_ref, bf16[1024,1024]{1,0:T(8,128)(2,1)} %get-tuple-element.146.v_ref, f32[16,1024,1024]{2,1,0:T(8,128)} %bias.5.bias_ref), custom_call_target="tpu_custom_call" | custom-call | flops 33999998976 | bytes 100000000 | tf_op jit(solution)/shard_map/attend/pallas_call | solution.py:322
  192.4 6.6 %convert_add_fusion.hidden_ref = f32[1024,1024]{1,0:T(8,128)} fusion(bf16[1,1024,1024]{2,1,0:T(8,128)(2,1)S(1)} %copy-done, bf16[1024,1024]{1,0:T(8,128)(2,1)} %get-tuple-element.148, bf16[1024,6656]{1,0:T(8,128)(2,1)} %all-gather.3.cloned.1.call-done.gate_ref.up_ref), kind=kOutput, calls=%fused_computation.2 | convolution fusion | flops 2149580800 | bytes 10485760 | tf_op jit(solution)/shard_map/dot_general | solution.py:42
  199.0 4.0 all-gather.5.cloned.1.call-done.down_ref
  202.9 74.5 %ffn.1 = (bf16[1024,1024]{1,0:T(8,128)(2,1)}, f32[1024,1024]{1,0:T(8,128)}, bf16[1024,1024]{1,0:T(8,128)(2,1)}, f32[1,1024]{1,0:T(1,128)}, bf16[512,2816]{1,0:T(...) custom-call(s32[1]{0:T(128)} %bitcast.core_ref, ...), custom_call_target="tpu_custom_call" | custom-call | flops 53150220288 | bytes 50000000 | tf_op jit(solution)/shard_map/ffn/pallas_call | solution.py:607
  282.6 6.1 %convolution_convert_fusion.3 = bf16[1024,1024]{1,0:T(8,128)(2,1)} fusion(bf16[1024,1024]{1,0:T(8,128)(2,1)} %get-tuple-element.148, bf16[1024,1024]{1,0:T(8,128)(2,1)} %get-tuple-element.151), kind=kOutput, calls=%fused_computation.38 | convolution fusion | flops 2148532224 | bytes 6291456 | tf_op jit(solution)/shard_map/dot_general | solution.py:46
  288.7 5.4 %convolution_convert_fusion.4.grad_ref = bf16[1024,1024]{1,0:T(8,128)(2,1)} fusion(bf16[1024,1024]{1,0:T(8,128)(2,1)S(1)} %copy-done.43, bf16[1024,6656]{1,0:T(8,128)(2,1)} %all-gather.3.cloned.1.call-done.gate_ref.up_ref), kind=kOutput, calls=%fused_computation.39 | convolution fusion | flops 2148532224 | bytes 6291456 | tf_op jit(solution)/shard_map/dot_general | solution.py:52
  295.8 2.6 fusion.2
  300.9 2.8 fusion.1
  310.5 2.0 collective-permute-start.20
  312.5 42.5 %attend_back.1 = (bf16[16,1024,1024]{2,1,0:T(8,128)(2,1)}, bf16[1024,1024]{1,0:T(8,128)(2,1)}, bf16[1024,1024]{1,0:T(8,128)(2,1)}, bf16[1024,1024]{1,0:T(8,128)(2,1)}) custom-call(bf16[1024,1024]{1,0:T(8,128)(2,1)} %get-tuple-element.144.q_ref, bf16[1024,1024]{1,0:T(8,128)(2,1)} %get-tuple-element.145.k_ref, bf16[1024,1024]{1,0:T(8,128)(2,1)} %get-tuple-element.146.v_ref, ...), custom_call_target="tpu_custom_call" | custom-call | flops 33999998976 | bytes 72000000 | tf_op jit(solution)/shard_map/attend_back/pallas_call | solution.py:394
  357.9 2.4 convolution_convert_fusion.2
  360.4 2.4 fusion.42
  368.0 2.1 fusion.13
  371.2 2.4 fusion.43
  373.6 2.4 add_add_fusion.1
  376.0 4.2 convolution_convert_fusion.1
  380.2 2.6 convolution_convert_fusion
  382.9 2.8 collective-permute-done.22
  385.7 2.3 collective-permute-done.23
  388.2 1.9 collective-permute-start.24
  400.0 2.6 fusion.8
  402.7 3.3 collective-permute-done.24
  407.7 1.9 collective-permute-start.30
  416.1 16.2 %table_back.3 = f32[96,256]{1,0:T(8,128)} custom-call(bf16[16,1024,1024]{2,1,0:T(8,128)(2,1)} %get-tuple-element.187.ds_ref, bf16[1024,1024]{1,0:T(8,128)(2,1)} %get-tuple-element.199.ix_ref, bf16[1024,1024]{1,0:T(8,128)(2,1)} %get-tuple-element.188.iy_ref, bf16[8,512,640]{2,1,0:T(8,128)(2,1)} %constant.214.near_ref), custom_call_target="tpu_custom_call" | custom-call | flops 10000000000 | bytes 10000000 | tf_op jit(solution)/shard_map/table_back/pallas_call | solution.py:477
  433.9 21.1 %table_back.4 = f32[96,256]{1,0:T(8,128)} custom-call(bf16[16,1024,1024]{2,1,0:T(8,128)(2,1)} %get-tuple-element.187.ds_ref, bf16[1024,1024]{1,0:T(8,128)(2,1)} %get-tuple-element.199.ix_ref, bf16[1024,1024]{1,0:T(8,128)(2,1)} %get-tuple-element.188.iy_ref, bf16[8,512,640]{2,1,0:T(8,128)(2,1)} %constant.214.near_ref), custom_call_target="tpu_custom_call" | custom-call | flops 15000000512 | bytes 15000000 | tf_op jit(solution)/shard_map/table_back/pallas_call | solution.py:477
  463.5 3.0 collective-permute-done.34
  466.5 2.4 collective-permute-done.35
  469.0 3.0 collective-permute-start.37
  474.4 21.3 %table_back.5 = f32[96,256]{1,0:T(8,128)} custom-call(bf16[16,1024,1024]{2,1,0:T(8,128)(2,1)} %get-tuple-element.187.ds_ref, bf16[1024,1024]{1,0:T(8,128)(2,1)} %get-tuple-element.199.ix_ref, bf16[1024,1024]{1,0:T(8,128)(2,1)} %get-tuple-element.188.iy_ref, bf16[8,512,640]{2,1,0:T(8,128)(2,1)} %constant.214.near_ref), custom_call_target="tpu_custom_call" | custom-call | flops 15000000512 | bytes 15000000 | tf_op jit(solution)/shard_map/table_back/pallas_call | solution.py:477
  498.9 3.7 all-to-all-start.1
  508.2 2.5 collective-permute-start.41
  512.5 3.1 collective-permute-done.41
  518.6 2.3 collective-permute-done.43
  523.2 3.1 collective-permute-done.44
  (305 shorter events, 108.9 us)
Async XLA Ops:
  7.2 185.2 %all-gather.3.cloned.1.call-start = ((), (), s32[]{:S(2)}) async-start(), calls=%async_computation.2 | async-start | bytes 14057472 | tf_op jit(solution)/shard_map/all_gather | solution.py:861
  12.4 19.3 %all-to-all-start = ((bf16[32,5,32]{2,1,0:T(8,128)(2,1)}), bf16[32,5,32]{2,1,0:T(8,128)(2,1)S(1)}, u32[]{:S(2)}, u32[]{:S(2)}) async-start(bf16[32,5,32]{2,1,0:T(8,128)(2,1)} %broadcast_in_dim.82), calls=%async_computation | async-start | bytes 131072 | tf_op jit(solution)/shard_map/all_to_all | solution.py:673
  19.7 183.2 %all-gather.5.cloned.1.call-start = ((), (), s32[]{:S(2)}) async-start(), calls=%async_computation.3 | async-start | bytes 5947392 | tf_op jit(solution)/shard_map/all_gather | solution.py:864
  19.8 19.0 %collective-permute-start = (bf16[1,32,1024]{2,1,0:T(8,128)(2,1)}, bf16[1,32,1024]{2,1,0:T(8,128)(2,1)S(1)}, u32[]{:S(2)}, u32[]{:S(2)}) collective-permute-start(bf16[1,32,1024]{2,1,0:T(8,128)(2,1)} %bitcast.218), channel_id=1, source_target_pairs={{0,8},{1,9},{2,10},{3,11},{4,12},{5,13},{6,14},{7,15},{8,0},{9,1},... | collective-permute-start | bytes 196616 | tf_op jit(solution)/shard_map/ppermute | solution.py:659
  21.6 17.2 %collective-permute-start.1 = (bf16[1,32,1024]{2,1,0:T(8,128)(2,1)}, bf16[1,32,1024]{2,1,0:T(8,128)(2,1)S(1)}, u32[]{:S(2)}, u32[]{:S(2)}) collective-permute-start(bf16[1,32,1024]{2,1,0:T(8,128)(2,1)} %bitcast.222), channel_id=1, source_target_pairs={{0,16},{1,17},{2,18},{3,19},{4,20},{5,21},{6,22},{7,23},{8,24},{9,... | collective-permute-start | bytes 196616 | tf_op jit(solution)/shard_map/ppermute | solution.py:659
  24.0 14.8 %collective-permute-start.2 = (bf16[1,32,1024]{2,1,0:T(8,128)(2,1)}, bf16[1,32,1024]{2,1,0:T(8,128)(2,1)S(1)}, u32[]{:S(2)}, u32[]{:S(2)}) collective-permute-start(bf16[1,32,1024]{2,1,0:T(8,128)(2,1)} %bitcast.226), channel_id=1, source_target_pairs={{0,16},{1,17},{2,18},{3,19},{4,20},{5,21},{6,22},{7,23},{8,24},{9,... | collective-permute-start | bytes 196616 | tf_op jit(solution)/shard_map/ppermute | solution.py:659
  39.9 21.1 %collective-permute-start.3 = (bf16[2,32,1024]{2,1,0:T(8,128)(2,1)S(1)}, bf16[2,32,1024]{2,1,0:T(8,128)(2,1)S(1)}, u32[]{:S(2)}, u32[]{:S(2)}) collective-permute-start(bf16[2,32,1024]{2,1,0:T(8,128)(2,1)S(1)} %pad_maximum_fusion.9), channel_id=1, source_target_pairs={{0,16},{1,17},{2,18},{3,19},{4,20},{5,21},{6,22},{7,23},{8,24},{9,... | collective-permute-start | bytes 393224 | tf_op jit(solution)/shard_map/ppermute | solution.py:659
  42.4 18.6 %collective-permute-start.4 = (bf16[2,32,1024]{2,1,0:T(8,128)(2,1)S(1)}, bf16[2,32,1024]{2,1,0:T(8,128)(2,1)S(1)}, u32[]{:S(2)}, u32[]{:S(2)}) collective-permute-start(bf16[2,32,1024]{2,1,0:T(8,128)(2,1)S(1)} %pad_maximum_fusion.10), channel_id=1, source_target_pairs={{0,1},{1,0},{2,3},{3,2},{4,5},{5,4},{6,7},{7,6},{8,9},{9,8},{10,11... | collective-permute-start | bytes 393224 | tf_op jit(solution)/shard_map/ppermute | solution.py:659
  44.0 17.0 %collective-permute-start.5 = (bf16[2,32,1024]{2,1,0:T(8,128)(2,1)S(1)}, bf16[2,32,1024]{2,1,0:T(8,128)(2,1)S(1)}, u32[]{:S(2)}, u32[]{:S(2)}) collective-permute-start(bf16[2,32,1024]{2,1,0:T(8,128)(2,1)S(1)} %pad_maximum_fusion.11), channel_id=1, source_target_pairs={{0,4},{1,5},{2,6},{3,7},{4,0},{5,1},{6,2},{7,3},{8,12},{9,13},{10,... | collective-permute-start | bytes 393224 | tf_op jit(solution)/shard_map/ppermute | solution.py:659
  61.0 17.8 %collective-permute-start.6 = (bf16[4,32,1024]{2,1,0:T(8,128)(2,1)S(1)}, bf16[4,32,1024]{2,1,0:T(8,128)(2,1)S(1)}, u32[]{:S(2)}, u32[]{:S(2)}) collective-permute-start(bf16[4,32,1024]{2,1,0:T(8,128)(2,1)S(1)} %pad_maximum_fusion.6), channel_id=1, source_target_pairs={{0,4},{1,5},{2,6},{3,7},{4,0},{5,1},{6,2},{7,3},{8,12},{9,13},{10,... | collective-permute-start | bytes 786440 | tf_op jit(solution)/shard_map/ppermute | solution.py:659
  61.7 17.2 %collective-permute-start.7 = (bf16[4,32,1024]{2,1,0:T(8,128)(2,1)S(1)}, bf16[4,32,1024]{2,1,0:T(8,128)(2,1)S(1)}, u32[]{:S(2)}, u32[]{:S(2)}) collective-permute-start(bf16[4,32,1024]{2,1,0:T(8,128)(2,1)S(1)} %pad_maximum_fusion.7), channel_id=1, source_target_pairs={{0,8},{1,9},{2,10},{3,11},{4,12},{5,13},{6,14},{7,15},{8,0},{9,1},... | collective-permute-start | bytes 786440 | tf_op jit(solution)/shard_map/ppermute | solution.py:659
  62.3 16.6 %collective-permute-start.8 = (bf16[4,32,1024]{2,1,0:T(8,128)(2,1)S(1)}, bf16[4,32,1024]{2,1,0:T(8,128)(2,1)S(1)}, u32[]{:S(2)}, u32[]{:S(2)}) collective-permute-start(bf16[4,32,1024]{2,1,0:T(8,128)(2,1)S(1)} %pad_maximum_fusion.8), channel_id=1, source_target_pairs={{0,1},{1,0},{2,3},{3,2},{4,5},{5,4},{6,7},{7,6},{8,9},{9,8},{10,11... | collective-permute-start | bytes 786440 | tf_op jit(solution)/shard_map/ppermute | solution.py:659
  79.8 30.2 %collective-permute-start.9 = (bf16[8,32,1024]{2,1,0:T(8,128)(2,1)}, bf16[8,32,1024]{2,1,0:T(8,128)(2,1)S(1)}, u32[]{:S(2)}, u32[]{:S(2)}) collective-permute-start(bf16[8,32,1024]{2,1,0:T(8,128)(2,1)} %pad_maximum_fusion.2), channel_id=1, source_target_pairs={{0,1},{1,0},{2,3},{3,2},{4,5},{5,4},{6,7},{7,6},{8,9},{9,8},{10,11... | collective-permute-start | bytes 1572872 | tf_op jit(solution)/shard_map/ppermute | solution.py:659
  82.1 27.9 %collective-permute-start.10 = (bf16[8,32,1024]{2,1,0:T(8,128)(2,1)}, bf16[8,32,1024]{2,1,0:T(8,128)(2,1)}, u32[]{:S(2)}, u32[]{:S(2)}) collective-permute-start(bf16[8,32,1024]{2,1,0:T(8,128)(2,1)} %pad_maximum_fusion.3), channel_id=1, source_target_pairs={{0,4},{1,5},{2,6},{3,7},{4,0},{5,1},{6,2},{7,3},{8,12},{9,13},{10,... | collective-permute-start | bytes 1572872 | tf_op jit(solution)/shard_map/ppermute | solution.py:659
  84.4 29.5 %collective-permute-start.11 = (bf16[8,32,1024]{2,1,0:T(8,128)(2,1)}, bf16[8,32,1024]{2,1,0:T(8,128)(2,1)}, u32[]{:S(2)}, u32[]{:S(2)}) collective-permute-start(bf16[8,32,1024]{2,1,0:T(8,128)(2,1)} %pad_maximum_fusion.4), channel_id=1, source_target_pairs={{0,8},{1,9},{2,10},{3,11},{4,12},{5,13},{6,14},{7,15},{8,0},{9,1},... | collective-permute-start | bytes 1572872 | tf_op jit(solution)/shard_map/ppermute | solution.py:659
  114.8 20.2 %collective-permute-start.12 = (bf16[16,32,1024]{2,1,0:T(8,128)(2,1)}, bf16[16,32,1024]{2,1,0:T(8,128)(2,1)S(1)}, u32[]{:S(2)}, u32[]{:S(2)}) collective-permute-start(bf16[16,32,1024]{2,1,0:T(8,128)(2,1)} %constant_dynamic-update-slice_fusion.refs_0_), channel_id=1, source_target_pairs={{0,2},{1,3},{2,0},{3,1},{4,6},{5,7},{6,4},{7,5},{8,10},{9,11},{10,... | collective-permute-start | bytes 3145736 | tf_op jit(solution)/shard_map/ppermute | solution.py:659
  116.6 18.4 %collective-permute-start.13 = (bf16[16,32,1024]{2,1,0:T(8,128)(2,1)}, bf16[16,32,1024]{2,1,0:T(8,128)(2,1)}, u32[]{:S(2)}, u32[]{:S(2)}) collective-permute-start(bf16[16,32,1024]{2,1,0:T(8,128)(2,1)} %constant_dynamic-update-slice_fusion.5.refs_2_), channel_id=1, source_target_pairs={{0,2},{1,3},{2,0},{3,1},{4,6},{5,7},{6,4},{7,5},{8,10},{9,11},{10,... | collective-permute-start | bytes 3145736 | tf_op jit(solution)/shard_map/ppermute | solution.py:659
  119.1 15.9 %collective-permute-start.14 = (bf16[16,32,1024]{2,1,0:T(8,128)(2,1)}, bf16[16,32,1024]{2,1,0:T(8,128)(2,1)}, u32[]{:S(2)}, u32[]{:S(2)}) collective-permute-start(bf16[16,32,1024]{2,1,0:T(8,128)(2,1)} %constant_dynamic-update-slice_fusion.10.refs_4_), channel_id=1, source_target_pairs={{0,2},{1,3},{2,0},{3,1},{4,6},{5,7},{6,4},{7,5},{8,10},{9,11},{10,... | collective-permute-start | bytes 3145736 | tf_op jit(solution)/shard_map/ppermute | solution.py:659
  277.4 16.7 %collective-permute-start.15 = (bf16[2,2,2,2,32,2816]{5,4,3,2,1,0:T(8,128)(2,1)}, bf16[2,2,2,2,32,2816]{5,4,3,2,1,0:T(8,128)(2,1)}, u32[]{:S(2)}, u32[]{:S(2)}) collective-permute-start(bf16[2,2,2,2,32,2816]{5,4,3,2,1,0:T(8,128)(2,1)} %bitcast.237), channel_id=1, source_target_pairs={{0,2},{1,3},{2,0},{3,1},{4,6},{5,7},{6,4},{7,5},{8,10},{9,11},{10,... | collective-permute-start | bytes 8650760 | tf_op jit(solution)/shard_map/ppermute | solution.py:659
  277.7 16.4 %collective-permute-start.16 = (bf16[2,2,2,2,32,2816]{5,4,3,2,1,0:T(8,128)(2,1)}, bf16[2,2,2,2,32,2816]{5,4,3,2,1,0:T(8,128)(2,1)}, u32[]{:S(2)}, u32[]{:S(2)}) collective-permute-start(bf16[2,2,2,2,32,2816]{5,4,3,2,1,0:T(8,128)(2,1)} %bitcast.236), channel_id=1, source_target_pairs={{0,2},{1,3},{2,0},{3,1},{4,6},{5,7},{6,4},{7,5},{8,10},{9,11},{10,... | collective-permute-start | bytes 8650760 | tf_op jit(solution)/shard_map/ppermute | solution.py:659
  278.0 16.1 %collective-permute-start.17 = (bf16[2,2,2,2,88,1024]{5,4,3,2,1,0:T(8,128)(2,1)}, bf16[2,2,2,2,88,1024]{5,4,3,2,1,0:T(8,128)(2,1)S(1)}, u32[]{:S(2)}, u32[]{:S(2)}) collective-permute-start(bf16[2,2,2,2,88,1024]{5,4,3,2,1,0:T(8,128)(2,1)} %bitcast.235), channel_id=1, source_target_pairs={{0,2},{1,3},{2,0},{3,1},{4,6},{5,7},{6,4},{7,5},{8,10},{9,11},{10,... | collective-permute-start | bytes 8650760 | tf_op jit(solution)/shard_map/ppermute | solution.py:659
  299.6 57.3 %collective-permute-start.18 = (bf16[2,2,2,32,2816]{4,3,2,1,0:T(8,128)(2,1)}, bf16[2,2,2,32,2816]{4,3,2,1,0:T(8,128)(2,1)}, u32[]{:S(2)}, u32[]{:S(2)}) collective-permute-start(bf16[2,2,2,32,2816]{4,3,2,1,0:T(8,128)(2,1)} %dynamic-slice_bitcast_fusion.2), channel_id=1, source_target_pairs={{0,1},{1,0},{2,3},{3,2},{4,5},{5,4},{6,7},{7,6},{8,9},{9,8},{10,11... | collective-permute-start | bytes 4325384 | tf_op jit(solution)/shard_map/ppermute | solution.py:659
  304.9 52.0 %collective-permute-start.19 = (bf16[2,2,2,32,2816]{4,3,2,1,0:T(8,128)(2,1)}, bf16[2,2,2,32,2816]{4,3,2,1,0:T(8,128)(2,1)}, u32[]{:S(2)}, u32[]{:S(2)}) collective-permute-start(bf16[2,2,2,32,2816]{4,3,2,1,0:T(8,128)(2,1)} %dynamic-slice_bitcast_fusion.1), channel_id=1, source_target_pairs={{0,4},{1,5},{2,6},{3,7},{4,0},{5,1},{6,2},{7,3},{8,12},{9,13},{10,... | collective-permute-start | bytes 4325384 | tf_op jit(solution)/shard_map/ppermute | solution.py:659
  310.5 46.4 %collective-permute-start.20 = (bf16[2,2,2,88,1024]{4,3,2,1,0:T(8,128)(2,1)}, bf16[2,2,2,88,1024]{4,3,2,1,0:T(8,128)(2,1)}, u32[]{:S(2)}, u32[]{:S(2)}) collective-permute-start(bf16[2,2,2,88,1024]{4,3,2,1,0:T(8,128)(2,1)} %dynamic-slice_bitcast_fusion), channel_id=1, source_target_pairs={{0,8},{1,9},{2,10},{3,11},{4,12},{5,13},{6,14},{7,15},{8,0},{9,1},... | collective-permute-start | bytes 4325384 | tf_op jit(solution)/shard_map/ppermute | solution.py:659
  364.7 18.2 %collective-permute-start.21 = (bf16[2,2,32,2816]{3,2,1,0:T(8,128)(2,1)S(1)}, bf16[2,2,32,2816]{3,2,1,0:T(8,128)(2,1)S(1)}, u32[]{:S(2)}, u32[]{:S(2)}) collective-permute-start(bf16[2,2,32,2816]{3,2,1,0:T(8,128)(2,1)S(1)} %dynamic-slice_bitcast_fusion.7), channel_id=1, source_target_pairs={{0,4},{1,5},{2,6},{3,7},{4,0},{5,1},{6,2},{7,3},{8,12},{9,13},{10,... | collective-permute-start | bytes 2162696 | tf_op jit(solution)/shard_map/ppermute | solution.py:659
  367.9 17.8 %collective-permute-start.22 = (bf16[2,2,32,2816]{3,2,1,0:T(8,128)(2,1)S(1)}, bf16[2,2,32,2816]{3,2,1,0:T(8,128)(2,1)S(1)}, u32[]{:S(2)}, u32[]{:S(2)}) collective-permute-start(bf16[2,2,32,2816]{3,2,1,0:T(8,128)(2,1)S(1)} %dynamic-slice_bitcast_fusion.6), channel_id=1, source_target_pairs={{0,8},{1,9},{2,10},{3,11},{4,12},{5,13},{6,14},{7,15},{8,0},{9,1},... | collective-permute-start | bytes 2162696 | tf_op jit(solution)/shard_map/ppermute | solution.py:659
  370.2 17.8 %collective-permute-start.23 = (bf16[2,2,88,1024]{3,2,1,0:T(8,128)(2,1)S(1)}, bf16[2,2,88,1024]{3,2,1,0:T(8,128)(2,1)S(1)}, u32[]{:S(2)}, u32[]{:S(2)}) collective-permute-start(bf16[2,2,88,1024]{3,2,1,0:T(8,128)(2,1)S(1)} %dynamic-slice_bitcast_fusion.5), channel_id=1, source_target_pairs={{0,1},{1,0},{2,3},{3,2},{4,5},{5,4},{6,7},{7,6},{8,9},{9,8},{10,11... | collective-permute-start | bytes 2162696 | tf_op jit(solution)/shard_map/ppermute | solution.py:659
  388.2 17.8 %collective-permute-start.24 = (bf16[2,32,2816]{2,1,0:T(8,128)(2,1)S(1)}, bf16[2,32,2816]{2,1,0:T(8,128)(2,1)S(1)}, u32[]{:S(2)}, u32[]{:S(2)}) collective-permute-start(bf16[2,32,2816]{2,1,0:T(8,128)(2,1)S(1)} %dynamic-slice_bitcast_fusion.13), channel_id=1, source_target_pairs={{0,16},{1,17},{2,18},{3,19},{4,20},{5,21},{6,22},{7,23},{8,24},{9,... | collective-permute-start | bytes 1081352 | tf_op jit(solution)/shard_map/ppermute | solution.py:659
  390.3 15.6 %collective-permute-start.25 = (bf16[2,32,2816]{2,1,0:T(8,128)(2,1)S(1)}, bf16[2,32,2816]{2,1,0:T(8,128)(2,1)S(1)}, u32[]{:S(2)}, u32[]{:S(2)}) collective-permute-start(bf16[2,32,2816]{2,1,0:T(8,128)(2,1)S(1)} %dynamic-slice_bitcast_fusion.12), channel_id=1, source_target_pairs={{0,1},{1,0},{2,3},{3,2},{4,5},{5,4},{6,7},{7,6},{8,9},{9,8},{10,11... | collective-permute-start | bytes 1081352 | tf_op jit(solution)/shard_map/ppermute | solution.py:659
  392.6 13.4 %collective-permute-start.27 = (bf16[2,2,2,2,32,1536]{5,4,1,0,2,3:T(8,128)(2,1)S(1)}, bf16[2,2,2,2,32,1536]{5,4,1,0,2,3:T(8,128)(2,1)S(1)}, u32[]{:S(2)}, u32[]{:S(2)}) collective-permute-start(bf16[2,2,2,2,32,1536]{5,4,1,0,2,3:T(8,128)(2,1)S(1)} %bitcast.215), channel_id=1, source_target_pairs={{0,2},{1,3},{2,0},{3,1},{4,6},{5,7},{6,4},{7,5},{8,10},{9,11},{10,... | collective-permute-start | bytes 4718600 | tf_op jit(solution)/shard_map/ppermute | solution.py:659
  393.4 12.6 %collective-permute-start.28 = (bf16[2,2,2,2,32,1536]{5,4,0,3,1,2:T(8,128)(2,1)S(1)}, bf16[2,2,2,2,32,1536]{5,4,0,3,1,2:T(8,128)(2,1)S(1)}, u32[]{:S(2)}, u32[]{:S(2)}) collective-permute-start(bf16[2,2,2,2,32,1536]{5,4,0,3,1,2:T(8,128)(2,1)S(1)} %bitcast.216), channel_id=1, source_target_pairs={{0,2},{1,3},{2,0},{3,1},{4,6},{5,7},{6,4},{7,5},{8,10},{9,11},{10,... | collective-permute-start | bytes 4718600 | tf_op jit(solution)/shard_map/ppermute | solution.py:659
  394.0 12.0 %collective-permute-start.26 = (bf16[2,88,1024]{2,1,0:T(8,128)(2,1)S(1)}, bf16[2,88,1024]{2,1,0:T(8,128)(2,1)S(1)}, u32[]{:S(2)}, u32[]{:S(2)}) collective-permute-start(bf16[2,88,1024]{2,1,0:T(8,128)(2,1)S(1)} %dynamic-slice_bitcast_fusion.11), channel_id=1, source_target_pairs={{0,4},{1,5},{2,6},{3,7},{4,0},{5,1},{6,2},{7,3},{8,12},{9,13},{10,... | collective-permute-start | bytes 1081352 | tf_op jit(solution)/shard_map/ppermute | solution.py:659
  406.8 25.5 %collective-permute-start.29 = (bf16[32,2816]{1,0:T(8,128)(2,1)}, bf16[32,2816]{1,0:T(8,128)(2,1)}, u32[]{:S(2)}, u32[]{:S(2)}) collective-permute-start(bf16[32,2816]{1,0:T(8,128)(2,1)} %dynamic-slice_bitcast_fusion.19), channel_id=1, source_target_pairs={{0,8},{1,9},{2,10},{3,11},{4,12},{5,13},{6,14},{7,15},{8,0},{9,1},... | collective-permute-start | bytes 540680 | tf_op jit(solution)/shard_map/ppermute | solution.py:659
  407.7 24.6 %collective-permute-start.30 = (bf16[32,2816]{1,0:T(8,128)(2,1)}, bf16[32,2816]{1,0:T(8,128)(2,1)}, u32[]{:S(2)}, u32[]{:S(2)}) collective-permute-start(bf16[32,2816]{1,0:T(8,128)(2,1)} %dynamic-slice_bitcast_fusion.18), channel_id=1, source_target_pairs={{0,16},{1,17},{2,18},{3,19},{4,20},{5,21},{6,22},{7,23},{8,24},{9,... | collective-permute-start | bytes 540680 | tf_op jit(solution)/shard_map/ppermute | solution.py:659
  410.4 21.9 %collective-permute-start.31 = (bf16[88,1024]{1,0:T(8,128)(2,1)}, bf16[88,1024]{1,0:T(8,128)(2,1)}, u32[]{:S(2)}, u32[]{:S(2)}) collective-permute-start(bf16[88,1024]{1,0:T(8,128)(2,1)} %dynamic-slice_bitcast_fusion.17), channel_id=1, source_target_pairs={{0,16},{1,17},{2,18},{3,19},{4,20},{5,21},{6,22},{7,23},{8,24},{9,... | collective-permute-start | bytes 540680 | tf_op jit(solution)/shard_map/ppermute | solution.py:659
  412.9 19.5 %collective-permute-start.32 = (bf16[2,2,2,32,1536]{4,3,1,0,2:T(8,128)(2,1)}, bf16[2,2,2,32,1536]{4,3,1,0,2:T(8,128)(2,1)}, u32[]{:S(2)}, u32[]{:S(2)}) collective-permute-start(bf16[2,2,2,32,1536]{4,3,1,0,2:T(8,128)(2,1)} %dynamic-slice_bitcast_fusion.4), channel_id=1, source_target_pairs={{0,1},{1,0},{2,3},{3,2},{4,5},{5,4},{6,7},{7,6},{8,9},{9,8},{10,11... | collective-permute-start | bytes 2359304 | tf_op jit(solution)/shard_map/ppermute | solution.py:659
  415.3 18.6 %collective-permute-start.33 = (bf16[2,2,2,32,1536]{4,3,0,2,1:T(8,128)(2,1)}, bf16[2,2,2,32,1536]{4,3,0,2,1:T(8,128)(2,1)}, u32[]{:S(2)}, u32[]{:S(2)}) collective-permute-start(bf16[2,2,2,32,1536]{4,3,0,2,1:T(8,128)(2,1)} %dynamic-slice_bitcast_fusion.3), channel_id=1, source_target_pairs={{0,4},{1,5},{2,6},{3,7},{4,0},{5,1},{6,2},{7,3},{8,12},{9,13},{10,... | collective-permute-start | bytes 2359304 | tf_op jit(solution)/shard_map/ppermute | solution.py:659
  432.3 31.2 %collective-permute-start.36 = (bf16[2,2,2,2,32,1024]{5,4,0,2,3,1:T(8,128)(2,1)}, bf16[2,2,2,2,32,1024]{5,4,0,2,3,1:T(8,128)(2,1)}, u32[]{:S(2)}, u32[]{:S(2)}) collective-permute-start(bf16[2,2,2,2,32,1024]{5,4,0,2,3,1:T(8,128)(2,1)} %bitcast.217), channel_id=1, source_target_pairs={{0,2},{1,3},{2,0},{3,1},{4,6},{5,7},{6,4},{7,5},{8,10},{9,11},{10,... | collective-permute-start | bytes 3145736 | tf_op jit(solution)/shard_map/ppermute | solution.py:659
  456.5 10.0 %collective-permute-start.34 = (bf16[2,2,32,1536]{3,2,1,0:T(8,128)(2,1)S(1)}, bf16[2,2,32,1536]{3,2,1,0:T(8,128)(2,1)S(1)}, u32[]{:S(2)}, u32[]{:S(2)}) collective-permute-start(bf16[2,2,32,1536]{3,2,1,0:T(8,128)(2,1)S(1)} %dynamic-slice_bitcast_fusion.10), channel_id=1, source_target_pairs={{0,4},{1,5},{2,6},{3,7},{4,0},{5,1},{6,2},{7,3},{8,12},{9,13},{10,... | collective-permute-start | bytes 1179656 | tf_op jit(solution)/shard_map/ppermute | solution.py:659
  458.2 10.7 %collective-permute-start.35 = (bf16[2,2,32,1536]{3,2,0,1:T(8,128)(2,1)S(1)}, bf16[2,2,32,1536]{3,2,0,1:T(8,128)(2,1)S(1)}, u32[]{:S(2)}, u32[]{:S(2)}) collective-permute-start(bf16[2,2,32,1536]{3,2,0,1:T(8,128)(2,1)S(1)} %dynamic-slice_bitcast_fusion.9), channel_id=1, source_target_pairs={{0,8},{1,9},{2,10},{3,11},{4,12},{5,13},{6,14},{7,15},{8,0},{9,1},... | collective-permute-start | bytes 1179656 | tf_op jit(solution)/shard_map/ppermute | solution.py:659
  469.0 26.6 %collective-permute-start.37 = (bf16[2,32,1536]{2,1,0:T(8,128)(2,1)S(1)}, bf16[2,32,1536]{2,1,0:T(8,128)(2,1)}, u32[]{:S(2)}, u32[]{:S(2)}) collective-permute-start(bf16[2,32,1536]{2,1,0:T(8,128)(2,1)S(1)} %dynamic-slice_bitcast_fusion.16), channel_id=1, source_target_pairs={{0,16},{1,17},{2,18},{3,19},{4,20},{5,21},{6,22},{7,23},{8,24},{9,... | collective-permute-start | bytes 589832 | tf_op jit(solution)/shard_map/ppermute | solution.py:659
  472.2 23.5 %collective-permute-start.38 = (bf16[2,32,1536]{2,1,0:T(8,128)(2,1)S(1)}, bf16[2,32,1536]{2,1,0:T(8,128)(2,1)}, u32[]{:S(2)}, u32[]{:S(2)}) collective-permute-start(bf16[2,32,1536]{2,1,0:T(8,128)(2,1)S(1)} %dynamic-slice_bitcast_fusion.15), channel_id=1, source_target_pairs={{0,1},{1,0},{2,3},{3,2},{4,5},{5,4},{6,7},{7,6},{8,9},{9,8},{10,11... | collective-permute-start | bytes 589832 | tf_op jit(solution)/shard_map/ppermute | solution.py:659
  474.0 21.7 %collective-permute-start.39 = (bf16[2,2,2,32,1024]{4,3,0,1,2:T(8,128)(2,1)S(1)}, bf16[2,2,2,32,1024]{4,3,0,1,2:T(8,128)(2,1)S(1)}, u32[]{:S(2)}, u32[]{:S(2)}) collective-permute-start(bf16[2,2,2,32,1024]{4,3,0,1,2:T(8,128)(2,1)S(1)} %dynamic-slice_bitcast_fusion.8), channel_id=1, source_target_pairs={{0,8},{1,9},{2,10},{3,11},{4,12},{5,13},{6,14},{7,15},{8,0},{9,1},... | collective-permute-start | bytes 1572872 | tf_op jit(solution)/shard_map/ppermute | solution.py:659
  498.9 13.5 %all-to-all-start.1 = ((f32[32,1,112]{2,1,0:T(1,128)}), f32[32,1,112]{2,1,0:T(1,128)S(1)}, u32[]{:S(2)}, u32[]{:S(2)}) async-start(f32[32,1,112]{2,1,0:T(1,128)} %bitcast.65), calls=%async_computation.1 | async-start | bytes 32768 | tf_op jit(solution)/shard_map/all_to_all | solution.py:676
  503.6 8.8 %collective-permute-start.40 = (bf16[32,1536]{1,0:T(8,128)(2,1)S(1)}, bf16[32,1536]{1,0:T(8,128)(2,1)S(1)}, u32[]{:S(2)}, u32[]{:S(2)}) collective-permute-start(bf16[32,1536]{1,0:T(8,128)(2,1)S(1)} %dynamic-slice_bitcast_fusion.22), channel_id=1, source_target_pairs={{0,8},{1,9},{2,10},{3,11},{4,12},{5,13},{6,14},{7,15},{8,0},{9,1},... | collective-permute-start | bytes 294920 | tf_op jit(solution)/shard_map/ppermute | solution.py:659
  506.7 8.9 %collective-permute-start.42 = (bf16[2,2,32,1024]{3,2,0,1:T(8,128)(2,1)S(1)}, bf16[2,2,32,1024]{3,2,0,1:T(8,128)(2,1)S(1)}, u32[]{:S(2)}, u32[]{:S(2)}) collective-permute-start(bf16[2,2,32,1024]{3,2,0,1:T(8,128)(2,1)S(1)} %dynamic-slice_bitcast_fusion.14), channel_id=1, source_target_pairs={{0,1},{1,0},{2,3},{3,2},{4,5},{5,4},{6,7},{7,6},{8,9},{9,8},{10,11... | collective-permute-start | bytes 786440 | tf_op jit(solution)/shard_map/ppermute | solution.py:659
  508.2 7.4 %collective-permute-start.41 = (bf16[32,1536]{1,0:T(8,128)(2,1)S(1)}, bf16[32,1536]{1,0:T(8,128)(2,1)S(1)}, u32[]{:S(2)}, u32[]{:S(2)}) collective-permute-start(bf16[32,1536]{1,0:T(8,128)(2,1)S(1)} %dynamic-slice_bitcast_fusion.21), channel_id=1, source_target_pairs={{0,16},{1,17},{2,18},{3,19},{4,20},{5,21},{6,22},{7,23},{8,24},{9,... | collective-permute-start | bytes 294920 | tf_op jit(solution)/shard_map/ppermute | solution.py:659
  515.7 5.3 collective-permute-start.43
  (45 other events, 453.5 us)
Sparse Core Ops, SparseCore 0:
  10.9 123.3 all-gather.2
  137.2 65.7 all-gather.4

commit v4 on v3

--- a/solution.py
+++ b/solution.py
@@ -924,7 +924,6 @@
     unused_one, norm_one_pull = jax.vjp(norm_apply, rows, gain_one)
     rows_part, grad_gain_one = norm_one_pull(grad_normed_one)
     grad_inputs = (grad_hidden + rows_part).reshape(inputs.shape)
-    grad_gain_one, ix = traffic.step(grad_gain_one, ix)
     parts = []
     pieces = 3
     for piece in range(pieces):

time: 540 us -> 569 us (1.054)
  local copies, waits for them, and re-layouts: 47.8 us -> 56.5 us
  waiting for transfers between devices: 32 us -> 39.7 us
  matrix products: 34.5 us -> 40.2 us
    ppermute x45, waiting for transfers between devices: 28 us -> 35.4 us  [swap(): return lax.ppermute(value, AXES, pairs)]
    unnamed x100 -> x150, local copies, waits for them, and re-layouts: 17.3 us -> 20.8 us
  transfers between devices with their start and end apart: 49 -> 49, of which waited for: 11 -> 11; matrix products, arithmetic and copies ran while one was open for 19% -> 20% of each run, Pallas kernels for 42% -> 40%
where the time goes in v4:
time: 569 us; the launch traced here: 564 us
  Pallas kernels  301 us (53%)
  starting transfers between devices  62.1 us (11%)
  local copies, waits for them, and re-layouts  56.5 us (10%)
  other arithmetic  48.9 us (9%)
  matrix products  40.2 us (7%)
  waiting for transfers between devices  39.7 us (7%)
  between operations  16 us (3%)
    pallas_call x1, Pallas kernels, ffn_call(): pl.pallas_call(functools.partial(ffn_kernel, unit, spots), grid=(count,),...  74.3 us
    pallas_call x3, Pallas kernels, table_call(): pl.pallas_call(functools.partial(table_kernel, begin), grid=(end - begin,...  58.5 us
    ppermute x45, starting transfers between devices, swap(): return lax.ppermute(value, AXES, pairs)  52.1 us
    pallas_call x3, Pallas kernels, bias_call(): pl.pallas_call(functools.partial(bias_kernel, begin), grid=(end - begin,)...  49.6 us
    pallas_call x1, Pallas kernels, attend_call(): pl.pallas_call(attend_kernel, grid=(pairs, slots // tile), in_specs=[rows...  44 us
    pallas_call x1, Pallas kernels, attend_back_call(): pl.pallas_call(attend_back_kernel, grid=(end - begin, slots // tile), in_...  42.9 us
    ppermute x45, waiting for transfers between devices, swap(): return lax.ppermute(value, AXES, pairs)  35.4 us
    convert_element_type x24, other arithmetic, land(): value = value.astype(jnp.bfloat16)  26 us
  transfers between devices with their start and end apart: 49, of which 11 were waited for; matrix products, arithmetic and copies ran while one was open for 20% of the time, Pallas kernels for 40%

profile of v4, /device:TPU:0, one launch (start us, length us, event | category | flops | bytes accessed | tf_op | source)
XLA Modules:
  0.0 564.0 jit_solution(3036766896142098063)
XLA Ops:
  12.4 7.3 %all-to-all-start = ((bf16[32,5,32]{2,1,0:T(8,128)(2,1)}), bf16[32,5,32]{2,1,0:T(8,128)(2,1)S(1)}, u32[]{:S(2)}, u32[]{:S(2)}) async-start(bf16[32,5,32]{2,1,0:T(8,128)(2,1)} %broadcast_in_dim.82), calls=%async_computation | async-start | bytes 131072 | tf_op jit(solution)/shard_map/all_to_all | solution.py:673
  21.6 2.4 collective-permute-start.1
  29.0 2.1 fusion.9
  33.7 5.1 prepare.1
  39.9 2.5 collective-permute-start.3
  46.8 13.9 %index.1 = (bf16[1024,1024]{1,0:T(8,128)(2,1)}, bf16[1024,1024]{1,0:T(8,128)(2,1)}, bf16[2048,1024]{1,0:T(8,128)(2,1)}, bf16[2048,1024]{1,0:T(8,128)(2,1)}) custom-call(s32[1]{0:T(128)S(6)} %copy.103.len_ref, s32[2,1024]{1,0:T(2,128)} %copy.63.box_ref, s32[1024,2]{1,0:T(8,128)} %bitcast.214), custom_call_target="tpu_custom_call" | custom-call | flops 1000000000 | bytes 4000000 | tf_op jit(solution)/shard_map/index/pallas_call | solution.py:147
  63.1 14.0 %bias.3.rest_0_ = f32[16,1024,1024]{2,1,0:T(8,128)} custom-call(bf16[2048,1024]{1,0:T(8,128)(2,1)} %get-tuple-element.118.ix_ref, bf16[2048,1024]{1,0:T(8,128)(2,1)} %get-tuple-element.119.iy_ref, bf16[128,512]{1,0:T(8,128)(2,1)} %get-tuple-element.134.lhs_ref, f32[16,128,640]{2,1,0:T(8,128)} %get-tuple-element.125.skew_ref), custom_call_target="tpu_custom_call" | custom-call | flops 8499999744 | bytes 18000000 | tf_op jit(solution)/shard_map/bias/pallas_call | solution.py:277
  86.2 21.7 %bias.4.rest_0_ = f32[16,1024,1024]{2,1,0:T(8,128)} custom-call(bf16[2048,1024]{1,0:T(8,128)(2,1)} %get-tuple-element.118.ix_ref, bf16[2048,1024]{1,0:T(8,128)(2,1)} %get-tuple-element.119.iy_ref, bf16[128,512]{1,0:T(8,128)(2,1)} %get-tuple-element.134.lhs_ref, f32[16,128,640]{2,1,0:T(8,128)} %get-tuple-element.125.skew_ref, ...), custom_call_target="tpu_custom_call", output_to_operand_aliasing={{}: (4, {})} | custom-call | flops 16999999488 | bytes 36000000 | tf_op jit(solution)/shard_map/bias/pallas_call | solution.py:277
  110.1 3.7 collective-permute-done.11
  114.6 1.9 constant_dynamic-update-slice_fusion.5.refs_2_
  117.0 2.0 constant_dynamic-update-slice_fusion.10.refs_4_
  119.0 1.9 fusion.5.x_ref
  120.9 13.9 %bias.5.bias_ref = f32[16,1024,1024]{2,1,0:T(8,128)} custom-call(bf16[2048,1024]{1,0:T(8,128)(2,1)} %get-tuple-element.118.ix_ref, bf16[2048,1024]{1,0:T(8,128)(2,1)} %get-tuple-element.119.iy_ref, bf16[128,512]{1,0:T(8,128)(2,1)} %get-tuple-element.134.lhs_ref, f32[16,128,640]{2,1,0:T(8,128)} %get-tuple-element.125.skew_ref, ...), custom_call_target="tpu_custom_call", output_to_operand_aliasing={{}: (4, {})} | custom-call | flops 8499999744 | bytes 18000000 | tf_op jit(solution)/shard_map/bias/pallas_call | solution.py:277
  135.7 12.4 %project.1 = (bf16[1024,1024]{1,0:T(8,128)(2,1)}, bf16[1024,1024]{1,0:T(8,128)(2,1)}, bf16[1024,1024]{1,0:T(8,128)(2,1)}, bf16[1024,1024]{1,0:T(8,128)(2,1)}, bf...) custom-call(s32[1]{0:T(128)} %bitcast.8.me_ref, bf16[1024,1024]{1,0:T(8,128)(2,1)} %fusion.5.x_ref, ...), custom_call_target="tpu_custom_call" | custom-call | flops 6442450944 | bytes 20000000 | tf_op jit(solution)/shard_map/project/pallas_call | solution.py:735
  148.2 44.0 %attend.1 = (bf16[16,1024,1024]{2,1,0:T(8,128)(2,1)}, bf16[1024,1024]{1,0:T(8,128)(2,1)}) custom-call(bf16[1024,1024]{1,0:T(8,128)(2,1)} %get-tuple-element.143.q_ref, bf16[1024,1024]{1,0:T(8,128)(2,1)} %get-tuple-element.144.k_ref, bf16[1024,1024]{1,0:T(8,128)(2,1)} %get-tuple-element.145.v_ref, f32[16,1024,1024]{2,1,0:T(8,128)} %bias.5.bias_ref), custom_call_target="tpu_custom_call" | custom-call | flops 33999998976 | bytes 100000000 | tf_op jit(solution)/shard_map/attend/pallas_call | solution.py:322
  192.2 6.6 %convert_add_fusion.hidden_ref = f32[1024,1024]{1,0:T(8,128)} fusion(bf16[1,1024,1024]{2,1,0:T(8,128)(2,1)S(1)} %copy-done, bf16[1024,1024]{1,0:T(8,128)(2,1)} %get-tuple-element.147, bf16[1024,6656]{1,0:T(8,128)(2,1)} %all-gather.3.cloned.1.call-done.gate_ref.up_ref), kind=kOutput, calls=%fused_computation.2 | convolution fusion | flops 2149580800 | bytes 10485760 | tf_op jit(solution)/shard_map/dot_general | solution.py:42
  198.7 4.2 all-gather.5.cloned.1.call-done.down_ref
  202.9 74.3 %ffn.1 = (bf16[1024,1024]{1,0:T(8,128)(2,1)}, f32[1024,1024]{1,0:T(8,128)}, bf16[1024,1024]{1,0:T(8,128)(2,1)}, f32[1,1024]{1,0:T(1,128)}, bf16[512,2816]{1,0:T(...) custom-call(s32[1]{0:T(128)} %bitcast.core_ref, ...), custom_call_target="tpu_custom_call" | custom-call | flops 53150220288 | bytes 50000000 | tf_op jit(solution)/shard_map/ffn/pallas_call | solution.py:607
  282.4 6.1 %convolution_convert_fusion.3 = bf16[1024,1024]{1,0:T(8,128)(2,1)} fusion(bf16[1024,1024]{1,0:T(8,128)(2,1)} %get-tuple-element.147, bf16[1024,1024]{1,0:T(8,128)(2,1)} %get-tuple-element.150), kind=kOutput, calls=%fused_computation.38 | convolution fusion | flops 2148532224 | bytes 6291456 | tf_op jit(solution)/shard_map/dot_general | solution.py:46
  288.5 5.5 convolution_convert_fusion.4.grad_ref
  295.6 2.6 fusion.2
  300.7 2.8 fusion.1
  310.3 2.0 collective-permute-start.20
  312.3 42.9 %attend_back.1 = (bf16[16,1024,1024]{2,1,0:T(8,128)(2,1)}, bf16[1024,1024]{1,0:T(8,128)(2,1)}, bf16[1024,1024]{1,0:T(8,128)(2,1)}, bf16[1024,1024]{1,0:T(8,128)(2,1)}) custom-call(bf16[1024,1024]{1,0:T(8,128)(2,1)} %get-tuple-element.143.q_ref, bf16[1024,1024]{1,0:T(8,128)(2,1)} %get-tuple-element.144.k_ref, bf16[1024,1024]{1,0:T(8,128)(2,1)} %get-tuple-element.145.v_ref, ...), custom_call_target="tpu_custom_call" | custom-call | flops 33999998976 | bytes 72000000 | tf_op jit(solution)/shard_map/attend_back/pallas_call | solution.py:394
  355.3 3.1 fusion.39
  358.4 3.7 convolution_convert_fusion.2
  362.2 2.4 fusion.42
  372.6 2.1 fusion.13
  376.5 2.4 fusion.43
  378.9 4.4 add_add_fusion.1
  383.4 16.0 %table_back.3 = f32[96,256]{1,0:T(8,128)} custom-call(bf16[16,1024,1024]{2,1,0:T(8,128)(2,1)} %get-tuple-element.178.ds_ref, bf16[1024,1024]{1,0:T(8,128)(2,1)} %get-tuple-element.193.ix_ref, bf16[1024,1024]{1,0:T(8,128)(2,1)} %get-tuple-element.179.iy_ref, bf16[8,512,640]{2,1,0:T(8,128)(2,1)} %constant.214.near_ref), custom_call_target="tpu_custom_call" | custom-call | flops 10000000000 | bytes 10000000 | tf_op jit(solution)/shard_map/table_back/pallas_call | solution.py:477
  399.4 5.5 convolution_convert_fusion.1
  404.9 3.7 convolution_convert_fusion
  408.7 1.9 fusion.6
  413.1 2.4 collective-permute-start.24
  426.3 2.6 fusion.8
  428.9 2.5 collective-permute-done.24
  444.4 21.4 %table_back.4 = f32[96,256]{1,0:T(8,128)} custom-call(bf16[16,1024,1024]{2,1,0:T(8,128)(2,1)} %get-tuple-element.178.ds_ref, bf16[1024,1024]{1,0:T(8,128)(2,1)} %get-tuple-element.193.ix_ref, bf16[1024,1024]{1,0:T(8,128)(2,1)} %get-tuple-element.179.iy_ref, bf16[8,512,640]{2,1,0:T(8,128)(2,1)} %constant.214.near_ref), custom_call_target="tpu_custom_call" | custom-call | flops 15000000512 | bytes 15000000 | tf_op jit(solution)/shard_map/table_back/pallas_call | solution.py:477
  466.7 21.1 %table_back.5 = f32[96,256]{1,0:T(8,128)} custom-call(bf16[16,1024,1024]{2,1,0:T(8,128)(2,1)} %get-tuple-element.178.ds_ref, bf16[1024,1024]{1,0:T(8,128)(2,1)} %get-tuple-element.193.ix_ref, bf16[1024,1024]{1,0:T(8,128)(2,1)} %get-tuple-element.179.iy_ref, bf16[8,512,640]{2,1,0:T(8,128)(2,1)} %constant.214.near_ref), custom_call_target="tpu_custom_call" | custom-call | flops 15000000512 | bytes 15000000 | tf_op jit(solution)/shard_map/table_back/pallas_call | solution.py:477
  494.6 6.4 %collective-permute-done.34 = bf16[2,2,32,1536]{3,2,1,0:T(8,128)(2,1)S(1)} collective-permute-done((bf16[2,2,32,1536]{3,2,1,0:T(8,128)(2,1)S(1)}, bf16[2,2,32,1536]{3,2,1,0:T(8,128)(2,1)S(1)}, u32[]{:S(2)}, u32[]{:S(2)}) %collective-permute-start.34) | collective-permute-done | bytes 393248 | tf_op jit(solution)/shard_map/ppermute | solution.py:659
  501.0 2.2 collective-permute-done.35
  505.5 2.6 all-to-all-start.1
  510.1 2.7 collective-permute-start.37
  522.7 11.0 %collective-permute-done.39 = bf16[2,2,2,32,1024]{4,3,0,1,2:T(8,128)(2,1)S(1)} collective-permute-done((bf16[2,2,2,32,1024]{4,3,0,1,2:T(8,128)(2,1)S(1)}, bf16[2,2,2,32,1024]{4,3,0,1,2:T(8,128)(2,1)S(1)}, u32[]{:S(2)}, u32[]{:S(2)}) %collective-permute-start.39) | collective-permute-done | bytes 524320 | tf_op jit(solution)/shard_map/ppermute | solution.py:659
  537.4 3.0 collective-permute-start.41
  542.1 2.5 collective-permute-done.41
  547.8 2.0 collective-permute-done.43
  549.9 2.8 collective-permute-start.44
  (355 shorter events, 121.9 us)
Async XLA Ops:
  7.2 185.0 %all-gather.3.cloned.1.call-start = ((), (), s32[]{:S(2)}) async-start(), calls=%async_computation.2 | async-start | bytes 14057472 | tf_op jit(solution)/shard_map/all_gather | solution.py:861
  12.4 19.3 %all-to-all-start = ((bf16[32,5,32]{2,1,0:T(8,128)(2,1)}), bf16[32,5,32]{2,1,0:T(8,128)(2,1)S(1)}, u32[]{:S(2)}, u32[]{:S(2)}) async-start(bf16[32,5,32]{2,1,0:T(8,128)(2,1)} %broadcast_in_dim.82), calls=%async_computation | async-start | bytes 131072 | tf_op jit(solution)/shard_map/all_to_all | solution.py:673
  19.7 183.2 %all-gather.5.cloned.1.call-start = ((), (), s32[]{:S(2)}) async-start(), calls=%async_computation.3 | async-start | bytes 5947392 | tf_op jit(solution)/shard_map/all_gather | solution.py:864
  19.8 19.0 %collective-permute-start = (bf16[1,32,1024]{2,1,0:T(8,128)(2,1)}, bf16[1,32,1024]{2,1,0:T(8,128)(2,1)S(1)}, u32[]{:S(2)}, u32[]{:S(2)}) collective-permute-start(bf16[1,32,1024]{2,1,0:T(8,128)(2,1)} %bitcast.218), channel_id=1, source_target_pairs={{0,8},{1,9},{2,10},{3,11},{4,12},{5,13},{6,14},{7,15},{8,0},{9,1},... | collective-permute-start | bytes 196616 | tf_op jit(solution)/shard_map/ppermute | solution.py:659
  21.6 17.2 %collective-permute-start.1 = (bf16[1,32,1024]{2,1,0:T(8,128)(2,1)}, bf16[1,32,1024]{2,1,0:T(8,128)(2,1)S(1)}, u32[]{:S(2)}, u32[]{:S(2)}) collective-permute-start(bf16[1,32,1024]{2,1,0:T(8,128)(2,1)} %bitcast.222), channel_id=1, source_target_pairs={{0,16},{1,17},{2,18},{3,19},{4,20},{5,21},{6,22},{7,23},{8,24},{9,... | collective-permute-start | bytes 196616 | tf_op jit(solution)/shard_map/ppermute | solution.py:659
  24.0 14.8 %collective-permute-start.2 = (bf16[1,32,1024]{2,1,0:T(8,128)(2,1)}, bf16[1,32,1024]{2,1,0:T(8,128)(2,1)S(1)}, u32[]{:S(2)}, u32[]{:S(2)}) collective-permute-start(bf16[1,32,1024]{2,1,0:T(8,128)(2,1)} %bitcast.226), channel_id=1, source_target_pairs={{0,16},{1,17},{2,18},{3,19},{4,20},{5,21},{6,22},{7,23},{8,24},{9,... | collective-permute-start | bytes 196616 | tf_op jit(solution)/shard_map/ppermute | solution.py:659
  39.9 21.4 %collective-permute-start.3 = (bf16[2,32,1024]{2,1,0:T(8,128)(2,1)S(1)}, bf16[2,32,1024]{2,1,0:T(8,128)(2,1)S(1)}, u32[]{:S(2)}, u32[]{:S(2)}) collective-permute-start(bf16[2,32,1024]{2,1,0:T(8,128)(2,1)S(1)} %pad_maximum_fusion.9), channel_id=1, source_target_pairs={{0,16},{1,17},{2,18},{3,19},{4,20},{5,21},{6,22},{7,23},{8,24},{9,... | collective-permute-start | bytes 393224 | tf_op jit(solution)/shard_map/ppermute | solution.py:659
  42.4 18.9 %collective-permute-start.4 = (bf16[2,32,1024]{2,1,0:T(8,128)(2,1)S(1)}, bf16[2,32,1024]{2,1,0:T(8,128)(2,1)S(1)}, u32[]{:S(2)}, u32[]{:S(2)}) collective-permute-start(bf16[2,32,1024]{2,1,0:T(8,128)(2,1)S(1)} %pad_maximum_fusion.10), channel_id=1, source_target_pairs={{0,1},{1,0},{2,3},{3,2},{4,5},{5,4},{6,7},{7,6},{8,9},{9,8},{10,11... | collective-permute-start | bytes 393224 | tf_op jit(solution)/shard_map/ppermute | solution.py:659
  43.9 17.3 %collective-permute-start.5 = (bf16[2,32,1024]{2,1,0:T(8,128)(2,1)S(1)}, bf16[2,32,1024]{2,1,0:T(8,128)(2,1)S(1)}, u32[]{:S(2)}, u32[]{:S(2)}) collective-permute-start(bf16[2,32,1024]{2,1,0:T(8,128)(2,1)S(1)} %pad_maximum_fusion.11), channel_id=1, source_target_pairs={{0,4},{1,5},{2,6},{3,7},{4,0},{5,1},{6,2},{7,3},{8,12},{9,13},{10,... | collective-permute-start | bytes 393224 | tf_op jit(solution)/shard_map/ppermute | solution.py:659
  61.3 17.8 %collective-permute-start.6 = (bf16[4,32,1024]{2,1,0:T(8,128)(2,1)S(1)}, bf16[4,32,1024]{2,1,0:T(8,128)(2,1)S(1)}, u32[]{:S(2)}, u32[]{:S(2)}) collective-permute-start(bf16[4,32,1024]{2,1,0:T(8,128)(2,1)S(1)} %pad_maximum_fusion.6), channel_id=1, source_target_pairs={{0,4},{1,5},{2,6},{3,7},{4,0},{5,1},{6,2},{7,3},{8,12},{9,13},{10,... | collective-permute-start | bytes 786440 | tf_op jit(solution)/shard_map/ppermute | solution.py:659
  61.9 17.2 %collective-permute-start.7 = (bf16[4,32,1024]{2,1,0:T(8,128)(2,1)S(1)}, bf16[4,32,1024]{2,1,0:T(8,128)(2,1)S(1)}, u32[]{:S(2)}, u32[]{:S(2)}) collective-permute-start(bf16[4,32,1024]{2,1,0:T(8,128)(2,1)S(1)} %pad_maximum_fusion.7), channel_id=1, source_target_pairs={{0,8},{1,9},{2,10},{3,11},{4,12},{5,13},{6,14},{7,15},{8,0},{9,1},... | collective-permute-start | bytes 786440 | tf_op jit(solution)/shard_map/ppermute | solution.py:659
  62.5 16.6 %collective-permute-start.8 = (bf16[4,32,1024]{2,1,0:T(8,128)(2,1)S(1)}, bf16[4,32,1024]{2,1,0:T(8,128)(2,1)S(1)}, u32[]{:S(2)}, u32[]{:S(2)}) collective-permute-start(bf16[4,32,1024]{2,1,0:T(8,128)(2,1)S(1)} %pad_maximum_fusion.8), channel_id=1, source_target_pairs={{0,1},{1,0},{2,3},{3,2},{4,5},{5,4},{6,7},{7,6},{8,9},{9,8},{10,11... | collective-permute-start | bytes 786440 | tf_op jit(solution)/shard_map/ppermute | solution.py:659
  80.0 30.1 %collective-permute-start.9 = (bf16[8,32,1024]{2,1,0:T(8,128)(2,1)}, bf16[8,32,1024]{2,1,0:T(8,128)(2,1)S(1)}, u32[]{:S(2)}, u32[]{:S(2)}) collective-permute-start(bf16[8,32,1024]{2,1,0:T(8,128)(2,1)} %pad_maximum_fusion.2), channel_id=1, source_target_pairs={{0,1},{1,0},{2,3},{3,2},{4,5},{5,4},{6,7},{7,6},{8,9},{9,8},{10,11... | collective-permute-start | bytes 1572872 | tf_op jit(solution)/shard_map/ppermute | solution.py:659
  82.3 27.8 %collective-permute-start.10 = (bf16[8,32,1024]{2,1,0:T(8,128)(2,1)}, bf16[8,32,1024]{2,1,0:T(8,128)(2,1)}, u32[]{:S(2)}, u32[]{:S(2)}) collective-permute-start(bf16[8,32,1024]{2,1,0:T(8,128)(2,1)} %pad_maximum_fusion.3), channel_id=1, source_target_pairs={{0,4},{1,5},{2,6},{3,7},{4,0},{5,1},{6,2},{7,3},{8,12},{9,13},{10,... | collective-permute-start | bytes 1572872 | tf_op jit(solution)/shard_map/ppermute | solution.py:659
  84.6 29.1 %collective-permute-start.11 = (bf16[8,32,1024]{2,1,0:T(8,128)(2,1)}, bf16[8,32,1024]{2,1,0:T(8,128)(2,1)}, u32[]{:S(2)}, u32[]{:S(2)}) collective-permute-start(bf16[8,32,1024]{2,1,0:T(8,128)(2,1)} %pad_maximum_fusion.4), channel_id=1, source_target_pairs={{0,8},{1,9},{2,10},{3,11},{4,12},{5,13},{6,14},{7,15},{8,0},{9,1},... | collective-permute-start | bytes 1572872 | tf_op jit(solution)/shard_map/ppermute | solution.py:659
  114.6 20.2 %collective-permute-start.12 = (bf16[16,32,1024]{2,1,0:T(8,128)(2,1)}, bf16[16,32,1024]{2,1,0:T(8,128)(2,1)S(1)}, u32[]{:S(2)}, u32[]{:S(2)}) collective-permute-start(bf16[16,32,1024]{2,1,0:T(8,128)(2,1)} %constant_dynamic-update-slice_fusion.refs_0_), channel_id=1, source_target_pairs={{0,2},{1,3},{2,0},{3,1},{4,6},{5,7},{6,4},{7,5},{8,10},{9,11},{10,... | collective-permute-start | bytes 3145736 | tf_op jit(solution)/shard_map/ppermute | solution.py:659
  116.5 18.3 %collective-permute-start.13 = (bf16[16,32,1024]{2,1,0:T(8,128)(2,1)}, bf16[16,32,1024]{2,1,0:T(8,128)(2,1)}, u32[]{:S(2)}, u32[]{:S(2)}) collective-permute-start(bf16[16,32,1024]{2,1,0:T(8,128)(2,1)} %constant_dynamic-update-slice_fusion.5.refs_2_), channel_id=1, source_target_pairs={{0,2},{1,3},{2,0},{3,1},{4,6},{5,7},{6,4},{7,5},{8,10},{9,11},{10,... | collective-permute-start | bytes 3145736 | tf_op jit(solution)/shard_map/ppermute | solution.py:659
  119.0 15.8 %collective-permute-start.14 = (bf16[16,32,1024]{2,1,0:T(8,128)(2,1)}, bf16[16,32,1024]{2,1,0:T(8,128)(2,1)}, u32[]{:S(2)}, u32[]{:S(2)}) collective-permute-start(bf16[16,32,1024]{2,1,0:T(8,128)(2,1)} %constant_dynamic-update-slice_fusion.10.refs_4_), channel_id=1, source_target_pairs={{0,2},{1,3},{2,0},{3,1},{4,6},{5,7},{6,4},{7,5},{8,10},{9,11},{10,... | collective-permute-start | bytes 3145736 | tf_op jit(solution)/shard_map/ppermute | solution.py:659
  277.2 16.7 %collective-permute-start.15 = (bf16[2,2,2,2,32,2816]{5,4,3,2,1,0:T(8,128)(2,1)}, bf16[2,2,2,2,32,2816]{5,4,3,2,1,0:T(8,128)(2,1)}, u32[]{:S(2)}, u32[]{:S(2)}) collective-permute-start(bf16[2,2,2,2,32,2816]{5,4,3,2,1,0:T(8,128)(2,1)} %bitcast.237), channel_id=1, source_target_pairs={{0,2},{1,3},{2,0},{3,1},{4,6},{5,7},{6,4},{7,5},{8,10},{9,11},{10,... | collective-permute-start | bytes 8650760 | tf_op jit(solution)/shard_map/ppermute | solution.py:659
  277.6 16.4 %collective-permute-start.16 = (bf16[2,2,2,2,32,2816]{5,4,3,2,1,0:T(8,128)(2,1)}, bf16[2,2,2,2,32,2816]{5,4,3,2,1,0:T(8,128)(2,1)}, u32[]{:S(2)}, u32[]{:S(2)}) collective-permute-start(bf16[2,2,2,2,32,2816]{5,4,3,2,1,0:T(8,128)(2,1)} %bitcast.236), channel_id=1, source_target_pairs={{0,2},{1,3},{2,0},{3,1},{4,6},{5,7},{6,4},{7,5},{8,10},{9,11},{10,... | collective-permute-start | bytes 8650760 | tf_op jit(solution)/shard_map/ppermute | solution.py:659
  277.8 16.2 %collective-permute-start.17 = (bf16[2,2,2,2,88,1024]{5,4,3,2,1,0:T(8,128)(2,1)}, bf16[2,2,2,2,88,1024]{5,4,3,2,1,0:T(8,128)(2,1)S(1)}, u32[]{:S(2)}, u32[]{:S(2)}) collective-permute-start(bf16[2,2,2,2,88,1024]{5,4,3,2,1,0:T(8,128)(2,1)} %bitcast.235), channel_id=1, source_target_pairs={{0,2},{1,3},{2,0},{3,1},{4,6},{5,7},{6,4},{7,5},{8,10},{9,11},{10,... | collective-permute-start | bytes 8650760 | tf_op jit(solution)/shard_map/ppermute | solution.py:659
  299.4 59.0 %collective-permute-start.18 = (bf16[2,2,2,32,2816]{4,3,2,1,0:T(8,128)(2,1)}, bf16[2,2,2,32,2816]{4,3,2,1,0:T(8,128)(2,1)}, u32[]{:S(2)}, u32[]{:S(2)}) collective-permute-start(bf16[2,2,2,32,2816]{4,3,2,1,0:T(8,128)(2,1)} %dynamic-slice_bitcast_fusion.2), channel_id=1, source_target_pairs={{0,1},{1,0},{2,3},{3,2},{4,5},{5,4},{6,7},{7,6},{8,9},{9,8},{10,11... | collective-permute-start | bytes 4325384 | tf_op jit(solution)/shard_map/ppermute | solution.py:659
  304.7 53.8 %collective-permute-start.19 = (bf16[2,2,2,32,2816]{4,3,2,1,0:T(8,128)(2,1)}, bf16[2,2,2,32,2816]{4,3,2,1,0:T(8,128)(2,1)}, u32[]{:S(2)}, u32[]{:S(2)}) collective-permute-start(bf16[2,2,2,32,2816]{4,3,2,1,0:T(8,128)(2,1)} %dynamic-slice_bitcast_fusion.1), channel_id=1, source_target_pairs={{0,4},{1,5},{2,6},{3,7},{4,0},{5,1},{6,2},{7,3},{8,12},{9,13},{10,... | collective-permute-start | bytes 4325384 | tf_op jit(solution)/shard_map/ppermute | solution.py:659
  310.3 48.1 %collective-permute-start.20 = (bf16[2,2,2,88,1024]{4,3,2,1,0:T(8,128)(2,1)}, bf16[2,2,2,88,1024]{4,3,2,1,0:T(8,128)(2,1)}, u32[]{:S(2)}, u32[]{:S(2)}) collective-permute-start(bf16[2,2,2,88,1024]{4,3,2,1,0:T(8,128)(2,1)} %dynamic-slice_bitcast_fusion), channel_id=1, source_target_pairs={{0,8},{1,9},{2,10},{3,11},{4,12},{5,13},{6,14},{7,15},{8,0},{9,1},... | collective-permute-start | bytes 4325384 | tf_op jit(solution)/shard_map/ppermute | solution.py:659
  368.5 40.2 %collective-permute-start.21 = (bf16[2,2,32,2816]{3,2,1,0:T(8,128)(2,1)}, bf16[2,2,32,2816]{3,2,1,0:T(8,128)(2,1)}, u32[]{:S(2)}, u32[]{:S(2)}) collective-permute-start(bf16[2,2,32,2816]{3,2,1,0:T(8,128)(2,1)} %dynamic-slice_bitcast_fusion.7), channel_id=1, source_target_pairs={{0,4},{1,5},{2,6},{3,7},{4,0},{5,1},{6,2},{7,3},{8,12},{9,13},{10,... | collective-permute-start | bytes 2162696 | tf_op jit(solution)/shard_map/ppermute | solution.py:659
  372.5 36.1 %collective-permute-start.22 = (bf16[2,2,32,2816]{3,2,1,0:T(8,128)(2,1)}, bf16[2,2,32,2816]{3,2,1,0:T(8,128)(2,1)}, u32[]{:S(2)}, u32[]{:S(2)}) collective-permute-start(bf16[2,2,32,2816]{3,2,1,0:T(8,128)(2,1)} %dynamic-slice_bitcast_fusion.6), channel_id=1, source_target_pairs={{0,8},{1,9},{2,10},{3,11},{4,12},{5,13},{6,14},{7,15},{8,0},{9,1},... | collective-permute-start | bytes 2162696 | tf_op jit(solution)/shard_map/ppermute | solution.py:659
  375.6 33.1 %collective-permute-start.23 = (bf16[2,2,88,1024]{3,2,1,0:T(8,128)(2,1)}, bf16[2,2,88,1024]{3,2,1,0:T(8,128)(2,1)}, u32[]{:S(2)}, u32[]{:S(2)}) collective-permute-start(bf16[2,2,88,1024]{3,2,1,0:T(8,128)(2,1)} %dynamic-slice_bitcast_fusion.5), channel_id=1, source_target_pairs={{0,1},{1,0},{2,3},{3,2},{4,5},{5,4},{6,7},{7,6},{8,9},{9,8},{10,11... | collective-permute-start | bytes 2162696 | tf_op jit(solution)/shard_map/ppermute | solution.py:659
  413.1 18.3 %collective-permute-start.24 = (bf16[2,32,2816]{2,1,0:T(8,128)(2,1)S(1)}, bf16[2,32,2816]{2,1,0:T(8,128)(2,1)S(1)}, u32[]{:S(2)}, u32[]{:S(2)}) collective-permute-start(bf16[2,32,2816]{2,1,0:T(8,128)(2,1)S(1)} %dynamic-slice_bitcast_fusion.13), channel_id=1, source_target_pairs={{0,16},{1,17},{2,18},{3,19},{4,20},{5,21},{6,22},{7,23},{8,24},{9,... | collective-permute-start | bytes 1081352 | tf_op jit(solution)/shard_map/ppermute | solution.py:659
  417.4 15.6 %collective-permute-start.27 = (bf16[2,2,2,2,32,1536]{5,4,1,0,2,3:T(8,128)(2,1)S(1)}, bf16[2,2,2,2,32,1536]{5,4,1,0,2,3:T(8,128)(2,1)S(1)}, u32[]{:S(2)}, u32[]{:S(2)}) collective-permute-start(bf16[2,2,2,2,32,1536]{5,4,1,0,2,3:T(8,128)(2,1)S(1)} %bitcast.215), channel_id=1, source_target_pairs={{0,2},{1,3},{2,0},{3,1},{4,6},{5,7},{6,4},{7,5},{8,10},{9,11},{10,... | collective-permute-start | bytes 4718600 | tf_op jit(solution)/shard_map/ppermute | solution.py:659
  419.8 13.3 %collective-permute-start.28 = (bf16[2,2,2,2,32,1536]{5,4,0,3,1,2:T(8,128)(2,1)S(1)}, bf16[2,2,2,2,32,1536]{5,4,0,3,1,2:T(8,128)(2,1)S(1)}, u32[]{:S(2)}, u32[]{:S(2)}) collective-permute-start(bf16[2,2,2,2,32,1536]{5,4,0,3,1,2:T(8,128)(2,1)S(1)} %bitcast.216), channel_id=1, source_target_pairs={{0,2},{1,3},{2,0},{3,1},{4,6},{5,7},{6,4},{7,5},{8,10},{9,11},{10,... | collective-permute-start | bytes 4718600 | tf_op jit(solution)/shard_map/ppermute | solution.py:659
  419.9 11.5 %collective-permute-start.25 = (bf16[2,32,2816]{2,1,0:T(8,128)(2,1)S(1)}, bf16[2,32,2816]{2,1,0:T(8,128)(2,1)S(1)}, u32[]{:S(2)}, u32[]{:S(2)}) collective-permute-start(bf16[2,32,2816]{2,1,0:T(8,128)(2,1)S(1)} %dynamic-slice_bitcast_fusion.12), channel_id=1, source_target_pairs={{0,1},{1,0},{2,3},{3,2},{4,5},{5,4},{6,7},{7,6},{8,9},{9,8},{10,11... | collective-permute-start | bytes 1081352 | tf_op jit(solution)/shard_map/ppermute | solution.py:659
  422.4 10.6 %collective-permute-start.26 = (bf16[2,88,1024]{2,1,0:T(8,128)(2,1)S(1)}, bf16[2,88,1024]{2,1,0:T(8,128)(2,1)S(1)}, u32[]{:S(2)}, u32[]{:S(2)}) collective-permute-start(bf16[2,88,1024]{2,1,0:T(8,128)(2,1)S(1)} %dynamic-slice_bitcast_fusion.11), channel_id=1, source_target_pairs={{0,4},{1,5},{2,6},{3,7},{4,0},{5,1},{6,2},{7,3},{8,12},{9,13},{10,... | collective-permute-start | bytes 1081352 | tf_op jit(solution)/shard_map/ppermute | solution.py:659
  433.9 31.9 %collective-permute-start.29 = (bf16[32,2816]{1,0:T(8,128)(2,1)S(1)}, bf16[32,2816]{1,0:T(8,128)(2,1)}, u32[]{:S(2)}, u32[]{:S(2)}) collective-permute-start(bf16[32,2816]{1,0:T(8,128)(2,1)S(1)} %dynamic-slice_bitcast_fusion.19), channel_id=1, source_target_pairs={{0,8},{1,9},{2,10},{3,11},{4,12},{5,13},{6,14},{7,15},{8,0},{9,1},... | collective-permute-start | bytes 540680 | tf_op jit(solution)/shard_map/ppermute | solution.py:659
  435.9 29.9 %collective-permute-start.30 = (bf16[32,2816]{1,0:T(8,128)(2,1)}, bf16[32,2816]{1,0:T(8,128)(2,1)}, u32[]{:S(2)}, u32[]{:S(2)}) collective-permute-start(bf16[32,2816]{1,0:T(8,128)(2,1)} %dynamic-slice_bitcast_fusion.18), channel_id=1, source_target_pairs={{0,16},{1,17},{2,18},{3,19},{4,20},{5,21},{6,22},{7,23},{8,24},{9,... | collective-permute-start | bytes 540680 | tf_op jit(solution)/shard_map/ppermute | solution.py:659
  438.3 27.5 %collective-permute-start.31 = (bf16[88,1024]{1,0:T(8,128)(2,1)}, bf16[88,1024]{1,0:T(8,128)(2,1)}, u32[]{:S(2)}, u32[]{:S(2)}) collective-permute-start(bf16[88,1024]{1,0:T(8,128)(2,1)} %dynamic-slice_bitcast_fusion.17), channel_id=1, source_target_pairs={{0,16},{1,17},{2,18},{3,19},{4,20},{5,21},{6,22},{7,23},{8,24},{9,... | collective-permute-start | bytes 540680 | tf_op jit(solution)/shard_map/ppermute | solution.py:659
  441.2 24.6 %collective-permute-start.32 = (bf16[2,2,2,32,1536]{4,3,1,0,2:T(8,128)(2,1)}, bf16[2,2,2,32,1536]{4,3,1,0,2:T(8,128)(2,1)}, u32[]{:S(2)}, u32[]{:S(2)}) collective-permute-start(bf16[2,2,2,32,1536]{4,3,1,0,2:T(8,128)(2,1)} %dynamic-slice_bitcast_fusion.4), channel_id=1, source_target_pairs={{0,1},{1,0},{2,3},{3,2},{4,5},{5,4},{6,7},{7,6},{8,9},{9,8},{10,11... | collective-permute-start | bytes 2359304 | tf_op jit(solution)/shard_map/ppermute | solution.py:659
  443.6 22.2 %collective-permute-start.33 = (bf16[2,2,2,32,1536]{4,3,0,2,1:T(8,128)(2,1)}, bf16[2,2,2,32,1536]{4,3,0,2,1:T(8,128)(2,1)S(1)}, u32[]{:S(2)}, u32[]{:S(2)}) collective-permute-start(bf16[2,2,2,32,1536]{4,3,0,2,1:T(8,128)(2,1)} %dynamic-slice_bitcast_fusion.3), channel_id=1, source_target_pairs={{0,4},{1,5},{2,6},{3,7},{4,0},{5,1},{6,2},{7,3},{8,12},{9,13},{10,... | collective-permute-start | bytes 2359304 | tf_op jit(solution)/shard_map/ppermute | solution.py:659
  465.8 28.8 %collective-permute-start.36 = (bf16[2,2,2,2,32,1024]{5,4,0,2,3,1:T(8,128)(2,1)}, bf16[2,2,2,2,32,1024]{5,4,0,2,3,1:T(8,128)(2,1)}, u32[]{:S(2)}, u32[]{:S(2)}) collective-permute-start(bf16[2,2,2,2,32,1024]{5,4,0,2,3,1:T(8,128)(2,1)} %bitcast.217), channel_id=1, source_target_pairs={{0,2},{1,3},{2,0},{3,1},{4,6},{5,7},{6,4},{7,5},{8,10},{9,11},{10,... | collective-permute-start | bytes 3145736 | tf_op jit(solution)/shard_map/ppermute | solution.py:659
  489.4 11.6 %collective-permute-start.34 = (bf16[2,2,32,1536]{3,2,1,0:T(8,128)(2,1)S(1)}, bf16[2,2,32,1536]{3,2,1,0:T(8,128)(2,1)S(1)}, u32[]{:S(2)}, u32[]{:S(2)}) collective-permute-start(bf16[2,2,32,1536]{3,2,1,0:T(8,128)(2,1)S(1)} %dynamic-slice_bitcast_fusion.10), channel_id=1, source_target_pairs={{0,4},{1,5},{2,6},{3,7},{4,0},{5,1},{6,2},{7,3},{8,12},{9,13},{10,... | collective-permute-start | bytes 1179656 | tf_op jit(solution)/shard_map/ppermute | solution.py:659
  491.8 11.4 %collective-permute-start.35 = (bf16[2,2,32,1536]{3,2,0,1:T(8,128)(2,1)S(1)}, bf16[2,2,32,1536]{3,2,0,1:T(8,128)(2,1)}, u32[]{:S(2)}, u32[]{:S(2)}) collective-permute-start(bf16[2,2,32,1536]{3,2,0,1:T(8,128)(2,1)S(1)} %dynamic-slice_bitcast_fusion.9), channel_id=1, source_target_pairs={{0,8},{1,9},{2,10},{3,11},{4,12},{5,13},{6,14},{7,15},{8,0},{9,1},... | collective-permute-start | bytes 1179656 | tf_op jit(solution)/shard_map/ppermute | solution.py:659
  505.5 15.6 %all-to-all-start.1 = ((f32[32,1,112]{2,1,0:T(1,128)}), f32[32,1,112]{2,1,0:T(1,128)S(1)}, u32[]{:S(2)}, u32[]{:S(2)}) async-start(f32[32,1,112]{2,1,0:T(1,128)} %bitcast.59), calls=%async_computation.1 | async-start | bytes 32768 | tf_op jit(solution)/shard_map/all_to_all | solution.py:676
  510.1 12.6 %collective-permute-start.37 = (bf16[2,32,1536]{2,1,0:T(8,128)(2,1)}, bf16[2,32,1536]{2,1,0:T(8,128)(2,1)}, u32[]{:S(2)}, u32[]{:S(2)}) collective-permute-start(bf16[2,32,1536]{2,1,0:T(8,128)(2,1)} %dynamic-slice_bitcast_fusion.16), channel_id=1, source_target_pairs={{0,16},{1,17},{2,18},{3,19},{4,20},{5,21},{6,22},{7,23},{8,24},{9,... | collective-permute-start | bytes 589832 | tf_op jit(solution)/shard_map/ppermute | solution.py:659
  514.6 8.1 %collective-permute-start.38 = (bf16[2,32,1536]{2,1,0:T(8,128)(2,1)}, bf16[2,32,1536]{2,1,0:T(8,128)(2,1)}, u32[]{:S(2)}, u32[]{:S(2)}) collective-permute-start(bf16[2,32,1536]{2,1,0:T(8,128)(2,1)} %dynamic-slice_bitcast_fusion.15), channel_id=1, source_target_pairs={{0,1},{1,0},{2,3},{3,2},{4,5},{5,4},{6,7},{7,6},{8,9},{9,8},{10,11... | collective-permute-start | bytes 589832 | tf_op jit(solution)/shard_map/ppermute | solution.py:659
  517.8 15.9 %collective-permute-start.39 = (bf16[2,2,2,32,1024]{4,3,0,1,2:T(8,128)(2,1)S(1)}, bf16[2,2,2,32,1024]{4,3,0,1,2:T(8,128)(2,1)S(1)}, u32[]{:S(2)}, u32[]{:S(2)}) collective-permute-start(bf16[2,2,2,32,1024]{4,3,0,1,2:T(8,128)(2,1)S(1)} %dynamic-slice_bitcast_fusion.8), channel_id=1, source_target_pairs={{0,8},{1,9},{2,10},{3,11},{4,12},{5,13},{6,14},{7,15},{8,0},{9,1},... | collective-permute-start | bytes 1572872 | tf_op jit(solution)/shard_map/ppermute | solution.py:659
  534.7 7.4 %collective-permute-start.40 = (bf16[32,1536]{1,0:T(8,128)(2,1)S(1)}, bf16[32,1536]{1,0:T(8,128)(2,1)S(1)}, u32[]{:S(2)}, u32[]{:S(2)}) collective-permute-start(bf16[32,1536]{1,0:T(8,128)(2,1)S(1)} %dynamic-slice_bitcast_fusion.22), channel_id=1, source_target_pairs={{0,8},{1,9},{2,10},{3,11},{4,12},{5,13},{6,14},{7,15},{8,0},{9,1},... | collective-permute-start | bytes 294920 | tf_op jit(solution)/shard_map/ppermute | solution.py:659
  536.0 8.6 %collective-permute-start.42 = (bf16[2,2,32,1024]{3,2,0,1:T(8,128)(2,1)S(1)}, bf16[2,2,32,1024]{3,2,0,1:T(8,128)(2,1)S(1)}, u32[]{:S(2)}, u32[]{:S(2)}) collective-permute-start(bf16[2,2,32,1024]{3,2,0,1:T(8,128)(2,1)S(1)} %dynamic-slice_bitcast_fusion.14), channel_id=1, source_target_pairs={{0,1},{1,0},{2,3},{3,2},{4,5},{5,4},{6,7},{7,6},{8,9},{9,8},{10,11... | collective-permute-start | bytes 786440 | tf_op jit(solution)/shard_map/ppermute | solution.py:659
  537.4 7.2 %collective-permute-start.41 = (bf16[32,1536]{1,0:T(8,128)(2,1)S(1)}, bf16[32,1536]{1,0:T(8,128)(2,1)S(1)}, u32[]{:S(2)}, u32[]{:S(2)}) collective-permute-start(bf16[32,1536]{1,0:T(8,128)(2,1)S(1)} %dynamic-slice_bitcast_fusion.21), channel_id=1, source_target_pairs={{0,16},{1,17},{2,18},{3,19},{4,20},{5,21},{6,22},{7,23},{8,24},{9,... | collective-permute-start | bytes 294920 | tf_op jit(solution)/shard_map/ppermute | solution.py:659
  549.9 5.2 collective-permute-start.44
  (70 other events, 565.3 us)
Sparse Core Ops, SparseCore 0:
  10.9 123.5 all-gather.2
  137.4 65.4 all-gather.4
